TPU v7x, 32 devices: a whole 2x2x4 slice. The times are simulated.
32 devices in a mesh: blk: 4 (over y, core), dp: 8 (over z, x).
Axes of the slice: x: 2, y: 2, z: 4, core: 2. Of those that a mesh axis runs over, the one named last changes fastest.
Arguments:
- fingerprints: bfloat16 [12288, 2048], P(('blk', 'dp')), may hold values from 0 to 3, as said below
- w_first: bfloat16 [2048, 1024], replicated, may hold values from -0.3125 to 0.3125
- w_second: bfloat16 [1024, 512], replicated, may hold values from -0.0625 to 0.0625
Outputs:
- grad_first: float32 [2048, 1024], P('dp')
- grad_second: float32 [1024, 512], P('dp')
Inputs may be any that keep to these rules, and one draw needn't show every extreme that they name: `fingerprints`: Non-negative feature weights; every molecule has a third or more of its features nonzero.
All inputs are finite; a program needn't handle non-finite values.
Results may differ from a plain program's by a relative error of at most 0.003.
Values may be sent and summed in bfloat16 or wider, within the bound.
No kernel may reach another device: no remote copies, remote signals or barrier semaphores. Data moves between devices by JAX's collectives and lax.ppermute only.
A program may use at most 64 MiB of HBM per device.

v0:
```python
import math

import jax
import jax.numpy as jnp
from jax import lax
from jax.sharding import PartitionSpec as P


def pair_tile(mine_feats, mine_embed, mine_sqn, other, width):
    other_feats = other[:, :width]
    other_embed = other[:, width:]
    other_sqn = jnp.sum(jnp.square(other_feats.astype(jnp.float32)), axis=1)
    contract = (((1,), (1,)), ((), ()))
    inter = lax.dot_general(mine_feats, other_feats, contract, preferred_element_type=jnp.float32)
    tanimoto = inter / (mine_sqn[:, None] + other_sqn[None, :] - inter)
    scale = 1.0 / math.sqrt(mine_embed.shape[1])
    pred = (
        lax.dot_general(mine_embed, other_embed, contract, preferred_element_type=jnp.float32)
        * scale
    )
    return ((pred - tanimoto).astype(jnp.bfloat16), other_embed)


def column_product(left, right):
    return lax.dot_general(
        left, right, (((0,), (0,)), ((), ())), preferred_element_type=jnp.float32
    )


def per_device(fingerprints, w_first, w_second):
    tok_rows, width = fingerprints.shape
    blk_count = lax.axis_size("blk")
    dp_count = lax.axis_size("dp")
    group_rows = tok_rows * blk_count
    all_rows = group_rows * dp_count
    pre = jnp.dot(fingerprints, w_first, preferred_element_type=jnp.float32)
    sig = jax.nn.sigmoid(pre)
    hidden = (pre * sig).astype(jnp.bfloat16)
    embed = jnp.dot(hidden, w_second, preferred_element_type=jnp.float32).astype(jnp.bfloat16)
    mine_sqn = jnp.sum(jnp.square(fingerprints.astype(jnp.float32)), axis=1)
    packed = jnp.concatenate([fingerprints, embed], axis=1)
    resid, other_embed = pair_tile(
        fingerprints, embed, mine_sqn, lax.all_gather(packed, "blk", axis=0, tiled=True), width
    )
    summed = jnp.dot(resid, other_embed, preferred_element_type=jnp.float32)
    dembed = (summed * (2.0 / math.sqrt(group_rows * all_rows))).astype(jnp.bfloat16)
    dhidden = lax.dot_general(
        dembed, w_second, (((1,), (1,)), ((), ())), preferred_element_type=jnp.float32
    )
    dpre = (dhidden * sig * (1.0 + pre * (1.0 - sig))).astype(jnp.bfloat16)
    first_part = lax.psum_scatter(
        column_product(fingerprints, dpre), "dp", scatter_dimension=0, tiled=True
    )
    second_part = lax.psum_scatter(
        column_product(hidden, dembed), "dp", scatter_dimension=0, tiled=True
    )
    grad_first, grad_second = lax.psum((first_part, second_part), "blk")
    return (grad_first, grad_second)


def solution(mesh):
    in_specs = (P(("blk", "dp"), None), P(), P())
    out_specs = (P("dp", None), P("dp", None))
    return jax.shard_map(
        per_device, mesh=mesh, in_specs=in_specs, out_specs=out_specs, check_vma=False
    )
```

profile of v0, /device:TPU:0, one launch (start us, length us, event | category | flops | bytes accessed | tf_op | source)
XLA Modules:
  0.0 364.3 jit_solution(12797798440034670853)
XLA Ops:
  7.2 0.0 copy-start
  7.2 0.0 all-gather.2.cloned.1.call-start
  7.2 4.5 %fusion.22 = f32[384,1024]{1,0:T(8,128)S(1)} fusion(bf16[384,2048]{1,0:T(8,128)(2,1)} %param.3, bf16[2048,1024]{1,0:T(8,128)(2,1)} %param.4), kind=kOutput, calls=%fused_computation.24 | convolution fusion | flops 1610612736 | bytes 7340032 | tf_op jit(solution)/shard_map/dot_general | solution.py:36
  11.8 0.0 copy-start.3
  11.8 1.1 copy-done.3
  12.9 0.0 copy-done
  12.9 0.0 copy-start.1
  12.9 0.6 convolution_convert_fusion
  13.5 0.8 copy-done.1
  14.3 1.5 pad_maximum_fusion
  15.8 0.0 all-gather.2.cloned.1.call-update
  15.9 0.0 reduce-scatter.5.cloned.1.call-start
  15.9 0.4 multiply_reduce_fusion.1
  16.3 57.7 %all-gather.2.cloned.1.call-done = bf16[1536,2560]{1,0:T(8,128)(2,1)} async-done(((bf16[384,2560]{1,0:T(8,128)(2,1)}), bf16[1536,2560]{1,0:T(8,128)(2,1)}) %all-gather.2.cloned.1.call-update) | async-done | bytes 7864336 | tf_op jit(solution)/shard_map/all_gather | solution.py:43
  74.0 4.1 %multiply_reduce_fusion = f32[1536]{0:T(1024)S(1)} fusion(bf16[1536,2560]{1,0:T(8,128)(2,1)} %all-gather.2.cloned.1.call-done), kind=kLoop, calls=%fused_computation | loop fusion | flops 9435648 | bytes 6297600 | tf_op jit(solution)/shard_map/reduce_sum | solution.py:12
  78.1 7.7 %fusion.3 = f32[384,1536]{0,1:T(8,128)} fusion(bf16[384,2048]{1,0:T(8,128)(2,1)S(1)} %copy-done.1, bf16[1536,2560]{1,0:T(8,128)(2,1)} %all-gather.2.cloned.1.call-done), kind=kOutput, calls=%fused_computation.8 | convolution fusion | flops 2415919104 | bytes 10223616 | tf_op jit(solution)/shard_map/dot_general | solution.py:14
  85.8 4.4 %fusion.13 = bf16[384,512]{1,0:T(8,128)(2,1)S(1)} fusion(bf16[1536,2560]{1,0:T(8,128)(2,1)} %all-gather.2.cloned.1.call-done, bf16[384,512]{1,0:T(8,128)(2,1)S(1)} %convolution_convert_fusion, f32[384,1536]{0,1:T(8,128)} %fusion.3, f32[1536]{0:T(1024)S(1)} %multiply_reduce_fusion, f32[384]{0:T(512)S(1)} %multiply_reduce_fusion.1), kind=kOutput, calls=%fused_computation.18 | convolution fusion | flops 1211891712 | bytes 6299136 | tf_op jit(solution)/shard_map/dot_general | solution.py:45
  90.2 3.5 fusion.21
  93.8 0.0 reduce-scatter.5.cloned.1.call-update
  93.8 0.0 reduce-scatter.3.cloned.1.call-start
  93.9 6.5 %convolution_bitcast_fusion = f32[2048,1024]{0,1:T(8,128)} fusion(bf16[384,2048]{1,0:T(8,128)(2,1)S(1)} %copy-done.1, f32[384,1024]{1,0:T(8,128)} %copy-done.3, bf16[384,512]{1,0:T(8,128)(2,1)S(1)} %fusion.13, bf16[1024,512]{1,0:T(8,128)(2,1)S(1)} %copy-done), kind=kOutput, calls=%fused_computation.3 | convolution fusion | flops 2016804864 | bytes 12976128 | tf_op jit(solution)/shard_map/dot_general | solution.py:25
  100.4 0.0 reduce-scatter.3.cloned.1.call-update
  100.4 0.0 all-reduce.3.cloned.1.call-start
  100.5 61.2 %reduce-scatter.5.cloned.1.call-done = f32[128,512]{1,0:T(8,128)} async-done(((f32[1024,512]{1,0:T(8,128)}), f32[128,512]{1,0:T(8,128)}) %reduce-scatter.5.cloned.1.call-update) | async-done | bytes 262160 | tf_op jit(solution)/shard_map/reduce_scatter | solution.py:54
  161.6 152.2 %reduce-scatter.3.cloned.1.call-done = f32[256,1024]{0,1:T(8,128)} async-done(((f32[2048,1024]{0,1:T(8,128)}), f32[256,1024]{0,1:T(8,128)}) %reduce-scatter.3.cloned.1.call-update) | async-done | bytes 1048592 | tf_op jit(solution)/shard_map/reduce_scatter | solution.py:51
  313.8 0.0 all-reduce.3.cloned.1.call-update
  313.9 40.6 %all-reduce.3.cloned.1.call-done = (f32[256,1024]{0,1:T(8,128)}, f32[128,512]{1,0:T(8,128)}) async-done(((f32[256,1024]{0,1:T(8,128)}, f32[128,512]{1,0:T(8,128)}), (f32[256,1024]{0,1:T(8,128)}, f32[128,512]{1,0:T(8,128)})) %all-reduce.3.cloned.1.call-update) | async-done | bytes 1310736 | tf_op jit(solution)/shard_map/psum | solution.py:57
  354.5 0.0 copy-start.2
  354.5 2.6 copy.5
  357.1 0.0 copy-done.2
  357.1 0.7 copy.8
Async XLA Ops:
  7.2 5.7 %copy-start = (bf16[1024,512]{1,0:T(8,128)(2,1)S(1)}, bf16[1024,512]{1,0:T(8,128)(2,1)}, u32[]{:S(2)}) copy-start(bf16[1024,512]{1,0:T(8,128)(2,1)} %param.5) | copy-start | bytes 3145732
  7.2 66.8 %all-gather.2.cloned.1.call-start = ((), (), s32[]{:S(2)}) async-start(), calls=%async_computation.2 | async-start | bytes 9830400 | tf_op jit(solution)/shard_map/all_gather | solution.py:43
  11.8 1.1 copy-start.3
  12.9 1.4 copy-start.1
  15.9 145.8 %reduce-scatter.5.cloned.1.call-start = ((), (), s32[]{:S(2)}) async-start(), calls=%async_computation.4 | async-start | bytes 2359296 | tf_op jit(solution)/shard_map/reduce_scatter | solution.py:54
  93.8 220.0 %reduce-scatter.3.cloned.1.call-start = ((), (), s32[]{:S(2)}) async-start(), calls=%async_computation.3 | async-start | bytes 9437184 | tf_op jit(solution)/shard_map/reduce_scatter | solution.py:51
  100.4 254.1 %all-reduce.3.cloned.1.call-start = ((), (), s32[]{:S(2)}) async-start(), calls=%async_computation.5 | async-start | bytes 2621440 | tf_op jit(solution)/shard_map/psum | solution.py:57
  354.5 2.6 copy-start.2
Sparse Core Ops, SparseCore 0:
  16.0 58.0 all-gather.1
  93.9 67.6 reduce-scatter.4
  165.3 148.5 reduce-scatter.2
  316.3 38.0 all-reduce.2
where the time goes:
time: 365 us; the launch traced here: 364 us
  waiting for transfers between devices  312 us (85%)
  matrix products  27.3 us (7%)
  between operations  13.8 us (4%)
  other arithmetic  5.98 us (2%)
  local copies, waits for them, and re-layouts  5.23 us (1%)
    reduce_scatter x1, waiting for transfers between devices, per_device(): lax.psum_scatter(column_product(fingerprints, dpre), 'dp', scatter_dimens...  152 us
    reduce_scatter x1, waiting for transfers between devices, per_device(): lax.psum_scatter(column_product(hidden, dembed), 'dp', scatter_dimension=...  61.2 us
    all_gather x1, waiting for transfers between devices, per_device(): lax.all_gather(packed, 'blk', axis=0, tiled=True)  57.7 us
    psum x1, waiting for transfers between devices, per_device(): grad_first, grad_second = lax.psum((first_part, second_part), 'blk')  40.6 us
    dot_general x2, matrix products, column_product(): lax.dot_general(left, right, (((0,), (0,)), ((), ())), preferred_element_...  10.1 us
    dot_general x1, matrix products, pair_tile(): lax.dot_general(mine_feats, other_feats, contract, preferred_element_type...  7.73 us
  transfers between devices with their start and end apart: 4, of which 4 were waited for; matrix products, arithmetic and copies ran while one was open for 2% of the time, Pallas kernels for 0%

commit v1 on v0

v1 whole, which is shorter than its diff:
```python
import functools
import math

import jax
import jax.numpy as jnp
from jax import lax
from jax.experimental import pallas as pl
from jax.experimental.pallas import tpu as pltpu
from jax.sharding import PartitionSpec as P

F32 = jnp.float32
BF16 = jnp.bfloat16
F16 = jnp.float16
NN = (((1,), (0,)), ((), ()))
NT = (((1,), (1,)), ((), ()))
TN = (((0,), (0,)), ((), ()))
CHUNKS = 3
CUT = 144
VMEM_LIMIT = 20 * 1024 * 1024


def dot(left, right, dims=NN):
    return lax.dot_general(left, right, dims, preferred_element_type=F32)


def blk_swap(value, bit):
    count = lax.axis_size("blk")
    return lax.ppermute(value, "blk", [(b, b ^ bit) for b in range(count)])


def dp_swap(value, bit):
    count = lax.axis_size("dp")
    return lax.ppermute(value, "dp", [(d, d ^ bit) for d in range(count)])


def quarter_of(place, j):
    return pl.multiple_of((place ^ j) * 256, 256)


def encode(place, feats, kept, w_first, w_second, hidden_out, gate_out, acc):
    for j in range(4):
        units = pl.ds(quarter_of(place, j), 256)
        pre = dot(feats[...], w_first[:, units])
        sig = jax.nn.sigmoid(pre)
        hidden = (pre * sig).astype(BF16)
        hidden_out[:, j * 256 : (j + 1) * 256] = hidden[:kept]
        if j < 2:
            gate = sig[:kept] * (1.0 + pre[:kept] * (1.0 - sig[:kept]))
            gate_out[j] = gate.T
        part = dot(hidden, w_second[units, :])
        if j == 0:
            acc[...] = part
        else:
            acc[...] += part
    return acc[...].astype(BF16)


def residual(inter, pred, sq_rows, sq_cols, emb):
    tanimoto = inter / (sq_rows + sq_cols - inter)
    return (pred * (1.0 / math.sqrt(emb)) - tanimoto).astype(BF16)


def first_stage(i, o, s):
    tok, emb = i["own"].shape[0], i["w_second"].shape[1]
    feats = o["feats"]
    feats[:tok] = i["own"][...]
    feats[tok:] = i["sib"][...]
    embed = encode(
        i["place"][0], feats, tok, i["w_first"], i["w_second"], o["hidden"], o["gate"], s["acc"]
    )
    o["embed"][...] = embed
    wide = feats[...].astype(F32)
    sq = jnp.broadcast_to(jnp.sum(wide * wide, axis=1, keepdims=True), o["sq"].shape)
    o["sq"][...] = sq
    sq_cols = sq.T[:1]
    inter = dot(feats[:tok], feats[...], NT)
    pred = dot(embed[:tok], embed, NT)
    resid = residual(inter, pred, sq[:tok, :1], sq_cols, emb)
    o["summed", 0][...] = dot(resid, embed)
    o["token"][...] = jnp.zeros((8, 128), F32)


def add_columns(k, feats, embed, sq, embed_new, summed, emb, tok, part):
    top = feats[k][...]
    inter = dot(top, top, NT)
    at = lax.broadcasted_iota(jnp.int32, inter.shape, 0)
    to = lax.broadcasted_iota(jnp.int32, inter.shape, 1)
    diagonal = jnp.where(at == to, inter, 0.0)
    sq_rows = jnp.sum(diagonal, axis=1, keepdims=True)
    sq_cols = jnp.sum(diagonal, axis=0, keepdims=True)
    sq[k][...] = jnp.broadcast_to(sq_rows, sq[k].shape)
    resid = residual(inter, dot(embed_new, embed_new, NT), sq_rows, sq_cols, emb)
    total = dot(resid[:, :part], embed_new, TN)
    for j in range(k):
        pieces = [(0, tok, True), (tok, tok, False)] if j == 0 else [(0, 2 * part, True)]
        for start, count, keep in pieces:
            rows = pl.ds(start, count)
            old_embed = embed[j][rows, :]
            inter = dot(feats[j][rows, :], top, NT)
            pred = dot(old_embed, embed_new, NT)
            resid = residual(inter, pred, sq[j][rows, :1], sq_cols, emb)
            if keep:
                mine = resid if j == 0 else resid[:part]
                summed[j][...] += dot(mine, embed_new)
            total += dot(resid[:, :part], old_embed, TN)
    return total


def next_stage(k, i, o, s):
    tok, part, emb = i["summed", 0].shape[0], i["rem"].shape[0], i["w_second"].shape[1]
    feats = [i["feats", j] for j in range(k)] + [o["feats"]]
    feats[k][:part] = i["rem"][...]
    half = part // 2
    feats[k][part : part + half] = i["rs", 0][...]
    feats[k][part + half :] = i["rs", 1][...]
    embed = [i["embed", j] for j in range(k)]
    sq = [i["sq", j] for j in range(k)] + [o["sq"]]
    embed_new = encode(
        i["place"][0], feats[k], part, i["w_first"], i["w_second"], o["hidden"], o["gate"], s["acc"]
    )
    o["embed"][...] = embed_new
    summed = [o["summed", j] for j in range(k + 1)]
    for j in range(k):
        summed[j][...] = i["summed", j][...]
    summed[k][...] = add_columns(k, feats, embed, sq, embed_new, summed, emb, tok, part)
    if "token" in o:
        o["token"][...] = jnp.zeros((8, 128), F32)


def last_stage(factor, i, o, s):
    k = CHUNKS
    place = i["place"][0]
    next_stage(k, i, {**s, **o}, s)
    tok, part = i["summed", 0].shape[0], i["rem"].shape[0]
    wide = i["w_second"].shape[1] // 4
    starts = [0] + [tok + part * j for j in range(k)]
    sizes = [tok] + [part] * k
    for j in range(k + 1):
        rows = pl.ds(starts[j], sizes[j])
        piece = (s["summed", j][...] * factor).astype(BF16)
        s["sum_embed"][rows, :] = piece
        for q in range(4):
            s["dembed"][q, rows, :] = piece[:, q * wide : (q + 1) * wide]
    gates = [i["gate", j] for j in range(k)] + [s["gate"]]
    hiddens = [i["hidden", j] for j in range(k)] + [s["hidden"]]
    for n, name in ((1, "give"), (0, "keep")):
        units = pl.ds(quarter_of(place, n), 256)
        turned = dot(i["w_second"][units, :], s["sum_embed"][...], NT)
        for j in range(k + 1):
            rows = slice(starts[j], starts[j] + sizes[j])
            o[name][:, rows] = (turned[:, rows] * gates[j][n]).astype(BF16)
        second_share(place, place ^ n, s["dembed"], hiddens, o["second_" + name])


def second_share(place, quarter, dembed, hiddens, out):
    total, start = None, 0
    for hidden in hiddens:
        count = hidden.shape[0]
        part = dot(dembed[quarter, start : start + count, :], hidden[...], TN)
        total = part if total is None else total + part
        start += count
    for j in range(4):
        out[:, pl.ds(quarter_of(place, j), 256)] = total[:, j * 256 : (j + 1) * 256]


def exponent(bound):
    return jnp.clip(jnp.ceil(jnp.log2(jnp.maximum(bound, 1e-30))) + 1.0, -100.0, 120.0)


def gradients(i, o, s):
    second = i["second_keep"][...] + i["second_got"][...]
    sums = jnp.sum(jnp.abs(i["keep"][...].astype(F32)), axis=1, keepdims=True)
    sums += jnp.sum(jnp.abs(i["got"][...].astype(F32)), axis=1, keepdims=True)
    exp_first = exponent(3.0 * jnp.max(sums, axis=0, keepdims=True))
    most = jnp.max(jnp.abs(second), axis=1, keepdims=True)
    exp_second = exponent(jnp.max(most, axis=0, keepdims=True))
    exp_first = jnp.broadcast_to(exp_first, (8, 256))
    exp_second = jnp.broadcast_to(exp_second, (8, 256))
    one, two = o["one"], o["two"]
    top, bottom = CUT, 256 - CUT
    for d in range(8):
        block = second[:, d * 128 : (d + 1) * 128]
        one[d, top : top + 64, :128] = block[:64]
        one[d, top : top + 64, 128:] = block[64:]
        one[d, top + 64 : top + 72] = exp_first
        one[d, top + 72 :] = exp_second
        two[d, bottom : bottom + 8] = exp_first
        two[d, bottom + 8 :] = exp_first
    o["kind_one"][:top] = jnp.zeros((top, 256), F32)
    o["kind_one"][top : top + 64] = jnp.ones((64, 256), F32)
    o["kind_one"][top + 64 :] = jnp.full((16, 256), 2.0, F32)
    o["kind_two"][:bottom] = jnp.zeros((bottom, 256), F32)
    o["kind_two"][bottom:] = jnp.full((16, 256), 2.0, F32)
    for d in range(8):
        block, at = None, 0
        for j in range(CHUNKS + 1):
            f = i["feats", j]
            count = f.shape[0] // 2
            for half, name in enumerate(("keep", "got")):
                rows = f[half * count : (half + 1) * count, d * 256 : (d + 1) * 256]
                piece = dot(i[name][:, at : at + count], rows)
                block = piece if block is None else block + piece
            at += count
        one[d, :top] = block[:top]
        two[d, :bottom] = block[top:]


def run(body, ins, outs, scratch, limit=VMEM_LIMIT):
    names_in, names_out, names_s = list(ins), list(outs), list(scratch)

    def kernel(*refs):
        n, m = len(names_in), len(names_out)
        i = dict(zip(names_in, refs[:n]))
        o = dict(zip(names_out, refs[n : n + m]))
        body(i, o, dict(zip(names_s, refs[n + m :])))

    vmem = pltpu.VMEM
    spaces = {"place": pltpu.SMEM, "arg": pl.ANY}
    shapes = [jax.ShapeDtypeStruct(*v) for v in outs.values()]
    got = pl.pallas_call(
        kernel,
        out_shape=shapes,
        in_specs=[pl.BlockSpec(memory_space=spaces.get(n, vmem)) for n in names_in],
        out_specs=[pl.BlockSpec(memory_space=vmem)] * len(shapes),
        scratch_shapes=[vmem(*v) if isinstance(v, tuple) else v for v in scratch.values()],
        compiler_params=pltpu.CompilerParams(vmem_limit_bytes=limit),
        cost_estimate=pl.CostEstimate(flops=1, bytes_accessed=1, transcendentals=0),
    )(*ins.values())
    return dict(zip(names_out, got))


def split(i, o, s):
    half = i["rem"].shape[0] // 2
    for h in range(2):
        o["rows", h][...] = i["rem"][h * half : (h + 1) * half]


def fetch(pairs, i, o, s):
    copies = []
    for n, (source, start, count, target) in enumerate(pairs):
        rows = i[source].at[pl.ds(start, count), :]
        copies.append(pltpu.make_async_copy(rows, o[target], s["sems"].at[n]))
        copies[-1].start()
    for copy in copies:
        copy.wait()


def encode16(total, kind, tail):
    first, second = exps_of(total, tail)
    e = jnp.where(kind == 0.0, first, second)
    scale = jnp.where(kind == 2.0, 1.0, jnp.exp2(15.0 - e))
    return (total * scale).astype(F16)


def decode16(got, kind, tail):
    got = got.astype(F32)
    first, second = exps_of(got, tail)
    e = jnp.where(kind == 0.0, first, second)
    return got * jnp.where(kind == 2.0, 1.0, jnp.exp2(e - 15.0))


def exps_of(value, tail):
    rows = value.ndim - 2
    return [lax.slice_in_dim(value, tail + at, tail + at + 1, axis=rows) for at in (0, 8)]


def halves(value, axis, mine):
    low = lax.index_in_dim(value, 0, axis, keepdims=False)
    high = lax.index_in_dim(value, 1, axis, keepdims=False)
    return jnp.where(mine == 0, low, high), jnp.where(mine == 0, high, low)


def pick(total, axis, index):
    return lax.dynamic_index_in_dim(total, index, axis, keepdims=False)


class Sum:
    def __init__(self, total, kind, order):
        self.total, self.kind = total, kind
        self.tail = total.shape[-2] - 16
        self.axes = list(range(total.ndim - 2))
        self.order = order

    def send(self, step, shifts):
        axis = self.order[step]
        at, size = self.axes.index(axis), self.total.shape[self.axes.index(axis)]
        me = (lax.axis_index("dp") >> shifts[axis]) & (size - 1)
        gots = []
        for o in range(1, size):
            give = pick(self.total, at, me ^ o)
            gots.append(dp_swap(encode16(give, self.kind, self.tail), o << shifts[axis]))
        self.axes.pop(at)
        self.keep = pick(self.total, at, me)
        return gots

    def receive(self, gots):
        others = [decode16(g, self.kind, self.tail) for g in gots]
        total, top = self.keep, self.keep
        for other in others:
            total = total + other
            top = jnp.maximum(top, other)
        self.total = jnp.where(self.kind == 2.0, top + float(len(others)), total)


def split_lanes(packed, bounds, count):
    if count == 1:
        return packed
    blocks, rows, lanes = packed.shape
    plain = packed.reshape(blocks, rows, count, lanes // count)
    paired = packed.reshape(blocks, rows, 2, count, lanes // 2 // count)
    plain = jnp.moveaxis(plain, 2, 1)
    paired = jnp.moveaxis(paired, 3, 1).reshape(plain.shape)
    row = lax.broadcasted_iota(jnp.int32, plain.shape, 2)
    both = jnp.where((row >= bounds[0]) & (row < bounds[1]), paired, plain)
    return both.reshape(blocks * count, rows, lanes // count)


def per_device(fingerprints, w_first, w_second):
    tok, width = fingerprints.shape
    hid, emb = w_second.shape
    blk_count = lax.axis_size("blk")
    dp_count = lax.axis_size("dp")
    group_rows = tok * blk_count
    all_rows = group_rows * dp_count
    factor = 2.0 / math.sqrt(group_rows * all_rows)
    bits = dp_count.bit_length() - 1
    b = lax.axis_index("blk")
    y, c = b >> 1, b & 1
    place = b.astype(jnp.int32).reshape(1)
    k = CHUNKS
    part = tok // k

    rem = []
    for start, count in ((0, 1), (1, k - 1)):
        names = [("rows", j) for j in range(start, start + count)]
        out = run(
            functools.partial(fetch, [("arg", j * part, part, ("rows", j)) for _, j in names]),
            {"arg": fingerprints},
            {name: ((part, width), BF16) for name in names},
            {"sems": pltpu.SemaphoreType.DMA((count,))},
            limit=2 << 20,
        )
        rem += [blk_swap(out[name], 2) for name in names]
    sib = blk_swap(fingerprints, 1)
    rs = []

    base = {"place": place, "w_first": w_first, "w_second": w_second}
    out = run(
        first_stage,
        {**base, "own": fingerprints, "sib": sib},
        {
            "feats": ((2 * tok, width), BF16),
            "hidden": ((tok, hid), BF16),
            "gate": ((2, 256, tok), F32),
            "embed": ((2 * tok, emb), BF16),
            "sq": ((2 * tok, 128), F32),
            ("summed", 0): ((tok, emb), F32),
            "token": ((8, 128), F32),
        },
        {"acc": ((2 * tok, emb), F32)},
    )
    token = out["token"]
    hidden, gate, feats = [out["hidden"]], [out["gate"]], [out["feats"]]
    embed, sq, summed = [out["embed"]], [out["sq"]], [out["summed", 0]]
    for step in range(1, k + 1):
        last = step == k
        half = part // 2
        out = run(
            split,
            {"rem": rem[step - 1], "token": token},
            {("rows", h): ((half, width), BF16) for h in range(2)},
            {},
            limit=2 << 20,
        )
        ins = {**base, "rem": rem[step - 1]}
        for h in range(2):
            ins["rs", h] = blk_swap(out["rows", h], 1)
        for j in range(step):
            ins["feats", j] = feats[j]
            ins["embed", j] = embed[j]
            ins["sq", j] = sq[j]
            ins["summed", j] = summed[j]
        outs = {
            "feats": ((2 * part, width), BF16),
            "hidden": ((part, hid), BF16),
            "gate": ((2, 256, part), F32),
        }
        more = {
            "embed": ((2 * part, emb), BF16),
            "sq": ((2 * part, 128), F32),
            **{("summed", j): ((tok if j == 0 else part, emb), F32) for j in range(step + 1)},
        }
        scratch = {"acc": ((2 * part, emb), F32)}
        if last:
            for j in range(step):
                ins["hidden", j] = hidden[j]
                ins["gate", j] = gate[j]
            scratch = {**scratch, **more, "hidden": outs.pop("hidden"), "gate": outs.pop("gate")}
            scratch["sum_embed"] = ((2 * tok, emb), BF16)
            scratch["dembed"] = ((4, 2 * tok, emb // 4), BF16)
            for name in ("give", "keep"):
                outs[name] = ((256, 2 * tok), BF16)
                outs["second_" + name] = ((emb // 4, hid), F32)
            body = functools.partial(last_stage, factor)
        else:
            outs = {**outs, **more, "token": ((8, 128), F32)}
            body = functools.partial(next_stage, step)
        out = run(body, ins, outs, scratch)
        feats.append(out["feats"])
        if not last:
            hidden.append(out["hidden"])
            gate.append(out["gate"])
            token = out["token"]
            embed.append(out["embed"])
            sq.append(out["sq"])
            summed = [out["summed", j] for j in range(step + 1)]

    got = blk_swap(out["give"], 1)
    second_got = blk_swap(out["second_give"], 1)
    ins = {
        "keep": out["keep"],
        "got": got,
        "second_keep": out["second_keep"],
        "second_got": second_got,
    }
    for j in range(k + 1):
        ins["feats", j] = feats[j]
    rows_one, rows_two = CUT + 64 + 16, 256 - CUT + 16
    out = run(
        gradients,
        ins,
        {
            "one": ((8, rows_one, 256), F32),
            "two": ((8, rows_two, 256), F32),
            "kind_one": ((rows_one, 256), F32),
            "kind_two": ((rows_two, 256), F32),
        },
        {},
    )
    lanes = 256 * 8 // dp_count
    extra = dp_count // 8
    one = split_lanes(out["one"], (CUT, CUT + 64), extra)
    two = split_lanes(out["two"], (0, 0), extra)
    kind_one, kind_two = out["kind_one"][:, :lanes], out["kind_two"][:, :lanes]
    more = extra.bit_length() - 1
    shape = (2,) * more + (4, 2)
    shifts = [3 + more - 1 - n for n in range(more)] + [1, 0]
    zed, ex, rest = more, more + 1, list(range(more))
    one = Sum(one.reshape(shape + one.shape[1:]), kind_one, [ex, zed] + rest)
    two = Sum(two.reshape(shape + two.shape[1:]), kind_two, [zed] + rest + [ex])
    for step in range(more + 2):
        gots = lax.optimization_barrier((one.send(step, shifts), two.send(step, shifts)))
        one.receive(gots[0])
        two.receive(gots[1])

    packed = jnp.concatenate(
        [encode16(one.total, kind_one, one.tail), encode16(two.total, kind_two, two.tail)], 0
    )
    across = blk_swap(packed, 2)
    pair = jnp.stack([packed, across])
    beside = blk_swap(pair, 1)
    here = halves(jnp.stack([packed, beside[0]]), 0, c)
    there = halves(jnp.stack([across, beside[1]]), 0, c)
    low = [jnp.where(y == 0, h, t) for h, t in zip(here, there)]
    high = [jnp.where(y == 0, t, h) for h, t in zip(here, there)]
    every = jnp.stack(low + high)
    one = decode16(every[:, :rows_one], kind_one, one.tail)
    two = decode16(every[:, rows_one:], kind_two, two.tail)
    first = jnp.concatenate([one[:, :CUT], two[:, : 256 - CUT]], 1).reshape(hid, lanes)
    second = one[:, CUT : CUT + 64]
    second = jnp.concatenate([second[..., : lanes // 2], second[..., lanes // 2 :]], 1)
    return first.T, second.reshape(emb, lanes // 2).T


def solution(mesh):
    in_specs = (P(("blk", "dp"), None), P(), P())
    out_specs = (P("dp", None), P("dp", None))
    return jax.shard_map(
        per_device, mesh=mesh, in_specs=in_specs, out_specs=out_specs, check_vma=False
    )
```

time: 365 us -> 110 us (0.30)
  waiting for transfers between devices: 312 us -> 27.2 us
  Pallas kernels: 0 us -> 35.6 us
  matrix products: 27.3 us -> 0 us
  starting transfers between devices: 0.16 us -> 20 us
  local copies, waits for them, and re-layouts: 5.23 us -> 19.9 us
  between operations: 13.8 us -> 1.29 us
    reduce_scatter x2 -> x0, waiting for transfers between devices: 213 us -> none  [the longest x1 152 us: per_device(): lax.psum_scatter(column_product(fingerprints, dpre), 'dp', scatter_dimens...]
    all_gather x1 -> x0, waiting for transfers between devices: 57.7 us -> none  [per_device(): lax.all_gather(packed, 'blk', axis=0, tiled=True)]
    psum x1 -> x0, waiting for transfers between devices: 40.6 us -> none  [per_device(): grad_first, grad_second = lax.psum((first_part, second_part), 'blk')]
    pallas_call x0 -> x10, Pallas kernels: none -> 35.6 us  [run(): pl.pallas_call(kernel, out_shape=shapes, in_specs=[pl.BlockSpec(memory_sp...]
    dot_general x6 -> x0, matrix products: 27.3 us -> none  [the longest x2 10.1 us: column_product(): lax.dot_general(left, right, (((0,), (0,)), ((), ())), preferred_element_...]
    ppermute x0 -> x22, waiting for transfers between devices: none -> 27.2 us  [the longest x8 16.5 us: dp_swap(): return lax.ppermute(value, 'dp', [(d, d ^ bit) for d in range(count)])]
    ppermute x0 -> x22, starting transfers between devices: none -> 20 us  [the longest x8 11.1 us: dp_swap(): return lax.ppermute(value, 'dp', [(d, d ^ bit) for d in range(count)])]
    unnamed x10 -> x58, local copies, waits for them, and re-layouts: 5.23 us -> 17.5 us
  transfers between devices with their start and end apart: 4 -> 22, of which waited for: 4 -> 11; matrix products, arithmetic and copies ran while one was open for 2% -> 2% of each run, Pallas kernels for 0% -> 22%
where the time goes in v1:
time: 110 us
  Pallas kernels  35.6 us (32%)
  waiting for transfers between devices  27.2 us (25%)
  starting transfers between devices  20 us (18%)
  local copies, waits for them, and re-layouts  19.9 us (18%)
  other arithmetic  5.46 us (5%)
  between operations  1.29 us (1%)
    pallas_call x10, Pallas kernels, run(): pl.pallas_call(kernel, out_shape=shapes, in_specs=[pl.BlockSpec(memory_sp...  35.6 us
    unnamed x58, local copies, waits for them, and re-layouts  17.5 us
    ppermute x8, waiting for transfers between devices, dp_swap(): return lax.ppermute(value, 'dp', [(d, d ^ bit) for d in range(count)])  16.5 us
    ppermute x8, starting transfers between devices, dp_swap(): return lax.ppermute(value, 'dp', [(d, d ^ bit) for d in range(count)])  11.1 us
    ppermute x14, waiting for transfers between devices, blk_swap(): return lax.ppermute(value, 'blk', [(b, b ^ bit) for b in range(count)])  10.8 us
    ppermute x14, starting transfers between devices, blk_swap(): return lax.ppermute(value, 'blk', [(b, b ^ bit) for b in range(count)])  8.98 us
  transfers between devices with their start and end apart: 22, of which 11 were waited for; matrix products, arithmetic and copies ran while one was open for 2% of the time, Pallas kernels for 22%

profile of v1, /device:TPU:0, one launch (start us, length us, event | category | flops | bytes accessed | tf_op | source)
XLA Modules:
  0.0 109.6 jit_solution(14479673448490495860)
XLA Ops:
  0.6 0.5 collective-permute-start.3
  1.1 1.4 %copy-done.3 = bf16[384,2048]{1,0:T(8,128)(2,1)S(1)} copy-done((bf16[384,2048]{1,0:T(8,128)(2,1)S(1)}, bf16[384,2048]{1,0:T(8,128)(2,1)}, u32[]{:S(2)}) %copy-start.3) | copy-done | bytes 1572888
  2.6 0.8 shard_map.51
  3.4 2.6 %collective-permute-start.2 = (bf16[128,2048]{1,0:T(8,128)(2,1)}, bf16[128,2048]{1,0:T(8,128)(2,1)}, u32[]{:S(2)}, u32[]{:S(2)}) collective-permute-start(bf16[128,2048]{1,0:T(8,128)(2,1)} %shard_map.51), channel_id=1, source_target_pairs={{0,16},{8,24},{16,0},{24,8},{1,17},{9,25},{17,1},{25,9},{2,18},{10... | collective-permute-start | bytes 1572872 | tf_op jit(solution)/shard_map/ppermute | solution.py:28
  6.0 0.9 shard_map.50
  6.9 0.8 copy-done.18
  7.7 1.2 %copy-done.11 = bf16[384,2048]{1,0:T(8,128)(2,1)} copy-done((bf16[384,2048]{1,0:T(8,128)(2,1)}, bf16[384,2048]{1,0:T(8,128)(2,1)S(1)}, u32[]{:S(2)}) %copy-start.11) | copy-done | bytes 1572888
  8.9 2.2 %copy-done = bf16[2048,1024]{1,0:T(8,128)(2,1)S(1)} copy-done((bf16[2048,1024]{1,0:T(8,128)(2,1)S(1)}, bf16[2048,1024]{1,0:T(8,128)(2,1)}, u32[]{:S(2)}) %copy-start) | copy-done | bytes 4194328
  11.1 1.2 %copy-done.2 = bf16[1024,512]{1,0:T(8,128)(2,1)S(1)} copy-done((bf16[1024,512]{1,0:T(8,128)(2,1)S(1)}, bf16[1024,512]{1,0:T(8,128)(2,1)}, u32[]{:S(2)}) %copy-start.2) | copy-done | bytes 1048600
  12.3 1.4 %copy-done.4 = bf16[384,2048]{1,0:T(8,128)(2,1)S(1)} copy-done((bf16[384,2048]{1,0:T(8,128)(2,1)S(1)}, bf16[384,2048]{1,0:T(8,128)(2,1)}, u32[]{:S(2)}) %copy-start.4) | copy-done | bytes 1572888
  13.7 1.4 %copy-done.12 = bf16[384,2048]{1,0:T(8,128)(2,1)S(1)} copy-done((bf16[384,2048]{1,0:T(8,128)(2,1)S(1)}, bf16[384,2048]{1,0:T(8,128)(2,1)}, u32[]{:S(2)}) %copy-start.12) | copy-done | bytes 1572888
  15.1 7.8 %shard_map.52 = (bf16[768,2048]{1,0:T(8,128)(2,1)S(1)}, bf16[384,1024]{1,0:T(8,128)(2,1)S(1)}, f32[2,256,384]{2,1,0:T(8,128)S(1)}, bf16[768,512]{1,0:T(8,128)(2,...) custom-call(s32[1]{0:T(128)} %bitcast.refs_0_, bf16[2048,1024]{1,0:T(8,128)(2,1)S(1)} %copy-done, ...), custom_call_target="tpu_custom_call" | custom-call | flops 1 | bytes 1 | tf_op jit(solution)/shard_map/pallas_call | solution.py:220
  22.9 1.1 shard_map.53
  24.0 0.3 collective-permute-start.4
  24.3 0.3 collective-permute-start.5
  24.6 2.0 %collective-permute-start = (bf16[128,2048]{1,0:T(8,128)(2,1)S(1)}, bf16[128,2048]{1,0:T(8,128)(2,1)S(1)}, u32[]{:S(2)}, u32[]{:S(2)}) collective-permute-start(bf16[128,2048]{1,0:T(8,128)(2,1)S(1)} %copy-done.19), channel_id=1, source_target_pairs={{0,16},{8,24},{16,0},{24,8},{1,17},{9,25},{17,1},{25,9},{2,18},{10... | collective-permute-start | bytes 1572872 | tf_op jit(solution)/shard_map/ppermute | solution.py:28
  26.6 6.1 %shard_map.54 = (bf16[256,2048]{1,0:T(8,128)(2,1)S(1)}, bf16[128,1024]{1,0:T(8,128)(2,1)S(1)}, f32[2,256,128]{2,1,0:T(8,128)S(1)}, bf16[256,512]{1,0:T(8,128)(2,...) custom-call(s32[1]{0:T(128)} %bitcast.refs_0_, ...), custom_call_target="tpu_custom_call" | custom-call | flops 1 | bytes 1 | tf_op jit(solution)/shard_map/pallas_call | solution.py:220
  32.7 1.5 %shard_map.55 = (bf16[64,2048]{1,0:T(8,128)(2,1)S(1)}, bf16[64,2048]{1,0:T(8,128)(2,1)S(1)}) custom-call(bf16[128,2048]{1,0:T(8,128)(2,1)} %collective-permute-done.1.refs_0_.refs_3_, f32[8,128]{1,0:T(8,128)S(1)} %get-tuple-element.60.refs_1_), custom_call_target="tpu_custom_call" | custom-call | flops 1 | bytes 1 | tf_op jit(solution)/shard_map/pallas_call | solution.py:220
  34.3 0.5 collective-permute-start.7
  34.8 1.0 collective-permute-done.6.refs_4_
  35.8 0.4 collective-permute-done.7.refs_5_
  36.2 6.2 %shard_map.56 = (bf16[256,2048]{1,0:T(8,128)(2,1)S(1)}, bf16[128,1024]{1,0:T(8,128)(2,1)S(1)}, f32[2,256,128]{2,1,0:T(8,128)S(1)}, bf16[256,512]{1,0:T(8,128)(2,...) custom-call(s32[1]{0:T(128)} %bitcast.refs_0_, ...), custom_call_target="tpu_custom_call" | custom-call | flops 1 | bytes 1 | tf_op jit(solution)/shard_map/pallas_call | solution.py:220
  42.5 0.2 collective-permute-start.8
  42.7 0.4 collective-permute-start.9
  43.0 1.0 collective-permute-done.8.refs_4_
  44.1 0.4 collective-permute-done.9.refs_5_
  44.5 7.2 %shard_map.58 = (bf16[256,2048]{1,0:T(8,128)(2,1)S(1)}, bf16[256,768]{1,0:T(8,128)(2,1)}, f32[128,1024]{1,0:T(8,128)}, bf16[256,768]{1,0:T(8,128)(2,1)S(1)}, f32[128,1024]{1,0:T(8,128)S(1)}) custom-call(s32[1]{0:T(128)} %bitcast.refs_0_, bf16[2048,1024]{1,0:T(8,128)(2,1)S(1)} %copy-done.1, bf16[1024,512]{1,0:T(8,128)(2,1)S(1)} %copy-done.2, ...), custom_call_target="tpu_custom_call" | custom-call | flops 1 | bytes 1 | tf_op jit(solution)/shard_map/pallas_call | solution.py:220
  51.6 1.0 copy-done.14
  52.6 0.8 copy-done.16
  53.5 0.4 collective-permute-start.10
  53.9 2.3 %collective-permute-done.10.refs_1_ = bf16[256,768]{1,0:T(8,128)(2,1)} collective-permute-done((bf16[256,768]{1,0:T(8,128)(2,1)}, bf16[256,768]{1,0:T(8,128)(2,1)}, u32[]{:S(2)}, u32[]{:S(2)}) %collective-permute-start.10) | collective-permute-done | bytes 393248 | tf_op jit(solution)/shard_map/ppermute | solution.py:28
  56.2 1.2 %copy-done.6 = bf16[256,2048]{1,0:T(8,128)(2,1)S(1)} copy-done((bf16[256,2048]{1,0:T(8,128)(2,1)S(1)}, bf16[256,2048]{1,0:T(8,128)(2,1)}, u32[]{:S(2)}) %copy-start.6) | copy-done | bytes 1048600
  57.4 1.2 %copy-done.8 = bf16[256,2048]{1,0:T(8,128)(2,1)S(1)} copy-done((bf16[256,2048]{1,0:T(8,128)(2,1)S(1)}, bf16[256,2048]{1,0:T(8,128)(2,1)}, u32[]{:S(2)}) %copy-start.8) | copy-done | bytes 1048600
  58.7 1.2 %copy-done.15 = bf16[256,2048]{1,0:T(8,128)(2,1)S(1)} copy-done((bf16[256,2048]{1,0:T(8,128)(2,1)S(1)}, bf16[256,2048]{1,0:T(8,128)(2,1)}, u32[]{:S(2)}) %copy-start.15) | copy-done | bytes 1048600
  59.9 1.0 copy-done.17
  60.9 4.0 %shard_map.59 = (f32[8,224,256]{2,1,0:T(8,128)S(1)}, f32[8,128,256]{2,1,0:T(8,128)S(1)}, f32[224,256]{1,0:T(8,128)S(1)}, f32[128,256]{1,0:T(8,128)S(1)}) custom-call(bf16[256,768]{1,0:T(8,128)(2,1)S(1)} %get-tuple-element.83.refs_0_, bf16[256,768]{1,0:T(8,128)(2,1)} %collective-permute-done.10.refs_1_, f32[128,1024]{1,0:T(8,128)S(1)} %copy-done.17, ...), custom_call_target="tpu_custom_call" | custom-call | flops 1 | bytes 1 | tf_op jit(solution)/shard_map/pallas_call | solution.py:220
  65.3 0.6 copy-done.13
  66.0 0.6 copy-done.9
  66.6 0.3 multiply_convert_fusion
  66.9 1.6 %collective-permute-start.12 = (f16[4,224,256]{2,1,0:T(8,128)(2,1)S(1)}, f16[4,224,256]{2,1,0:T(8,128)(2,1)S(1)}, u32[]{:S(2)}, u32[]{:S(2)}) collective-permute-start(f16[4,224,256]{2,1,0:T(8,128)(2,1)S(1)} %multiply_convert_fusion), channel_id=1, source_target_pairs={{0,1},{1,0},{2,3},{3,2},{4,5},{5,4},{6,7},{7,6},{8,9},{9,8},{10,11... | collective-permute-start | bytes 1376264 | tf_op jit(solution)/shard_map/ppermute | solution.py:33
  68.5 0.9 multiply_convert_fusion.1
  69.5 1.6 %collective-permute-start.13 = (f16[2,128,256]{2,1,0:T(8,128)(2,1)}, f16[2,128,256]{2,1,0:T(8,128)(2,1)S(1)}, u32[]{:S(2)}, u32[]{:S(2)}) collective-permute-start(f16[2,128,256]{2,1,0:T(8,128)(2,1)} %get-tuple-element.160), channel_id=1, source_target_pairs={{0,2},{1,3},{2,0},{3,1},{4,6},{5,7},{6,4},{7,5},{8,10},{9,11},{10,... | collective-permute-start | bytes 393224 | tf_op jit(solution)/shard_map/ppermute | solution.py:33
  71.0 2.6 %collective-permute-start.14 = (f16[2,128,256]{2,1,0:T(8,128)(2,1)}, f16[2,128,256]{2,1,0:T(8,128)(2,1)S(1)}, u32[]{:S(2)}, u32[]{:S(2)}) collective-permute-start(f16[2,128,256]{2,1,0:T(8,128)(2,1)} %get-tuple-element.159), channel_id=1, source_target_pairs={{0,4},{1,5},{2,6},{3,7},{4,0},{5,1},{6,2},{7,3},{8,12},{9,13},{10,... | collective-permute-start | bytes 393224 | tf_op jit(solution)/shard_map/ppermute | solution.py:33
  73.6 0.2 collective-permute-start.15
  73.8 2.7 %collective-permute-done.13 = f16[2,128,256]{2,1,0:T(8,128)(2,1)S(1)} collective-permute-done((f16[2,128,256]{2,1,0:T(8,128)(2,1)}, f16[2,128,256]{2,1,0:T(8,128)(2,1)S(1)}, u32[]{:S(2)}, u32[]{:S(2)}) %collective-permute-start.13) | collective-permute-done | bytes 131104 | tf_op jit(solution)/shard_map/ppermute | solution.py:33
  76.6 7.6 %collective-permute-done.14 = f16[2,128,256]{2,1,0:T(8,128)(2,1)S(1)} collective-permute-done((f16[2,128,256]{2,1,0:T(8,128)(2,1)}, f16[2,128,256]{2,1,0:T(8,128)(2,1)S(1)}, u32[]{:S(2)}, u32[]{:S(2)}) %collective-permute-start.14) | collective-permute-done | bytes 131104 | tf_op jit(solution)/shard_map/ppermute | solution.py:33
  84.5 0.4 fusion.1
  84.9 0.5 fusion.8
  85.4 2.0 %collective-permute-start.16 = (f16[224,256]{1,0:T(8,128)(2,1)S(1)}, f16[224,256]{1,0:T(8,128)(2,1)S(1)}, u32[]{:S(2)}, u32[]{:S(2)}) collective-permute-start(f16[224,256]{1,0:T(8,128)(2,1)S(1)} %get-tuple-element.105), channel_id=1, source_target_pairs={{0,2},{1,3},{2,0},{3,1},{4,6},{5,7},{6,4},{7,5},{8,10},{9,11},{10,... | collective-permute-start | bytes 344072 | tf_op jit(solution)/shard_map/ppermute | solution.py:33
  87.4 1.1 %collective-permute-start.17 = (f16[224,256]{1,0:T(8,128)(2,1)S(1)}, f16[224,256]{1,0:T(8,128)(2,1)S(1)}, u32[]{:S(2)}, u32[]{:S(2)}) collective-permute-start(f16[224,256]{1,0:T(8,128)(2,1)S(1)} %get-tuple-element.104), channel_id=1, source_target_pairs={{0,4},{1,5},{2,6},{3,7},{4,0},{5,1},{6,2},{7,3},{8,12},{9,13},{10,... | collective-permute-start | bytes 344072 | tf_op jit(solution)/shard_map/ppermute | solution.py:33
  88.5 1.4 %collective-permute-start.18 = (f16[224,256]{1,0:T(8,128)(2,1)S(1)}, f16[224,256]{1,0:T(8,128)(2,1)S(1)}, u32[]{:S(2)}, u32[]{:S(2)}) collective-permute-start(f16[224,256]{1,0:T(8,128)(2,1)S(1)} %get-tuple-element.103), channel_id=1, source_target_pairs={{0,6},{1,7},{2,4},{3,5},{4,2},{5,3},{6,0},{7,1},{8,14},{9,15},{10,... | collective-permute-start | bytes 344072 | tf_op jit(solution)/shard_map/ppermute | solution.py:33
  89.9 1.2 %fusion.5 = f32[2,128,256]{2,1,0:T(8,128)S(1)} fusion(f32[4,2,128,256]{3,2,1,0:T(8,128)} %bitcast.208, s32[]{:T(128)S(6)} %select_n.230, f32[2,256]{1,0:T(2,128)S(1)} %bitcast.220, f32[2,256]{1,0:T(2,128)S(1)} %bitcast.221, f32[2,256]{1,0:T(2,128)S(1)} %bitcast.222, f32[2,256]{1,0:T(2,128)S(1)} %bitcast.223, f32[2,256]{1,0:T(2,128)S(1)} %bitcast.224, ...), kind=kLoop, calls=%fused_computation.19 | loop fusion | flops 1703936 | bytes 995332 | tf_op jit(solution)/shard_map/jit(_where)/select_n | solution.py:302
  91.3 0.6 collective-permute-start.19
  91.8 3.7 %collective-permute-done.19 = f16[128,256]{1,0:T(8,128)(2,1)S(1)} collective-permute-done((f16[128,256]{1,0:T(8,128)(2,1)S(1)}, f16[128,256]{1,0:T(8,128)(2,1)S(1)}, u32[]{:S(2)}, u32[]{:S(2)}) %collective-permute-start.19) | collective-permute-done | bytes 65568 | tf_op jit(solution)/shard_map/ppermute | solution.py:33
  95.6 2.4 %collective-permute-done.17 = f16[224,256]{1,0:T(8,128)(2,1)S(1)} collective-permute-done((f16[224,256]{1,0:T(8,128)(2,1)S(1)}, f16[224,256]{1,0:T(8,128)(2,1)S(1)}, u32[]{:S(2)}, u32[]{:S(2)}) %collective-permute-start.17) | collective-permute-done | bytes 114720 | tf_op jit(solution)/shard_map/ppermute | solution.py:33
  98.1 0.3 fusion.14
  98.7 1.5 %collective-permute-start.20 = (f16[352,256]{1,0:T(8,128)(2,1)S(1)}, f16[352,256]{1,0:T(8,128)(2,1)S(1)}, u32[]{:S(2)}, u32[]{:S(2)}) collective-permute-start(f16[352,256]{1,0:T(8,128)(2,1)S(1)} %get-tuple-element.151), channel_id=1, source_target_pairs={{0,16},{8,24},{16,0},{24,8},{1,17},{9,25},{17,1},{25,9},{2,18},{10... | collective-permute-start | bytes 540680 | tf_op jit(solution)/shard_map/ppermute | solution.py:28
  100.3 4.0 %collective-permute-done.20 = f16[352,256]{1,0:T(8,128)(2,1)S(1)} collective-permute-done((f16[352,256]{1,0:T(8,128)(2,1)S(1)}, f16[352,256]{1,0:T(8,128)(2,1)S(1)}, u32[]{:S(2)}, u32[]{:S(2)}) %collective-permute-start.20) | collective-permute-done | bytes 180256 | tf_op jit(solution)/shard_map/ppermute | solution.py:28
  104.5 1.6 %collective-permute-done.21 = f16[2,352,256]{2,1,0:T(8,128)(2,1)S(1)} collective-permute-done((f16[2,352,256]{2,1,0:T(8,128)(2,1)S(1)}, f16[2,352,256]{2,1,0:T(8,128)(2,1)S(1)}, u32[]{:S(2)}, u32[]{:S(2)}) %collective-permute-start.21) | collective-permute-done | bytes 360480 | tf_op jit(solution)/shard_map/ppermute | solution.py:28
  106.1 0.2 select_bitcast_fusion.3
  106.4 0.2 pad_maximum_fusion.1
  106.7 0.3 select_multiply_fusion
  107.2 0.8 copy.8
  108.3 1.3 %copy.7 = f32[1024,256]{0,1:T(8,128)} copy(f32[1024,256]{1,0:T(8,128)S(1)} %bitcast.209) | data formatting | bytes 2097152 | tf_op jit(solution)/shard_map/reshape | solution.py:469
  (103 shorter events, 1.9 us)
Async XLA Ops:
  0.6 7.1 %collective-permute-start.3 = (bf16[384,2048]{1,0:T(8,128)(2,1)}, bf16[384,2048]{1,0:T(8,128)(2,1)S(1)}, u32[]{:S(2)}, u32[]{:S(2)}) collective-permute-start(bf16[384,2048]{1,0:T(8,128)(2,1)} %refs_3_.1), channel_id=1, source_target_pairs={{0,8},{8,0},{16,24},{24,16},{1,9},{9,1},{17,25},{25,17},{2,10},{10... | collective-permute-start | bytes 4718600 | tf_op jit(solution)/shard_map/ppermute | solution.py:28
  1.1 1.4 %copy-start.3 = (bf16[384,2048]{1,0:T(8,128)(2,1)S(1)}, bf16[384,2048]{1,0:T(8,128)(2,1)}, u32[]{:S(2)}) copy-start(bf16[384,2048]{1,0:T(8,128)(2,1)} %refs_3_.1) | copy-start | bytes 4718596
  3.4 19.5 %collective-permute-start.2 = (bf16[128,2048]{1,0:T(8,128)(2,1)}, bf16[128,2048]{1,0:T(8,128)(2,1)}, u32[]{:S(2)}, u32[]{:S(2)}) collective-permute-start(bf16[128,2048]{1,0:T(8,128)(2,1)} %shard_map.51), channel_id=1, source_target_pairs={{0,16},{8,24},{16,0},{24,8},{1,17},{9,25},{17,1},{25,9},{2,18},{10... | collective-permute-start | bytes 1572872 | tf_op jit(solution)/shard_map/ppermute | solution.py:28
  6.9 0.8 copy-start.18
  7.7 25.0 %collective-permute-start.1 = (bf16[128,2048]{1,0:T(8,128)(2,1)}, bf16[128,2048]{1,0:T(8,128)(2,1)}, u32[]{:S(2)}, u32[]{:S(2)}) collective-permute-start(bf16[128,2048]{1,0:T(8,128)(2,1)} %get-tuple-element.52), channel_id=1, source_target_pairs={{0,16},{8,24},{16,0},{24,8},{1,17},{9,25},{17,1},{25,9},{2,18},{10... | collective-permute-start | bytes 1572872 | tf_op jit(solution)/shard_map/ppermute | solution.py:28
  7.7 1.2 %copy-start.11 = (bf16[384,2048]{1,0:T(8,128)(2,1)}, bf16[384,2048]{1,0:T(8,128)(2,1)S(1)}, u32[]{:S(2)}) copy-start(bf16[384,2048]{1,0:T(8,128)(2,1)S(1)} %collective-permute-done.3.refs_4_) | copy-start | bytes 4718596
  8.9 2.2 %copy-start = (bf16[2048,1024]{1,0:T(8,128)(2,1)S(1)}, bf16[2048,1024]{1,0:T(8,128)(2,1)}, u32[]{:S(2)}) copy-start(bf16[2048,1024]{1,0:T(8,128)(2,1)} %refs_1_.7) | copy-start | bytes 12582916
  11.1 1.2 %copy-start.2 = (bf16[1024,512]{1,0:T(8,128)(2,1)S(1)}, bf16[1024,512]{1,0:T(8,128)(2,1)}, u32[]{:S(2)}) copy-start(bf16[1024,512]{1,0:T(8,128)(2,1)} %refs_2_.7) | copy-start | bytes 3145732
  12.3 1.4 %copy-start.4 = (bf16[384,2048]{1,0:T(8,128)(2,1)S(1)}, bf16[384,2048]{1,0:T(8,128)(2,1)}, u32[]{:S(2)}) copy-start(bf16[384,2048]{1,0:T(8,128)(2,1)} %refs_3_.1) | copy-start | bytes 4718596
  13.7 1.4 %copy-start.12 = (bf16[384,2048]{1,0:T(8,128)(2,1)S(1)}, bf16[384,2048]{1,0:T(8,128)(2,1)}, u32[]{:S(2)}) copy-start(bf16[384,2048]{1,0:T(8,128)(2,1)} %copy-done.11) | copy-start | bytes 4718596
  15.1 9.5 %copy-start.19 = (bf16[128,2048]{1,0:T(8,128)(2,1)S(1)}, bf16[128,2048]{1,0:T(8,128)(2,1)}, u32[]{:S(2)}) copy-start(bf16[128,2048]{1,0:T(8,128)(2,1)} %copy-done.18) | copy-start | bytes 1572868
  15.1 11.5 %copy-start.1 = (bf16[2048,1024]{1,0:T(8,128)(2,1)S(1)}, bf16[2048,1024]{1,0:T(8,128)(2,1)}, u32[]{:S(2)}) copy-start(bf16[2048,1024]{1,0:T(8,128)(2,1)} %refs_1_.7) | copy-start | bytes 12582916
  24.0 2.6 %collective-permute-start.4 = (bf16[64,2048]{1,0:T(8,128)(2,1)S(1)}, bf16[64,2048]{1,0:T(8,128)(2,1)S(1)}, u32[]{:S(2)}, u32[]{:S(2)}) collective-permute-start(bf16[64,2048]{1,0:T(8,128)(2,1)S(1)} %get-tuple-element.54), channel_id=1, source_target_pairs={{0,8},{8,0},{16,24},{24,16},{1,9},{9,1},{17,25},{25,17},{2,10},{10... | collective-permute-start | bytes 786440 | tf_op jit(solution)/shard_map/ppermute | solution.py:28
  24.3 2.3 %collective-permute-start.5 = (bf16[64,2048]{1,0:T(8,128)(2,1)S(1)}, bf16[64,2048]{1,0:T(8,128)(2,1)S(1)}, u32[]{:S(2)}, u32[]{:S(2)}) collective-permute-start(bf16[64,2048]{1,0:T(8,128)(2,1)S(1)} %get-tuple-element.55), channel_id=1, source_target_pairs={{0,8},{8,0},{16,24},{24,16},{1,9},{9,1},{17,25},{25,17},{2,10},{10... | collective-permute-start | bytes 786440 | tf_op jit(solution)/shard_map/ppermute | solution.py:28
  24.6 17.8 %collective-permute-start = (bf16[128,2048]{1,0:T(8,128)(2,1)S(1)}, bf16[128,2048]{1,0:T(8,128)(2,1)S(1)}, u32[]{:S(2)}, u32[]{:S(2)}) collective-permute-start(bf16[128,2048]{1,0:T(8,128)(2,1)S(1)} %copy-done.19), channel_id=1, source_target_pairs={{0,16},{8,24},{16,0},{24,8},{1,17},{9,25},{17,1},{25,9},{2,18},{10... | collective-permute-start | bytes 1572872 | tf_op jit(solution)/shard_map/ppermute | solution.py:28
  32.7 11.8 %copy-start.5 = (bf16[256,2048]{1,0:T(8,128)(2,1)}, bf16[256,2048]{1,0:T(8,128)(2,1)S(1)}, u32[]{:S(2)}) copy-start(bf16[256,2048]{1,0:T(8,128)(2,1)S(1)} %get-tuple-element.64.refs_10_.refs_5_) | copy-start | bytes 3145732
  34.2 1.6 %collective-permute-start.6 = (bf16[64,2048]{1,0:T(8,128)(2,1)S(1)}, bf16[64,2048]{1,0:T(8,128)(2,1)S(1)}, u32[]{:S(2)}, u32[]{:S(2)}) collective-permute-start(bf16[64,2048]{1,0:T(8,128)(2,1)S(1)} %get-tuple-element.61), channel_id=1, source_target_pairs={{0,8},{8,0},{16,24},{24,16},{1,9},{9,1},{17,25},{25,17},{2,10},{10... | collective-permute-start | bytes 786440 | tf_op jit(solution)/shard_map/ppermute | solution.py:28
  34.3 1.9 %collective-permute-start.7 = (bf16[64,2048]{1,0:T(8,128)(2,1)S(1)}, bf16[64,2048]{1,0:T(8,128)(2,1)S(1)}, u32[]{:S(2)}, u32[]{:S(2)}) collective-permute-start(bf16[64,2048]{1,0:T(8,128)(2,1)S(1)} %get-tuple-element.62), channel_id=1, source_target_pairs={{0,8},{8,0},{16,24},{24,16},{1,9},{9,1},{17,25},{25,17},{2,10},{10... | collective-permute-start | bytes 786440 | tf_op jit(solution)/shard_map/ppermute | solution.py:28
  42.4 9.2 %copy-start.7 = (bf16[256,2048]{1,0:T(8,128)(2,1)}, bf16[256,2048]{1,0:T(8,128)(2,1)S(1)}, u32[]{:S(2)}) copy-start(bf16[256,2048]{1,0:T(8,128)(2,1)S(1)} %get-tuple-element.73.refs_14_.refs_6_) | copy-start | bytes 3145732
  42.5 1.6 %collective-permute-start.8 = (bf16[64,2048]{1,0:T(8,128)(2,1)S(1)}, bf16[64,2048]{1,0:T(8,128)(2,1)S(1)}, u32[]{:S(2)}, u32[]{:S(2)}) collective-permute-start(bf16[64,2048]{1,0:T(8,128)(2,1)S(1)} %get-tuple-element.69), channel_id=1, source_target_pairs={{0,8},{8,0},{16,24},{24,16},{1,9},{9,1},{17,25},{25,17},{2,10},{10... | collective-permute-start | bytes 786440 | tf_op jit(solution)/shard_map/ppermute | solution.py:28
  42.7 1.8 %collective-permute-start.9 = (bf16[64,2048]{1,0:T(8,128)(2,1)S(1)}, bf16[64,2048]{1,0:T(8,128)(2,1)S(1)}, u32[]{:S(2)}, u32[]{:S(2)}) collective-permute-start(bf16[64,2048]{1,0:T(8,128)(2,1)S(1)} %get-tuple-element.70), channel_id=1, source_target_pairs={{0,8},{8,0},{16,24},{24,16},{1,9},{9,1},{17,25},{25,17},{2,10},{10... | collective-permute-start | bytes 786440 | tf_op jit(solution)/shard_map/ppermute | solution.py:28
  51.6 1.0 copy-start.14
  52.6 0.8 copy-start.16
  53.4 2.8 %collective-permute-start.11 = (f32[128,1024]{1,0:T(8,128)}, f32[128,1024]{1,0:T(8,128)}, u32[]{:S(2)}, u32[]{:S(2)}) collective-permute-start(f32[128,1024]{1,0:T(8,128)} %get-tuple-element.86), channel_id=1, source_target_pairs={{0,8},{8,0},{16,24},{24,16},{1,9},{9,1},{17,25},{25,17},{2,10},{10... | collective-permute-start | bytes 1572872 | tf_op jit(solution)/shard_map/ppermute | solution.py:28
  53.5 2.7 %collective-permute-start.10 = (bf16[256,768]{1,0:T(8,128)(2,1)}, bf16[256,768]{1,0:T(8,128)(2,1)}, u32[]{:S(2)}, u32[]{:S(2)}) collective-permute-start(bf16[256,768]{1,0:T(8,128)(2,1)} %get-tuple-element.84), channel_id=1, source_target_pairs={{0,8},{8,0},{16,24},{24,16},{1,9},{9,1},{17,25},{25,17},{2,10},{10... | collective-permute-start | bytes 1179656 | tf_op jit(solution)/shard_map/ppermute | solution.py:28
  56.2 1.2 %copy-start.6 = (bf16[256,2048]{1,0:T(8,128)(2,1)S(1)}, bf16[256,2048]{1,0:T(8,128)(2,1)}, u32[]{:S(2)}) copy-start(bf16[256,2048]{1,0:T(8,128)(2,1)} %copy-done.5) | copy-start | bytes 3145732
  57.4 1.2 %copy-start.8 = (bf16[256,2048]{1,0:T(8,128)(2,1)S(1)}, bf16[256,2048]{1,0:T(8,128)(2,1)}, u32[]{:S(2)}) copy-start(bf16[256,2048]{1,0:T(8,128)(2,1)} %copy-done.7) | copy-start | bytes 3145732
  58.7 1.2 %copy-start.15 = (bf16[256,2048]{1,0:T(8,128)(2,1)S(1)}, bf16[256,2048]{1,0:T(8,128)(2,1)}, u32[]{:S(2)}) copy-start(bf16[256,2048]{1,0:T(8,128)(2,1)} %copy-done.14) | copy-start | bytes 3145732
  59.9 1.0 copy-start.17
  65.0 1.0 copy-start.13
  65.0 1.6 %copy-start.9 = (f32[8,224,256]{2,1,0:T(8,128)}, f32[8,224,256]{2,1,0:T(8,128)S(1)}, u32[]{:S(2)}) copy-start(f32[8,224,256]{2,1,0:T(8,128)S(1)} %get-tuple-element.89) | copy-start | bytes 5505028
  66.9 17.3 %collective-permute-start.12 = (f16[4,224,256]{2,1,0:T(8,128)(2,1)S(1)}, f16[4,224,256]{2,1,0:T(8,128)(2,1)S(1)}, u32[]{:S(2)}, u32[]{:S(2)}) collective-permute-start(f16[4,224,256]{2,1,0:T(8,128)(2,1)S(1)} %multiply_convert_fusion), channel_id=1, source_target_pairs={{0,1},{1,0},{2,3},{3,2},{4,5},{5,4},{6,7},{7,6},{8,9},{9,8},{10,11... | collective-permute-start | bytes 1376264 | tf_op jit(solution)/shard_map/ppermute | solution.py:33
  68.5 16.0 %copy-start.10 = (f32[8,224,256]{2,1,0:T(8,128)S(1)}, f32[8,224,256]{2,1,0:T(8,128)}, u32[]{:S(2)}) copy-start(f32[8,224,256]{2,1,0:T(8,128)} %copy-done.9) | copy-start | bytes 5505028
  69.5 7.1 %collective-permute-start.13 = (f16[2,128,256]{2,1,0:T(8,128)(2,1)}, f16[2,128,256]{2,1,0:T(8,128)(2,1)S(1)}, u32[]{:S(2)}, u32[]{:S(2)}) collective-permute-start(f16[2,128,256]{2,1,0:T(8,128)(2,1)} %get-tuple-element.160), channel_id=1, source_target_pairs={{0,2},{1,3},{2,0},{3,1},{4,6},{5,7},{6,4},{7,5},{8,10},{9,11},{10,... | collective-permute-start | bytes 393224 | tf_op jit(solution)/shard_map/ppermute | solution.py:33
  71.0 13.2 %collective-permute-start.14 = (f16[2,128,256]{2,1,0:T(8,128)(2,1)}, f16[2,128,256]{2,1,0:T(8,128)(2,1)S(1)}, u32[]{:S(2)}, u32[]{:S(2)}) collective-permute-start(f16[2,128,256]{2,1,0:T(8,128)(2,1)} %get-tuple-element.159), channel_id=1, source_target_pairs={{0,4},{1,5},{2,6},{3,7},{4,0},{5,1},{6,2},{7,3},{8,12},{9,13},{10,... | collective-permute-start | bytes 393224 | tf_op jit(solution)/shard_map/ppermute | solution.py:33
  73.6 10.6 %collective-permute-start.15 = (f16[2,128,256]{2,1,0:T(8,128)(2,1)S(1)}, f16[2,128,256]{2,1,0:T(8,128)(2,1)S(1)}, u32[]{:S(2)}, u32[]{:S(2)}) collective-permute-start(f16[2,128,256]{2,1,0:T(8,128)(2,1)S(1)} %get-tuple-element.158), channel_id=1, source_target_pairs={{0,6},{1,7},{2,4},{3,5},{4,2},{5,3},{6,0},{7,1},{8,14},{9,15},{10,... | collective-permute-start | bytes 393224 | tf_op jit(solution)/shard_map/ppermute | solution.py:33
  85.4 10.2 %collective-permute-start.16 = (f16[224,256]{1,0:T(8,128)(2,1)S(1)}, f16[224,256]{1,0:T(8,128)(2,1)S(1)}, u32[]{:S(2)}, u32[]{:S(2)}) collective-permute-start(f16[224,256]{1,0:T(8,128)(2,1)S(1)} %get-tuple-element.105), channel_id=1, source_target_pairs={{0,2},{1,3},{2,0},{3,1},{4,6},{5,7},{6,4},{7,5},{8,10},{9,11},{10,... | collective-permute-start | bytes 344072 | tf_op jit(solution)/shard_map/ppermute | solution.py:33
  87.4 10.5 %collective-permute-start.17 = (f16[224,256]{1,0:T(8,128)(2,1)S(1)}, f16[224,256]{1,0:T(8,128)(2,1)S(1)}, u32[]{:S(2)}, u32[]{:S(2)}) collective-permute-start(f16[224,256]{1,0:T(8,128)(2,1)S(1)} %get-tuple-element.104), channel_id=1, source_target_pairs={{0,4},{1,5},{2,6},{3,7},{4,0},{5,1},{6,2},{7,3},{8,12},{9,13},{10,... | collective-permute-start | bytes 344072 | tf_op jit(solution)/shard_map/ppermute | solution.py:33
  88.5 9.4 %collective-permute-start.18 = (f16[224,256]{1,0:T(8,128)(2,1)S(1)}, f16[224,256]{1,0:T(8,128)(2,1)S(1)}, u32[]{:S(2)}, u32[]{:S(2)}) collective-permute-start(f16[224,256]{1,0:T(8,128)(2,1)S(1)} %get-tuple-element.103), channel_id=1, source_target_pairs={{0,6},{1,7},{2,4},{3,5},{4,2},{5,3},{6,0},{7,1},{8,14},{9,15},{10,... | collective-permute-start | bytes 344072 | tf_op jit(solution)/shard_map/ppermute | solution.py:33
  91.3 4.3 %collective-permute-start.19 = (f16[128,256]{1,0:T(8,128)(2,1)S(1)}, f16[128,256]{1,0:T(8,128)(2,1)S(1)}, u32[]{:S(2)}, u32[]{:S(2)}) collective-permute-start(f16[128,256]{1,0:T(8,128)(2,1)S(1)} %fusion.19), channel_id=1, source_target_pairs={{0,1},{1,0},{2,3},{3,2},{4,5},{5,4},{6,7},{7,6},{8,9},{9,8},{10,11... | collective-permute-start | bytes 196616 | tf_op jit(solution)/shard_map/ppermute | solution.py:33
  98.7 5.6 %collective-permute-start.20 = (f16[352,256]{1,0:T(8,128)(2,1)S(1)}, f16[352,256]{1,0:T(8,128)(2,1)S(1)}, u32[]{:S(2)}, u32[]{:S(2)}) collective-permute-start(f16[352,256]{1,0:T(8,128)(2,1)S(1)} %get-tuple-element.151), channel_id=1, source_target_pairs={{0,16},{8,24},{16,0},{24,8},{1,17},{9,25},{17,1},{25,9},{2,18},{10... | collective-permute-start | bytes 540680 | tf_op jit(solution)/shard_map/ppermute | solution.py:28
  104.4 1.7 %collective-permute-start.21 = (f16[2,352,256]{2,1,0:T(8,128)(2,1)S(1)}, f16[2,352,256]{2,1,0:T(8,128)(2,1)S(1)}, u32[]{:S(2)}, u32[]{:S(2)}) collective-permute-start(f16[2,352,256]{2,1,0:T(8,128)(2,1)S(1)} %pad_maximum_fusion.2), channel_id=1, source_target_pairs={{0,8},{8,0},{16,24},{24,16},{1,9},{9,1},{17,25},{25,17},{2,10},{10... | collective-permute-start | bytes 1081352 | tf_op jit(solution)/shard_map/ppermute | solution.py:28

commit v2 on v1

--- a/solution.py
+++ b/solution.py
@@ -66,7 +66,7 @@
     feats[:tok] = i["own"][...]
     feats[tok:] = i["sib"][...]
     embed = encode(
-        i["place"][0], feats, tok, i["w_first"], i["w_second"], o["hidden"], o["gate"], s["acc"]
+        lax.axis_index("blk"), feats, tok, i["w_first"], i["w_second"], o["hidden"], o["gate"], s["acc"]
     )
     o["embed"][...] = embed
     wide = feats[...].astype(F32)
@@ -116,7 +116,7 @@
     embed = [i["embed", j] for j in range(k)]
     sq = [i["sq", j] for j in range(k)] + [o["sq"]]
     embed_new = encode(
-        i["place"][0], feats[k], part, i["w_first"], i["w_second"], o["hidden"], o["gate"], s["acc"]
+        lax.axis_index("blk"), feats[k], part, i["w_first"], i["w_second"], o["hidden"], o["gate"], s["acc"]
     )
     o["embed"][...] = embed_new
     summed = [o["summed", j] for j in range(k + 1)]
@@ -129,7 +129,7 @@
 
 def last_stage(factor, i, o, s):
     k = CHUNKS
-    place = i["place"][0]
+    place = lax.axis_index("blk")
     next_stage(k, i, {**s, **o}, s)
     tok, part = i["summed", 0].shape[0], i["rem"].shape[0]
     wide = i["w_second"].shape[1] // 4
@@ -178,8 +178,10 @@
     exp_second = jnp.broadcast_to(exp_second, (8, 256))
     one, two = o["one"], o["two"]
     top, bottom = CUT, 256 - CUT
+    s["second"][...] = second
+    me = lax.axis_index("dp") // (lax.axis_size("dp") // 8)
     for d in range(8):
-        block = second[:, d * 128 : (d + 1) * 128]
+        block = s["second"][:, pl.ds(pl.multiple_of((me ^ d) * 128, 128), 128)]
         one[d, top : top + 64, :128] = block[:64]
         one[d, top : top + 64, 128:] = block[64:]
         one[d, top + 64 : top + 72] = exp_first
@@ -193,11 +195,12 @@
     o["kind_two"][bottom:] = jnp.full((16, 256), 2.0, F32)
     for d in range(8):
         block, at = None, 0
+        lanes = pl.ds(pl.multiple_of((me ^ d) * 256, 256), 256)
         for j in range(CHUNKS + 1):
             f = i["feats", j]
             count = f.shape[0] // 2
             for half, name in enumerate(("keep", "got")):
-                rows = f[half * count : (half + 1) * count, d * 256 : (d + 1) * 256]
+                rows = f[half * count : (half + 1) * count, lanes]
                 piece = dot(i[name][:, at : at + count], rows)
                 block = piece if block is None else block + piece
             at += count
@@ -215,7 +218,7 @@
         body(i, o, dict(zip(names_s, refs[n + m :])))
 
     vmem = pltpu.VMEM
-    spaces = {"place": pltpu.SMEM, "arg": pl.ANY}
+    spaces = {"arg": pl.ANY}
     shapes = [jax.ShapeDtypeStruct(*v) for v in outs.values()]
     got = pl.pallas_call(
         kernel,
@@ -245,6 +248,17 @@
         copy.wait()
 
 
+def place_quarters(i, o, s):
+    me = lax.axis_index("blk")
+    for j in range(4):
+        q = me ^ j
+        first = jnp.concatenate([i["one"][j, :CUT], i["two"][j, : 256 - CUT]], 0)
+        o["first"][:, pl.ds(pl.multiple_of(q * 256, 256), 256)] = first.T
+        block = i["one"][j, CUT : CUT + 64]
+        second = jnp.concatenate([block[:, :128], block[:, 128:]], 0)
+        o["second"][:, pl.ds(pl.multiple_of(q * 128, 128), 128)] = second.T
+
+
 def encode16(total, kind, tail):
     first, second = exps_of(total, tail)
     e = jnp.where(kind == 0.0, first, second)
@@ -271,22 +285,27 @@
 
 
 def pick(total, axis, index):
+    if isinstance(index, int):
+        return lax.index_in_dim(total, index, axis, keepdims=False)
     return lax.dynamic_index_in_dim(total, index, axis, keepdims=False)
 
 
 class Sum:
-    def __init__(self, total, kind, order):
+    def __init__(self, total, kind, order, relative):
         self.total, self.kind = total, kind
         self.tail = total.shape[-2] - 16
         self.axes = list(range(total.ndim - 2))
-        self.order = order
+        self.order, self.relative = order, relative
 
     def send(self, step, shifts):
         axis = self.order[step]
-        at, size = self.axes.index(axis), self.total.shape[self.axes.index(axis)]
-        me = (lax.axis_index("dp") >> shifts[axis]) & (size - 1)
+        at = self.axes.index(axis)
+        size = self.total.shape[at]
+        me = 0
+        if axis >= self.relative:
+            me = (lax.axis_index("dp") >> shifts[axis]) & (size - 1)
         gots = []
-        for o in range(1, size):
+        for o in range(size - 1, 0, -1):
             give = pick(self.total, at, me ^ o)
             gots.append(dp_swap(encode16(give, self.kind, self.tail), o << shifts[axis]))
         self.axes.pop(at)
@@ -324,14 +343,12 @@
     all_rows = group_rows * dp_count
     factor = 2.0 / math.sqrt(group_rows * all_rows)
     bits = dp_count.bit_length() - 1
-    b = lax.axis_index("blk")
-    y, c = b >> 1, b & 1
-    place = b.astype(jnp.int32).reshape(1)
     k = CHUNKS
     part = tok // k
 
     rem = []
-    for start, count in ((0, 1), (1, k - 1)):
+    rem.append(blk_swap(fingerprints[:part], 2))
+    for start, count in ((1, k - 1),):
         names = [("rows", j) for j in range(start, start + count)]
         out = run(
             functools.partial(fetch, [("arg", j * part, part, ("rows", j)) for _, j in names]),
@@ -344,7 +361,7 @@
     sib = blk_swap(fingerprints, 1)
     rs = []
 
-    base = {"place": place, "w_first": w_first, "w_second": w_second}
+    base = {"w_first": w_first, "w_second": w_second}
     out = run(
         first_stage,
         {**base, "own": fingerprints, "sib": sib},
@@ -435,7 +452,7 @@
             "kind_one": ((rows_one, 256), F32),
             "kind_two": ((rows_two, 256), F32),
         },
-        {},
+        {"second": ((emb // 4, hid), F32)},
     )
     lanes = 256 * 8 // dp_count
     extra = dp_count // 8
@@ -443,11 +460,11 @@
     two = split_lanes(out["two"], (0, 0), extra)
     kind_one, kind_two = out["kind_one"][:, :lanes], out["kind_two"][:, :lanes]
     more = extra.bit_length() - 1
-    shape = (2,) * more + (4, 2)
-    shifts = [3 + more - 1 - n for n in range(more)] + [1, 0]
-    zed, ex, rest = more, more + 1, list(range(more))
-    one = Sum(one.reshape(shape + one.shape[1:]), kind_one, [ex, zed] + rest)
-    two = Sum(two.reshape(shape + two.shape[1:]), kind_two, [zed] + rest + [ex])
+    shape = (4, 2) + (2,) * more
+    shifts = [more + 1, more] + [more - 1 - n for n in range(more)]
+    rest = list(range(2, more + 2))
+    one = Sum(one.reshape(shape + one.shape[1:]), kind_one, [1, 0] + rest, 2)
+    two = Sum(two.reshape(shape + two.shape[1:]), kind_two, [0] + rest + [1], 2)
     for step in range(more + 2):
         gots = lax.optimization_barrier((one.send(step, shifts), two.send(step, shifts)))
         one.receive(gots[0])
@@ -459,15 +476,21 @@
     across = blk_swap(packed, 2)
     pair = jnp.stack([packed, across])
     beside = blk_swap(pair, 1)
-    here = halves(jnp.stack([packed, beside[0]]), 0, c)
-    there = halves(jnp.stack([across, beside[1]]), 0, c)
-    low = [jnp.where(y == 0, h, t) for h, t in zip(here, there)]
-    high = [jnp.where(y == 0, t, h) for h, t in zip(here, there)]
-    every = jnp.stack(low + high)
+    every = jnp.stack([packed, beside[0], across, beside[1]])
     one = decode16(every[:, :rows_one], kind_one, one.tail)
     two = decode16(every[:, rows_one:], kind_two, two.tail)
-    first = jnp.concatenate([one[:, :CUT], two[:, : 256 - CUT]], 1).reshape(hid, lanes)
-    second = one[:, CUT : CUT + 64]
+    if extra == 1:
+        out = run(
+            place_quarters,
+            {"one": one, "two": two},
+            {"first": ((lanes, hid), F32), "second": ((lanes // 2, emb), F32)},
+            {},
+        )
+        return out["first"], out["second"]
+    b = lax.axis_index("blk")
+    order = jnp.arange(4) ^ b
+    first = jnp.concatenate([one[:, :CUT], two[:, : 256 - CUT]], 1)[order].reshape(hid, lanes)
+    second = one[order, CUT : CUT + 64]
     second = jnp.concatenate([second[..., : lanes // 2], second[..., lanes // 2 :]], 1)
     return first.T, second.reshape(emb, lanes // 2).T
 

time: 110 us -> 96.1 us (0.87)
  local copies, waits for them, and re-layouts: 19.9 us -> 6.15 us
  waiting for transfers between devices: 27.2 us -> 35.4 us
  Pallas kernels: 35.6 us -> 29.2 us
  other arithmetic: 5.46 us -> 3.56 us
    unnamed x58 -> x26, local copies, waits for them, and re-layouts: 17.5 us -> 4.85 us
    ppermute x14, waiting for transfers between devices: 10.8 us -> 17.8 us  [blk_swap(): return lax.ppermute(value, 'blk', [(b, b ^ bit) for b in range(count)])]
    pallas_call x10, Pallas kernels: 35.6 us -> 29.2 us  [run(): pl.pallas_call(kernel, out_shape=shapes, in_specs=[pl.BlockSpec(memory_sp...]
    reshape x2 -> x0, local copies, waits for them, and re-layouts: 2.15 us -> none  [the longest x1 1.31 us: per_device(): jnp.concatenate([one[:, :CUT], two[:, :256 - CUT]], 1).reshape(hid, lanes)]
  transfers between devices with their start and end apart: 22 -> 22, of which waited for: 11 -> 13; matrix products, arithmetic and copies ran while one was open for 2% -> 1% of each run, Pallas kernels for 22% -> 19%
where the time goes in v2:
time: 96.1 us; the launch traced here: 95.9 us
  waiting for transfers between devices  35.4 us (37%)
  Pallas kernels  29.2 us (30%)
  starting transfers between devices  20.5 us (21%)
  local copies, waits for them, and re-layouts  6.15 us (6%)
  other arithmetic  3.56 us (4%)
  between operations  1.17 us (1%)
    pallas_call x10, Pallas kernels, run(): pl.pallas_call(kernel, out_shape=shapes, in_specs=[pl.BlockSpec(memory_sp...  29.2 us
    ppermute x14, waiting for transfers between devices, blk_swap(): return lax.ppermute(value, 'blk', [(b, b ^ bit) for b in range(count)])  17.8 us
    ppermute x8, waiting for transfers between devices, dp_swap(): return lax.ppermute(value, 'dp', [(d, d ^ bit) for d in range(count)])  17.5 us
    ppermute x8, starting transfers between devices, dp_swap(): return lax.ppermute(value, 'dp', [(d, d ^ bit) for d in range(count)])  11.4 us
    ppermute x14, starting transfers between devices, blk_swap(): return lax.ppermute(value, 'blk', [(b, b ^ bit) for b in range(count)])  9.14 us
    unnamed x26, local copies, waits for them, and re-layouts  4.85 us
  transfers between devices with their start and end apart: 22, of which 13 were waited for; matrix products, arithmetic and copies ran while one was open for 1% of the time, Pallas kernels for 19%

profile of v2, /device:TPU:0, one launch (start us, length us, event | category | flops | bytes accessed | tf_op | source)
XLA Modules:
  0.0 95.9 jit_solution(10854287935929168023)
XLA Ops:
  0.6 0.5 collective-permute-start.3
  1.2 1.1 %slice.197 = bf16[128,2048]{1,0:T(8,128)(2,1)S(1)} slice(bf16[384,2048]{1,0:T(8,128)(2,1)} %refs_2_.1), slice={[0:128], [0:2048]} | slice | bytes 1048576 | tf_op jit(solution)/shard_map/slice | solution.py:350
  2.2 2.7 %collective-permute-start.2 = (bf16[128,2048]{1,0:T(8,128)(2,1)S(1)}, bf16[128,2048]{1,0:T(8,128)(2,1)S(1)}, u32[]{:S(2)}, u32[]{:S(2)}) collective-permute-start(bf16[128,2048]{1,0:T(8,128)(2,1)S(1)} %slice.197), channel_id=1, source_target_pairs={{0,16},{8,24},{16,0},{24,8},{1,17},{9,25},{17,1},{25,9},{2,18},{10... | collective-permute-start | bytes 1572872 | tf_op jit(solution)/shard_map/ppermute | solution.py:28
  4.9 1.4 %copy-done.3 = bf16[384,2048]{1,0:T(8,128)(2,1)S(1)} copy-done((bf16[384,2048]{1,0:T(8,128)(2,1)S(1)}, bf16[384,2048]{1,0:T(8,128)(2,1)}, u32[]{:S(2)}) %copy-start.3) | copy-done | bytes 1572888
  6.3 0.1 shard_map.50
  6.4 0.1 collective-permute-start.1
  6.5 1.2 %copy-done.4 = bf16[384,2048]{1,0:T(8,128)(2,1)S(1)} copy-done((bf16[384,2048]{1,0:T(8,128)(2,1)S(1)}, bf16[384,2048]{1,0:T(8,128)(2,1)}, u32[]{:S(2)}) %copy-start.4) | copy-done | bytes 1572888
  7.7 2.2 %copy-done = bf16[2048,1024]{1,0:T(8,128)(2,1)S(1)} copy-done((bf16[2048,1024]{1,0:T(8,128)(2,1)S(1)}, bf16[2048,1024]{1,0:T(8,128)(2,1)}, u32[]{:S(2)}) %copy-start) | copy-done | bytes 4194328
  9.9 7.8 %shard_map.51 = (bf16[768,2048]{1,0:T(8,128)(2,1)S(1)}, bf16[384,1024]{1,0:T(8,128)(2,1)S(1)}, f32[2,256,384]{2,1,0:T(8,128)S(1)}, bf16[768,512]{1,0:T(8,128)(2,...) custom-call(bf16[2048,1024]{1,0:T(8,128)(2,1)S(1)} %copy-done, ...), custom_call_target="tpu_custom_call" | custom-call | flops 1 | bytes 1 | tf_op jit(solution)/shard_map/pallas_call | solution.py:223
  17.8 0.2 collective-permute-start.4
  18.0 0.3 collective-permute-start.5
  18.3 1.9 %collective-permute-start = (bf16[128,2048]{1,0:T(8,128)(2,1)S(1)}, bf16[128,2048]{1,0:T(8,128)(2,1)S(1)}, u32[]{:S(2)}, u32[]{:S(2)}) collective-permute-start(bf16[128,2048]{1,0:T(8,128)(2,1)S(1)} %get-tuple-element.51), channel_id=1, source_target_pairs={{0,16},{8,24},{16,0},{24,8},{1,17},{9,25},{17,1},{25,9},{2,18},{10... | collective-permute-start | bytes 1572872 | tf_op jit(solution)/shard_map/ppermute | solution.py:28
  20.3 5.0 %shard_map.53 = (bf16[256,2048]{1,0:T(8,128)(2,1)S(1)}, bf16[128,1024]{1,0:T(8,128)(2,1)S(1)}, f32[2,256,128]{2,1,0:T(8,128)S(1)}, bf16[256,512]{1,0:T(8,128)(2,...) custom-call(bf16[2048,1024]{1,0:T(8,128)(2,1)S(1)} %copy-done.1, ...), custom_call_target="tpu_custom_call" | custom-call | flops 1 | bytes 1 | tf_op jit(solution)/shard_map/pallas_call | solution.py:223
  25.3 3.7 %collective-permute-done.1.refs_0_.refs_2_ = bf16[128,2048]{1,0:T(8,128)(2,1)S(1)} collective-permute-done((bf16[128,2048]{1,0:T(8,128)(2,1)S(1)}, bf16[128,2048]{1,0:T(8,128)(2,1)S(1)}, u32[]{:S(2)}, u32[]{:S(2)}) %collective-permute-start.1) | collective-permute-done | bytes 524320 | tf_op jit(solution)/shard_map/ppermute | solution.py:28
  29.0 0.1 collective-permute-start.6
  29.0 0.5 collective-permute-start.7
  29.5 1.0 %collective-permute-done.6.refs_3_ = bf16[64,2048]{1,0:T(8,128)(2,1)S(1)} collective-permute-done((bf16[64,2048]{1,0:T(8,128)(2,1)S(1)}, bf16[64,2048]{1,0:T(8,128)(2,1)S(1)}, u32[]{:S(2)}, u32[]{:S(2)}) %collective-permute-start.6) | collective-permute-done | bytes 262176 | tf_op jit(solution)/shard_map/ppermute | solution.py:28
  30.6 0.4 collective-permute-done.7.refs_4_
  30.9 5.2 %shard_map.55 = (bf16[256,2048]{1,0:T(8,128)(2,1)S(1)}, bf16[128,1024]{1,0:T(8,128)(2,1)S(1)}, f32[2,256,128]{2,1,0:T(8,128)S(1)}, bf16[256,512]{1,0:T(8,128)(2,...) custom-call(bf16[2048,1024]{1,0:T(8,128)(2,1)S(1)} %copy-done.1, ...), custom_call_target="tpu_custom_call" | custom-call | flops 1 | bytes 1 | tf_op jit(solution)/shard_map/pallas_call | solution.py:223
  36.1 3.8 %collective-permute-done.refs_0_.refs_2_ = bf16[128,2048]{1,0:T(8,128)(2,1)S(1)} collective-permute-done((bf16[128,2048]{1,0:T(8,128)(2,1)S(1)}, bf16[128,2048]{1,0:T(8,128)(2,1)S(1)}, u32[]{:S(2)}, u32[]{:S(2)}) %collective-permute-start) | collective-permute-done | bytes 524320 | tf_op jit(solution)/shard_map/ppermute | solution.py:28
  39.9 0.1 collective-permute-start.8
  40.0 0.5 collective-permute-start.9
  40.5 1.0 %collective-permute-done.8.refs_3_ = bf16[64,2048]{1,0:T(8,128)(2,1)S(1)} collective-permute-done((bf16[64,2048]{1,0:T(8,128)(2,1)S(1)}, bf16[64,2048]{1,0:T(8,128)(2,1)S(1)}, u32[]{:S(2)}, u32[]{:S(2)}) %collective-permute-start.8) | collective-permute-done | bytes 262176 | tf_op jit(solution)/shard_map/ppermute | solution.py:28
  41.5 0.4 collective-permute-done.9.refs_4_
  41.9 6.6 %shard_map.57 = (bf16[256,2048]{1,0:T(8,128)(2,1)S(1)}, bf16[256,768]{1,0:T(8,128)(2,1)S(1)}, f32[128,1024]{1,0:T(8,128)S(1)}, bf16[256,768]{1,0:T(8,128)(2,1)S(1)}, f32[128,1024]{1,0:T(8,128)S(1)}) custom-call(bf16[2048,1024]{1,0:T(8,128)(2,1)S(1)} %copy-done.1, bf16[1024,512]{1,0:T(8,128)(2,1)S(1)} %copy-done.2, ...), custom_call_target="tpu_custom_call" | custom-call | flops 1 | bytes 1 | tf_op jit(solution)/shard_map/pallas_call | solution.py:223
  48.5 0.2 collective-permute-start.11
  48.7 0.4 collective-permute-start.10
  49.1 2.0 %collective-permute-done.10.refs_1_ = bf16[256,768]{1,0:T(8,128)(2,1)S(1)} collective-permute-done((bf16[256,768]{1,0:T(8,128)(2,1)S(1)}, bf16[256,768]{1,0:T(8,128)(2,1)S(1)}, u32[]{:S(2)}, u32[]{:S(2)}) %collective-permute-start.10) | collective-permute-done | bytes 393248 | tf_op jit(solution)/shard_map/ppermute | solution.py:28
  51.1 3.0 %shard_map.58 = (f32[8,224,256]{2,1,0:T(8,128)S(1)}, f32[8,128,256]{2,1,0:T(8,128)S(1)}, f32[224,256]{1,0:T(8,128)S(1)}, f32[128,256]{1,0:T(8,128)S(1)}) custom-call(bf16[256,768]{1,0:T(8,128)(2,1)S(1)} %get-tuple-element.83.refs_0_, bf16[256,768]{1,0:T(8,128)(2,1)S(1)} %collective-permute-done.10.refs_1_, f32[128,1024]{1,0:T(8,128)S(1)} %get-tuple-element.85.refs_2_, ...), custom_call_target="tpu_custom_call" | custom-call | flops 1 | bytes 1 | tf_op jit(solution)/shard_map/pallas_call | solution.py:223
  54.0 0.1 broadcast_compare_fusion.1
  54.3 0.3 multiply_convert_fusion
  54.6 1.8 %collective-permute-start.12 = (f16[4,224,256]{2,1,0:T(8,128)(2,1)S(1)}, f16[4,224,256]{2,1,0:T(8,128)(2,1)S(1)}, u32[]{:S(2)}, u32[]{:S(2)}) collective-permute-start(f16[4,224,256]{2,1,0:T(8,128)(2,1)S(1)} %multiply_convert_fusion), channel_id=1, source_target_pairs={{0,1},{1,0},{2,3},{3,2},{4,5},{5,4},{6,7},{7,6},{8,9},{9,8},{10,11... | collective-permute-start | bytes 1376264 | tf_op jit(solution)/shard_map/ppermute | solution.py:33
  56.4 0.2 multiply_convert_fusion.1
  56.6 1.6 %collective-permute-start.15 = (f16[2,128,256]{2,1,0:T(8,128)(2,1)S(1)}, f16[2,128,256]{2,1,0:T(8,128)(2,1)S(1)}, u32[]{:S(2)}, u32[]{:S(2)}) collective-permute-start(f16[2,128,256]{2,1,0:T(8,128)(2,1)S(1)} %get-tuple-element.100), channel_id=1, source_target_pairs={{0,2},{1,3},{2,0},{3,1},{4,6},{5,7},{6,4},{7,5},{8,10},{9,11},{10,... | collective-permute-start | bytes 393224 | tf_op jit(solution)/shard_map/ppermute | solution.py:33
  58.3 2.6 %collective-permute-start.14 = (f16[2,128,256]{2,1,0:T(8,128)(2,1)S(1)}, f16[2,128,256]{2,1,0:T(8,128)(2,1)S(1)}, u32[]{:S(2)}, u32[]{:S(2)}) collective-permute-start(f16[2,128,256]{2,1,0:T(8,128)(2,1)S(1)} %get-tuple-element.101), channel_id=1, source_target_pairs={{0,4},{1,5},{2,6},{3,7},{4,0},{5,1},{6,2},{7,3},{8,12},{9,13},{10,... | collective-permute-start | bytes 393224 | tf_op jit(solution)/shard_map/ppermute | solution.py:33
  60.8 0.2 collective-permute-start.13
  61.1 2.5 %collective-permute-done.15 = f16[2,128,256]{2,1,0:T(8,128)(2,1)S(1)} collective-permute-done((f16[2,128,256]{2,1,0:T(8,128)(2,1)S(1)}, f16[2,128,256]{2,1,0:T(8,128)(2,1)S(1)}, u32[]{:S(2)}, u32[]{:S(2)}) %collective-permute-start.15) | collective-permute-done | bytes 131104 | tf_op jit(solution)/shard_map/ppermute | solution.py:33
  63.6 7.6 %collective-permute-done.14 = f16[2,128,256]{2,1,0:T(8,128)(2,1)S(1)} collective-permute-done((f16[2,128,256]{2,1,0:T(8,128)(2,1)S(1)}, f16[2,128,256]{2,1,0:T(8,128)(2,1)S(1)}, u32[]{:S(2)}, u32[]{:S(2)}) %collective-permute-start.14) | collective-permute-done | bytes 131104 | tf_op jit(solution)/shard_map/ppermute | solution.py:33
  71.4 0.3 add_select_fusion.1
  71.7 0.1 convert_element_type.64
  71.8 0.4 add_select_fusion
  72.2 0.5 fusion.1
  72.7 2.0 %collective-permute-start.18 = (f16[224,256]{1,0:T(8,128)(2,1)S(1)}, f16[224,256]{1,0:T(8,128)(2,1)S(1)}, u32[]{:S(2)}, u32[]{:S(2)}) collective-permute-start(f16[224,256]{1,0:T(8,128)(2,1)S(1)} %get-tuple-element.109), channel_id=1, source_target_pairs={{0,2},{1,3},{2,0},{3,1},{4,6},{5,7},{6,4},{7,5},{8,10},{9,11},{10,... | collective-permute-start | bytes 344072 | tf_op jit(solution)/shard_map/ppermute | solution.py:33
  74.7 1.1 %collective-permute-start.17 = (f16[224,256]{1,0:T(8,128)(2,1)S(1)}, f16[224,256]{1,0:T(8,128)(2,1)S(1)}, u32[]{:S(2)}, u32[]{:S(2)}) collective-permute-start(f16[224,256]{1,0:T(8,128)(2,1)S(1)} %get-tuple-element.110), channel_id=1, source_target_pairs={{0,4},{1,5},{2,6},{3,7},{4,0},{5,1},{6,2},{7,3},{8,12},{9,13},{10,... | collective-permute-start | bytes 344072 | tf_op jit(solution)/shard_map/ppermute | solution.py:33
  75.8 1.4 %collective-permute-start.16 = (f16[224,256]{1,0:T(8,128)(2,1)S(1)}, f16[224,256]{1,0:T(8,128)(2,1)S(1)}, u32[]{:S(2)}, u32[]{:S(2)}) collective-permute-start(f16[224,256]{1,0:T(8,128)(2,1)S(1)} %get-tuple-element.111), channel_id=1, source_target_pairs={{0,6},{1,7},{2,4},{3,5},{4,2},{5,3},{6,0},{7,1},{8,14},{9,15},{10,... | collective-permute-start | bytes 344072 | tf_op jit(solution)/shard_map/ppermute | solution.py:33
  77.2 0.1 fusion.7
  77.3 0.6 collective-permute-start.19
  77.9 3.7 %collective-permute-done.19 = f16[128,256]{1,0:T(8,128)(2,1)S(1)} collective-permute-done((f16[128,256]{1,0:T(8,128)(2,1)S(1)}, f16[128,256]{1,0:T(8,128)(2,1)S(1)}, u32[]{:S(2)}, u32[]{:S(2)}) %collective-permute-start.19) | collective-permute-done | bytes 65568 | tf_op jit(solution)/shard_map/ppermute | solution.py:33
  81.6 3.7 %collective-permute-done.17 = f16[224,256]{1,0:T(8,128)(2,1)S(1)} collective-permute-done((f16[224,256]{1,0:T(8,128)(2,1)S(1)}, f16[224,256]{1,0:T(8,128)(2,1)S(1)}, u32[]{:S(2)}, u32[]{:S(2)}) %collective-permute-start.17) | collective-permute-done | bytes 114720 | tf_op jit(solution)/shard_map/ppermute | solution.py:33
  85.3 0.1 add_select_fusion.3
  85.5 0.3 add_select_fusion.2
  85.8 0.1 multiply_convert_fusion.5
  85.9 0.1 multiply_convert_fusion.4
  86.0 1.6 %collective-permute-start.20 = (f16[352,256]{1,0:T(8,128)(2,1)S(1)}, f16[352,256]{1,0:T(8,128)(2,1)S(1)}, u32[]{:S(2)}, u32[]{:S(2)}) collective-permute-start(f16[352,256]{1,0:T(8,128)(2,1)S(1)} %get-tuple-element.147), channel_id=1, source_target_pairs={{0,16},{8,24},{16,0},{24,8},{1,17},{9,25},{17,1},{25,9},{2,18},{10... | collective-permute-start | bytes 540680 | tf_op jit(solution)/shard_map/ppermute | solution.py:28
  87.6 4.0 %collective-permute-done.20 = f16[352,256]{1,0:T(8,128)(2,1)S(1)} collective-permute-done((f16[352,256]{1,0:T(8,128)(2,1)S(1)}, f16[352,256]{1,0:T(8,128)(2,1)S(1)}, u32[]{:S(2)}, u32[]{:S(2)}) %collective-permute-start.20) | collective-permute-done | bytes 180256 | tf_op jit(solution)/shard_map/ppermute | solution.py:28
  91.6 0.1 pad_maximum_fusion.1
  91.7 0.1 collective-permute-start.21
  91.8 1.7 %collective-permute-done.21 = f16[2,352,256]{2,1,0:T(8,128)(2,1)S(1)} collective-permute-done((f16[2,352,256]{2,1,0:T(8,128)(2,1)S(1)}, f16[2,352,256]{2,1,0:T(8,128)(2,1)S(1)}, u32[]{:S(2)}, u32[]{:S(2)}) %collective-permute-start.21) | collective-permute-done | bytes 360480 | tf_op jit(solution)/shard_map/ppermute | solution.py:28
  93.4 0.1 fusion.15
  93.6 0.2 pad_maximum_fusion
  93.8 0.1 slice_convert_fusion
  94.0 0.3 select_multiply_fusion.refs_0_
  94.2 0.2 select_multiply_fusion.1.refs_1_
  94.5 1.5 %shard_map.59 = (f32[256,1024]{1,0:T(8,128)}, f32[128,512]{1,0:T(8,128)}) custom-call(f32[4,224,256]{2,1,0:T(8,128)S(1)} %select_multiply_fusion.refs_0_, f32[4,128,256]{2,1,0:T(8,128)S(1)} %select_multiply_fusion.1.refs_1_), custom_call_target="tpu_custom_call" | custom-call | flops 1 | bytes 1 | tf_op jit(solution)/shard_map/pallas_call | solution.py:223
  (62 shorter events, 0.6 us)
Async XLA Ops:
  0.6 5.9 %copy-start.2 = (bf16[1024,512]{1,0:T(8,128)(2,1)S(1)}, bf16[1024,512]{1,0:T(8,128)(2,1)}, u32[]{:S(2)}) copy-start(bf16[1024,512]{1,0:T(8,128)(2,1)} %refs_1_.7) | copy-start | bytes 3145732
  0.6 5.9 %collective-permute-start.3 = (bf16[384,2048]{1,0:T(8,128)(2,1)}, bf16[384,2048]{1,0:T(8,128)(2,1)S(1)}, u32[]{:S(2)}, u32[]{:S(2)}) collective-permute-start(bf16[384,2048]{1,0:T(8,128)(2,1)} %refs_2_.1), channel_id=1, source_target_pairs={{0,8},{8,0},{16,24},{24,16},{1,9},{9,1},{17,25},{25,17},{2,10},{10... | collective-permute-start | bytes 4718600 | tf_op jit(solution)/shard_map/ppermute | solution.py:28
  2.2 15.5 %collective-permute-start.2 = (bf16[128,2048]{1,0:T(8,128)(2,1)S(1)}, bf16[128,2048]{1,0:T(8,128)(2,1)S(1)}, u32[]{:S(2)}, u32[]{:S(2)}) collective-permute-start(bf16[128,2048]{1,0:T(8,128)(2,1)S(1)} %slice.197), channel_id=1, source_target_pairs={{0,16},{8,24},{16,0},{24,8},{1,17},{9,25},{17,1},{25,9},{2,18},{10... | collective-permute-start | bytes 1572872 | tf_op jit(solution)/shard_map/ppermute | solution.py:28
  4.9 1.4 %copy-start.3 = (bf16[384,2048]{1,0:T(8,128)(2,1)S(1)}, bf16[384,2048]{1,0:T(8,128)(2,1)}, u32[]{:S(2)}) copy-start(bf16[384,2048]{1,0:T(8,128)(2,1)} %refs_2_.1) | copy-start | bytes 4718596
  6.3 1.4 %copy-start.4 = (bf16[384,2048]{1,0:T(8,128)(2,1)S(1)}, bf16[384,2048]{1,0:T(8,128)(2,1)}, u32[]{:S(2)}) copy-start(bf16[384,2048]{1,0:T(8,128)(2,1)} %refs_2_.1) | copy-start | bytes 4718596
  6.4 22.5 %collective-permute-start.1 = (bf16[128,2048]{1,0:T(8,128)(2,1)S(1)}, bf16[128,2048]{1,0:T(8,128)(2,1)S(1)}, u32[]{:S(2)}, u32[]{:S(2)}) collective-permute-start(bf16[128,2048]{1,0:T(8,128)(2,1)S(1)} %get-tuple-element.52), channel_id=1, source_target_pairs={{0,16},{8,24},{16,0},{24,8},{1,17},{9,25},{17,1},{25,9},{2,18},{10... | collective-permute-start | bytes 1572872 | tf_op jit(solution)/shard_map/ppermute | solution.py:28
  7.7 2.2 %copy-start = (bf16[2048,1024]{1,0:T(8,128)(2,1)S(1)}, bf16[2048,1024]{1,0:T(8,128)(2,1)}, u32[]{:S(2)}) copy-start(bf16[2048,1024]{1,0:T(8,128)(2,1)} %refs_0_.9) | copy-start | bytes 12582916
  9.9 10.3 %copy-start.1 = (bf16[2048,1024]{1,0:T(8,128)(2,1)S(1)}, bf16[2048,1024]{1,0:T(8,128)(2,1)}, u32[]{:S(2)}) copy-start(bf16[2048,1024]{1,0:T(8,128)(2,1)} %refs_0_.9) | copy-start | bytes 12582916
  17.8 2.5 %collective-permute-start.4 = (bf16[64,2048]{1,0:T(8,128)(2,1)S(1)}, bf16[64,2048]{1,0:T(8,128)(2,1)S(1)}, u32[]{:S(2)}, u32[]{:S(2)}) collective-permute-start(bf16[64,2048]{1,0:T(8,128)(2,1)S(1)} %get-tuple-element.54), channel_id=1, source_target_pairs={{0,8},{8,0},{16,24},{24,16},{1,9},{9,1},{17,25},{25,17},{2,10},{10... | collective-permute-start | bytes 786440 | tf_op jit(solution)/shard_map/ppermute | solution.py:28
  18.0 2.3 %collective-permute-start.5 = (bf16[64,2048]{1,0:T(8,128)(2,1)S(1)}, bf16[64,2048]{1,0:T(8,128)(2,1)S(1)}, u32[]{:S(2)}, u32[]{:S(2)}) collective-permute-start(bf16[64,2048]{1,0:T(8,128)(2,1)S(1)} %get-tuple-element.55), channel_id=1, source_target_pairs={{0,8},{8,0},{16,24},{24,16},{1,9},{9,1},{17,25},{25,17},{2,10},{10... | collective-permute-start | bytes 786440 | tf_op jit(solution)/shard_map/ppermute | solution.py:28
  18.3 21.6 %collective-permute-start = (bf16[128,2048]{1,0:T(8,128)(2,1)S(1)}, bf16[128,2048]{1,0:T(8,128)(2,1)S(1)}, u32[]{:S(2)}, u32[]{:S(2)}) collective-permute-start(bf16[128,2048]{1,0:T(8,128)(2,1)S(1)} %get-tuple-element.51), channel_id=1, source_target_pairs={{0,16},{8,24},{16,0},{24,8},{1,17},{9,25},{17,1},{25,9},{2,18},{10... | collective-permute-start | bytes 1572872 | tf_op jit(solution)/shard_map/ppermute | solution.py:28
  29.0 1.6 %collective-permute-start.6 = (bf16[64,2048]{1,0:T(8,128)(2,1)S(1)}, bf16[64,2048]{1,0:T(8,128)(2,1)S(1)}, u32[]{:S(2)}, u32[]{:S(2)}) collective-permute-start(bf16[64,2048]{1,0:T(8,128)(2,1)S(1)} %get-tuple-element.61), channel_id=1, source_target_pairs={{0,8},{8,0},{16,24},{24,16},{1,9},{9,1},{17,25},{25,17},{2,10},{10... | collective-permute-start | bytes 786440 | tf_op jit(solution)/shard_map/ppermute | solution.py:28
  29.0 1.9 %collective-permute-start.7 = (bf16[64,2048]{1,0:T(8,128)(2,1)S(1)}, bf16[64,2048]{1,0:T(8,128)(2,1)S(1)}, u32[]{:S(2)}, u32[]{:S(2)}) collective-permute-start(bf16[64,2048]{1,0:T(8,128)(2,1)S(1)} %get-tuple-element.62), channel_id=1, source_target_pairs={{0,8},{8,0},{16,24},{24,16},{1,9},{9,1},{17,25},{25,17},{2,10},{10... | collective-permute-start | bytes 786440 | tf_op jit(solution)/shard_map/ppermute | solution.py:28
  39.9 1.6 %collective-permute-start.8 = (bf16[64,2048]{1,0:T(8,128)(2,1)S(1)}, bf16[64,2048]{1,0:T(8,128)(2,1)S(1)}, u32[]{:S(2)}, u32[]{:S(2)}) collective-permute-start(bf16[64,2048]{1,0:T(8,128)(2,1)S(1)} %get-tuple-element.69), channel_id=1, source_target_pairs={{0,8},{8,0},{16,24},{24,16},{1,9},{9,1},{17,25},{25,17},{2,10},{10... | collective-permute-start | bytes 786440 | tf_op jit(solution)/shard_map/ppermute | solution.py:28
  40.0 1.9 %collective-permute-start.9 = (bf16[64,2048]{1,0:T(8,128)(2,1)S(1)}, bf16[64,2048]{1,0:T(8,128)(2,1)S(1)}, u32[]{:S(2)}, u32[]{:S(2)}) collective-permute-start(bf16[64,2048]{1,0:T(8,128)(2,1)S(1)} %get-tuple-element.70), channel_id=1, source_target_pairs={{0,8},{8,0},{16,24},{24,16},{1,9},{9,1},{17,25},{25,17},{2,10},{10... | collective-permute-start | bytes 786440 | tf_op jit(solution)/shard_map/ppermute | solution.py:28
  48.5 2.5 %collective-permute-start.11 = (f32[128,1024]{1,0:T(8,128)S(1)}, f32[128,1024]{1,0:T(8,128)S(1)}, u32[]{:S(2)}, u32[]{:S(2)}) collective-permute-start(f32[128,1024]{1,0:T(8,128)S(1)} %get-tuple-element.86), channel_id=1, source_target_pairs={{0,8},{8,0},{16,24},{24,16},{1,9},{9,1},{17,25},{25,17},{2,10},{10... | collective-permute-start | bytes 1572872 | tf_op jit(solution)/shard_map/ppermute | solution.py:28
  48.7 2.3 %collective-permute-start.10 = (bf16[256,768]{1,0:T(8,128)(2,1)S(1)}, bf16[256,768]{1,0:T(8,128)(2,1)S(1)}, u32[]{:S(2)}, u32[]{:S(2)}) collective-permute-start(bf16[256,768]{1,0:T(8,128)(2,1)S(1)} %get-tuple-element.84), channel_id=1, source_target_pairs={{0,8},{8,0},{16,24},{24,16},{1,9},{9,1},{17,25},{25,17},{2,10},{10... | collective-permute-start | bytes 1179656 | tf_op jit(solution)/shard_map/ppermute | solution.py:28
  54.6 16.6 %collective-permute-start.12 = (f16[4,224,256]{2,1,0:T(8,128)(2,1)S(1)}, f16[4,224,256]{2,1,0:T(8,128)(2,1)S(1)}, u32[]{:S(2)}, u32[]{:S(2)}) collective-permute-start(f16[4,224,256]{2,1,0:T(8,128)(2,1)S(1)} %multiply_convert_fusion), channel_id=1, source_target_pairs={{0,1},{1,0},{2,3},{3,2},{4,5},{5,4},{6,7},{7,6},{8,9},{9,8},{10,11... | collective-permute-start | bytes 1376264 | tf_op jit(solution)/shard_map/ppermute | solution.py:33
  56.6 7.0 %collective-permute-start.15 = (f16[2,128,256]{2,1,0:T(8,128)(2,1)S(1)}, f16[2,128,256]{2,1,0:T(8,128)(2,1)S(1)}, u32[]{:S(2)}, u32[]{:S(2)}) collective-permute-start(f16[2,128,256]{2,1,0:T(8,128)(2,1)S(1)} %get-tuple-element.100), channel_id=1, source_target_pairs={{0,2},{1,3},{2,0},{3,1},{4,6},{5,7},{6,4},{7,5},{8,10},{9,11},{10,... | collective-permute-start | bytes 393224 | tf_op jit(solution)/shard_map/ppermute | solution.py:33
  58.3 12.9 %collective-permute-start.14 = (f16[2,128,256]{2,1,0:T(8,128)(2,1)S(1)}, f16[2,128,256]{2,1,0:T(8,128)(2,1)S(1)}, u32[]{:S(2)}, u32[]{:S(2)}) collective-permute-start(f16[2,128,256]{2,1,0:T(8,128)(2,1)S(1)} %get-tuple-element.101), channel_id=1, source_target_pairs={{0,4},{1,5},{2,6},{3,7},{4,0},{5,1},{6,2},{7,3},{8,12},{9,13},{10,... | collective-permute-start | bytes 393224 | tf_op jit(solution)/shard_map/ppermute | solution.py:33
  60.8 10.4 %collective-permute-start.13 = (f16[2,128,256]{2,1,0:T(8,128)(2,1)S(1)}, f16[2,128,256]{2,1,0:T(8,128)(2,1)S(1)}, u32[]{:S(2)}, u32[]{:S(2)}) collective-permute-start(f16[2,128,256]{2,1,0:T(8,128)(2,1)S(1)} %get-tuple-element.102), channel_id=1, source_target_pairs={{0,6},{1,7},{2,4},{3,5},{4,2},{5,3},{6,0},{7,1},{8,14},{9,15},{10,... | collective-permute-start | bytes 393224 | tf_op jit(solution)/shard_map/ppermute | solution.py:33
  72.7 8.9 %collective-permute-start.18 = (f16[224,256]{1,0:T(8,128)(2,1)S(1)}, f16[224,256]{1,0:T(8,128)(2,1)S(1)}, u32[]{:S(2)}, u32[]{:S(2)}) collective-permute-start(f16[224,256]{1,0:T(8,128)(2,1)S(1)} %get-tuple-element.109), channel_id=1, source_target_pairs={{0,2},{1,3},{2,0},{3,1},{4,6},{5,7},{6,4},{7,5},{8,10},{9,11},{10,... | collective-permute-start | bytes 344072 | tf_op jit(solution)/shard_map/ppermute | solution.py:33
  74.7 10.5 %collective-permute-start.17 = (f16[224,256]{1,0:T(8,128)(2,1)S(1)}, f16[224,256]{1,0:T(8,128)(2,1)S(1)}, u32[]{:S(2)}, u32[]{:S(2)}) collective-permute-start(f16[224,256]{1,0:T(8,128)(2,1)S(1)} %get-tuple-element.110), channel_id=1, source_target_pairs={{0,4},{1,5},{2,6},{3,7},{4,0},{5,1},{6,2},{7,3},{8,12},{9,13},{10,... | collective-permute-start | bytes 344072 | tf_op jit(solution)/shard_map/ppermute | solution.py:33
  75.8 9.4 %collective-permute-start.16 = (f16[224,256]{1,0:T(8,128)(2,1)S(1)}, f16[224,256]{1,0:T(8,128)(2,1)S(1)}, u32[]{:S(2)}, u32[]{:S(2)}) collective-permute-start(f16[224,256]{1,0:T(8,128)(2,1)S(1)} %get-tuple-element.111), channel_id=1, source_target_pairs={{0,6},{1,7},{2,4},{3,5},{4,2},{5,3},{6,0},{7,1},{8,14},{9,15},{10,... | collective-permute-start | bytes 344072 | tf_op jit(solution)/shard_map/ppermute | solution.py:33
  77.3 4.3 %collective-permute-start.19 = (f16[128,256]{1,0:T(8,128)(2,1)S(1)}, f16[128,256]{1,0:T(8,128)(2,1)S(1)}, u32[]{:S(2)}, u32[]{:S(2)}) collective-permute-start(f16[128,256]{1,0:T(8,128)(2,1)S(1)} %fusion.7), channel_id=1, source_target_pairs={{0,1},{1,0},{2,3},{3,2},{4,5},{5,4},{6,7},{7,6},{8,9},{9,8},{10,11... | collective-permute-start | bytes 196616 | tf_op jit(solution)/shard_map/ppermute | solution.py:33
  86.0 5.6 %collective-permute-start.20 = (f16[352,256]{1,0:T(8,128)(2,1)S(1)}, f16[352,256]{1,0:T(8,128)(2,1)S(1)}, u32[]{:S(2)}, u32[]{:S(2)}) collective-permute-start(f16[352,256]{1,0:T(8,128)(2,1)S(1)} %get-tuple-element.147), channel_id=1, source_target_pairs={{0,16},{8,24},{16,0},{24,8},{1,17},{9,25},{17,1},{25,9},{2,18},{10... | collective-permute-start | bytes 540680 | tf_op jit(solution)/shard_map/ppermute | solution.py:28
  91.7 1.7 %collective-permute-start.21 = (f16[2,352,256]{2,1,0:T(8,128)(2,1)S(1)}, f16[2,352,256]{2,1,0:T(8,128)(2,1)S(1)}, u32[]{:S(2)}, u32[]{:S(2)}) collective-permute-start(f16[2,352,256]{2,1,0:T(8,128)(2,1)S(1)} %pad_maximum_fusion.1), channel_id=1, source_target_pairs={{0,8},{8,0},{16,24},{24,16},{1,9},{9,1},{17,25},{25,17},{2,10},{10... | collective-permute-start | bytes 1081352 | tf_op jit(solution)/shard_map/ppermute | solution.py:28

commit v3 on v2

v3 whole, which is shorter than its diff:
```python
import functools
import math

import jax
import jax.numpy as jnp
from jax import lax
from jax.experimental import pallas as pl
from jax.experimental.pallas import tpu as pltpu
from jax.sharding import PartitionSpec as P

F32 = jnp.float32
BF16 = jnp.bfloat16
F16 = jnp.float16
NN = (((1,), (0,)), ((), ()))
NT = (((1,), (1,)), ((), ()))
TN = (((0,), (0,)), ((), ()))
CHUNKS = 3
CUT = 176
VMEM_LIMIT = 20 * 1024 * 1024


def dot(left, right, dims=NN):
    return lax.dot_general(left, right, dims, preferred_element_type=F32)


def blk_swap(value, bit):
    count = lax.axis_size("blk")
    return lax.ppermute(value, "blk", [(b, b ^ bit) for b in range(count)])


def dp_swap(value, bit):
    count = lax.axis_size("dp")
    return lax.ppermute(value, "dp", [(d, d ^ bit) for d in range(count)])


def quarter_of(place, j):
    return pl.multiple_of((place ^ j) * 256, 256)


def encode(feats, w_first, w_second, pre_out=None, hidden_out=None):
    pre = dot(feats, w_first[...])
    hidden = (pre * jax.nn.sigmoid(pre)).astype(BF16)
    if pre_out is not None:
        pre_out[...] = pre
        hidden_out[...] = hidden
    return dot(hidden, w_second[...]).astype(BF16)


def put_gates(place, pre, out):
    for n in range(2):
        quarter = pre[:, pl.ds(quarter_of(place, n), 256)]
        sig = jax.nn.sigmoid(quarter)
        out[n] = (sig * (1.0 + quarter * (1.0 - sig))).T


def residual(inter, pred, sq_rows, sq_cols, emb):
    tanimoto = inter / (sq_rows + sq_cols - inter)
    return (pred * (1.0 / math.sqrt(emb)) - tanimoto).astype(BF16)


def first_stage(i, o, s):
    tok, emb = i["own"].shape[0], i["w_second"].shape[1]
    feats = o["feats"]
    feats[:tok] = i["own"][...]
    feats[tok:] = i["sib"][...]
    step = tok // 3
    for r in range(0, tok, step):
        rows = slice(r, r + step)
        embed = encode(feats[rows, :], i["w_first"], i["w_second"], s["pre"], s["hidden"])
        o["embed"][rows, :] = embed
        o["hidden"][rows, :] = s["hidden"][...]
        for n in range(2):
            quarter = s["pre"][:, pl.ds(quarter_of(lax.axis_index("blk"), n), 256)]
            sig = jax.nn.sigmoid(quarter)
            o["gate"][n, :, rows] = (sig * (1.0 + quarter * (1.0 - sig))).T
    for r in range(tok, 2 * tok, step):
        rows = slice(r, r + step)
        o["embed"][rows, :] = encode(feats[rows, :], i["w_first"], i["w_second"])
    embed = o["embed"][...]
    wide = feats[...].astype(F32)
    sq = jnp.broadcast_to(jnp.sum(wide * wide, axis=1, keepdims=True), o["sq"].shape)
    o["sq"][...] = sq
    sq_cols = sq.T[:1]
    inter = dot(feats[:tok], feats[...], NT)
    pred = dot(embed[:tok], embed, NT)
    resid = residual(inter, pred, sq[:tok, :1], sq_cols, emb)
    o["summed", 0][...] = dot(resid, embed)
    o["token"][...] = jnp.zeros((8, 128), F32)


def diagonals(square):
    at = lax.broadcasted_iota(jnp.int32, square.shape, 0)
    to = lax.broadcasted_iota(jnp.int32, square.shape, 1)
    only = jnp.where(at == to, square, 0.0)
    return jnp.sum(only, axis=1, keepdims=True), jnp.sum(only, axis=0, keepdims=True)


def rem_stage(k, i, o, s):
    emb = i["w_second"].shape[1]
    top = i["new"][...]
    embed_new = encode(top, i["w_first"], i["w_second"], s["pre"], o["hidden"])
    put_gates(lax.axis_index("blk"), s["pre"], o["gate"])
    o["embed"][...] = embed_new
    _, sq_cols = diagonals(dot(top, top, NT))
    tok = i["feats", 0].shape[0] // 2
    total = None
    for name in [0] + [("rs", j) for j in range(1, k)]:
        rows = pl.ds(tok, tok) if name == 0 else pl.ds(0, top.shape[0])
        old = i["embed", name][rows, :]
        inter = dot(i["feats", name][rows, :], top, NT)
        resid = residual(inter, dot(old, embed_new, NT), i["sq", name][rows, :1], sq_cols, emb)
        part = dot(resid, old, TN)
        total = part if total is None else total + part
    o["total"][...] = total


def rs_stage(k, i, o, s):
    emb = i["w_second"].shape[1]
    half = i["new", 0].shape[0]
    part = 2 * half
    for h in range(2):
        o["feats"][h * half : (h + 1) * half] = i["new", h][...]
    embed_rs = encode(o["feats"][...], i["w_first"], i["w_second"])
    s["both"][:part] = i["feats", ("rem", k)][...]
    s["both"][part:] = o["feats"][...]
    s["embeds"][:part] = i["embed", ("rem", k)][...]
    s["embeds"][part:] = embed_rs
    top, embed_new = s["both"][...], s["embeds"][...]
    inter = dot(top, top, NT)
    sq_rows, sq_cols = diagonals(inter)
    if "embed" in o:
        o["embed"][...] = embed_rs
        o["sq_rem"][...] = jnp.broadcast_to(sq_rows[:part], o["sq_rem"].shape)
        o["sq_rs"][...] = jnp.broadcast_to(sq_rows[part:], o["sq_rs"].shape)
        o["token"][...] = jnp.zeros((8, 128), F32)
    pred = dot(embed_new[:part], embed_new, NT)
    resid = residual(inter[:part], pred, sq_rows[:part], sq_cols, emb)
    total = i["total"][...] + dot(resid, embed_new)
    out = []
    for j in range(k):
        name = ("rem", j) if j else 0
        rows = pl.ds(0, i["summed", j].shape[0])
        old = i["embed", name][rows, :]
        inter = dot(i["feats", name][rows, :], top, NT)
        pred = dot(old, embed_new, NT)
        resid = residual(inter, pred, i["sq", name][rows, :1], sq_cols, emb)
        total += dot(resid[:, :part], old, TN)
        out.append(i["summed", j][...] + dot(resid, embed_new))
    out.append(total)
    for j in range(k + 1):
        if ("summed", j) in o:
            o["summed", j][...] = out[j]
    return out


def last_stage(factor, i, o, s):
    place = lax.axis_index("blk")
    wide = i["w_second"].shape[1] // 4
    start = 0
    for value in rs_stage(CHUNKS, i, o, s):
        rows = pl.ds(start, value.shape[0])
        piece = (value * factor).astype(BF16)
        o["dembed"][rows, :] = piece
        for q in range(4):
            o["quarters"][q, rows, :] = piece[:, q * wide : (q + 1) * wide]
        start += value.shape[0]
    dpre_share(place, 1, i, o["dembed"], o["give"])
    second_share(place ^ 1, o["quarters"], hiddens_of(i), o["second_give"])


def hiddens_of(i):
    return [i["hidden", j] for j in range(CHUNKS + 1)]


def dpre_share(place, n, i, dembed, out):
    turned = dot(i["w_second"][pl.ds(quarter_of(place, n), 256), :], dembed[...], NT)
    start = 0
    for j in range(CHUNKS + 1):
        gate = i["gate", j][n]
        rows = slice(start, start + gate.shape[1])
        out[:, rows] = (turned[:, rows] * gate).astype(BF16)
        start = rows.stop


def own_share(i, o, s):
    place = lax.axis_index("blk")
    dpre_share(place, 0, i, i["dembed"], o["keep"])
    second_share(place, i["quarters"], hiddens_of(i), o["second"])
    me = dp_high()
    for d in range(8):
        o["first"][d] = first_block(o["keep"], core_rows(i, 0), me ^ d)


def dp_high():
    return lax.axis_index("dp") // (lax.axis_size("dp") // 8)


def core_rows(i, core):
    both = i["feats", 0]
    tok = both.shape[0] // 2
    name = ("rem", "rs")[core]
    return [(both, core * tok, tok)] + [
        (i["feats", (name, j)], 0, i["feats", (name, j)].shape[0]) for j in range(1, CHUNKS + 1)
    ]


def first_block(dpre, rows, block, top=0, bottom=256):
    lanes = pl.ds(pl.multiple_of(block * 256, 256), 256)
    total, at = None, 0
    for ref, start, count in rows:
        piece = dot(dpre[top:bottom, at : at + count], ref[pl.ds(start, count), lanes])
        total = piece if total is None else total + piece
        at += count
    return total


def second_share(quarter, dembed, hiddens, out):
    total, start = None, 0
    for hidden in hiddens:
        count = hidden.shape[0]
        part = dot(dembed[quarter, start : start + count, :], hidden[...], TN)
        total = part if total is None else total + part
        start += count
    out[...] = total


def exponent(bound):
    return jnp.clip(jnp.ceil(jnp.log2(jnp.maximum(bound, 1e-30))) + 1.0, -100.0, 120.0)


def put_tail(ref, d, start, exp_first, exp_second):
    ref[d, start : start + 8] = exp_first
    ref[d, start + 8 : start + 16] = exp_second


def put_second(ref, d, second, block):
    value = second[:, pl.ds(pl.multiple_of(block * 128, 128), 128)]
    ref[d, CUT : CUT + 64, :128] = value[:64]
    ref[d, CUT : CUT + 64, 128:] = value[64:]


def first_gradients(i, o, s):
    o["second"][...] = i["second_keep"][...] + i["second_got"][...]
    sums = jnp.sum(jnp.abs(i["keep"][...].astype(F32)), axis=1, keepdims=True)
    sums += jnp.sum(jnp.abs(i["got"][...].astype(F32)), axis=1, keepdims=True)
    exp_first = exponent(3.0 * jnp.max(sums, axis=0, keepdims=True))
    most = jnp.max(jnp.abs(o["second"][...]), axis=1, keepdims=True)
    exp_second = exponent(jnp.max(most, axis=0, keepdims=True))
    o["exps"][0] = jnp.broadcast_to(exp_first, (8, 256))
    o["exps"][1] = jnp.broadcast_to(exp_second, (8, 256))
    bottom = 256 - CUT
    o["kind_one"][:CUT] = jnp.zeros((CUT, 256), F32)
    o["kind_one"][CUT : CUT + 64] = jnp.ones((64, 256), F32)
    o["kind_one"][CUT + 64 :] = jnp.full((16, 256), 2.0, F32)
    o["kind_two"][:bottom] = jnp.zeros((bottom, 256), F32)
    o["kind_two"][bottom:] = jnp.full((16, 256), 2.0, F32)
    o["kind_all"][:256] = jnp.zeros((256, 256), F32)
    o["kind_all"][256:320] = jnp.ones((64, 256), F32)
    o["kind_all"][320:] = jnp.full((16, 256), 2.0, F32)
    me = dp_high()
    for z in range(4):
        d = 2 * z + 1
        value = first_block(i["got"], core_rows(i, 1), me ^ d, 0, CUT)
        o["one"][z, :CUT] = value + i["first"][d, :CUT]
        put_second(o["one"], z, o["second"], me ^ d)
        put_tail(o["one"], z, CUT + 64, o["exps"][0], o["exps"][1])


def other_gradients(i, o, s):
    me = dp_high()
    rows = core_rows(i, 1)
    bottom = 256 - CUT
    for z in range(4):
        for x in range(2):
            d = 2 * z + x
            top = CUT if x else 0
            value = first_block(i["got"], rows, me ^ d, top, 256) + i["first"][d, top:]
            o["two"][d, :bottom] = value[CUT - top :]
            put_tail(o["two"], d, bottom, i["exps"][0], i["exps"][0])
            if x == 0:
                o["one"][z, :CUT] = value[:CUT]
                put_second(o["one"], z, i["second"], me ^ d)
                put_tail(o["one"], z, CUT + 64, i["exps"][0], i["exps"][1])


def run(body, ins, outs, scratch, limit=VMEM_LIMIT):
    names_in, names_out, names_s = list(ins), list(outs), list(scratch)

    def kernel(*refs):
        n, m = len(names_in), len(names_out)
        i = dict(zip(names_in, refs[:n]))
        o = dict(zip(names_out, refs[n : n + m]))
        body(i, o, dict(zip(names_s, refs[n + m :])))

    vmem = pltpu.VMEM
    spaces = {"arg": pl.ANY}
    shapes = [jax.ShapeDtypeStruct(*v) for v in outs.values()]
    got = pl.pallas_call(
        kernel,
        out_shape=shapes,
        in_specs=[pl.BlockSpec(memory_space=spaces.get(n, vmem)) for n in names_in],
        out_specs=[pl.BlockSpec(memory_space=vmem)] * len(shapes),
        scratch_shapes=[vmem(*v) if isinstance(v, tuple) else v for v in scratch.values()],
        compiler_params=pltpu.CompilerParams(vmem_limit_bytes=limit),
        cost_estimate=pl.CostEstimate(flops=1, bytes_accessed=1, transcendentals=0),
    )(*ins.values())
    return dict(zip(names_out, got))


def split(i, o, s):
    half = i["rem"].shape[0] // 2
    for h in range(2):
        o["rows", h][...] = i["rem"][h * half : (h + 1) * half]


def fetch(pairs, i, o, s):
    copies = []
    for n, (source, start, count, target) in enumerate(pairs):
        rows = i[source].at[pl.ds(start, count), :]
        copies.append(pltpu.make_async_copy(rows, o[target], s["sems"].at[n]))
        copies[-1].start()
    for copy in copies:
        copy.wait()


def turn_quarter(i, o, s):
    one, two, out = i["one"], i["two"], o["all"]
    bottom = 256 - CUT
    out[:256] = jnp.concatenate([one[:CUT], two[:bottom]], 0).T
    block = one[CUT : CUT + 64]
    second = jnp.concatenate([block[:, :128], block[:, 128:]], 0).T
    out[256:320, :128] = second[:64]
    out[256:320, 128:] = second[64:]
    out[320:328, :128] = one[CUT + 64 : CUT + 72, :128]
    lane = lax.broadcasted_iota(jnp.int32, (8, 128), 1)
    tail = two[bottom : bottom + 8, 128:]
    out[320:328, 128:] = jnp.where(lane < CUT - 128, one[CUT + 64 : CUT + 72, 128:], tail)
    out[328:] = one[CUT + 72 :]


def place_quarters(i, o, s):
    me = lax.axis_index("blk")
    for j in range(4):
        q = me ^ j
        o["first"][:, pl.ds(pl.multiple_of(q * 256, 256), 256)] = i["all"][j, :256]
        columns = pl.ds(pl.multiple_of(q * 128, 128), 128)
        o["second"][:64, columns] = i["all"][j, 256:320, :128]
        o["second"][64:, columns] = i["all"][j, 256:320, 128:]


def encode16(total, kind, tail):
    first, second = [jnp.exp2(15.0 - e) for e in exps_of(total, tail)]
    scale = jnp.where(kind == 0.0, first, jnp.where(kind == 1.0, second, 1.0))
    return (total * scale).astype(F16)


def decode16(got, kind, tail):
    got = got.astype(F32)
    first, second = [jnp.exp2(e - 15.0) for e in exps_of(got, tail)]
    return got * jnp.where(kind == 0.0, first, jnp.where(kind == 1.0, second, 1.0))


def exps_of(value, tail):
    rows = value.ndim - 2
    return [lax.slice_in_dim(value, tail + at, tail + at + 1, axis=rows) for at in (0, 8)]


def halves(value, axis, mine):
    low = lax.index_in_dim(value, 0, axis, keepdims=False)
    high = lax.index_in_dim(value, 1, axis, keepdims=False)
    return jnp.where(mine == 0, low, high), jnp.where(mine == 0, high, low)


def pick(total, axis, index):
    if isinstance(index, int):
        return lax.index_in_dim(total, index, axis, keepdims=False)
    return lax.dynamic_index_in_dim(total, index, axis, keepdims=False)


class Sum:
    def __init__(self, total, kind, order, relative, halved=None):
        self.total, self.kind, self.halved = total, kind, halved
        self.tail = total.shape[-2] - 16
        self.axes = list(range(total.ndim - 2))
        self.order, self.relative = order, relative

    def pack(self, step, shifts):
        axis = self.order[step]
        at = self.axes.index(axis)
        size = self.total.shape[at]
        me = 0
        if axis >= self.relative:
            me = (lax.axis_index("dp") >> shifts[axis]) & (size - 1)
        self.axes.pop(at)
        if self.halved is not None:
            self.keep, gives = self.halved[0], [self.halved[1]]
            self.halved = None
        else:
            self.keep = pick(self.total, at, me)
            gives = [pick(self.total, at, me ^ o) for o in range(1, size)]
        return [encode16(give, self.kind, self.tail) for give in gives]

    def swap(self, step, shifts, packs):
        shift = shifts[self.order[step]]
        return [dp_swap(p, (n + 1) << shift) for n, p in enumerate(packs)]

    def receive(self, gots):
        others = [decode16(g, self.kind, self.tail) for g in gots]
        total, top = self.keep, self.keep
        for other in others:
            total = total + other
            top = jnp.maximum(top, other)
        self.total = jnp.where(self.kind == 2.0, top + float(len(others)), total)


def split_lanes(packed, bounds, count):
    if count == 1:
        return packed
    blocks, rows, lanes = packed.shape
    plain = packed.reshape(blocks, rows, count, lanes // count)
    paired = packed.reshape(blocks, rows, 2, count, lanes // 2 // count)
    plain = jnp.moveaxis(plain, 2, 1)
    paired = jnp.moveaxis(paired, 3, 1).reshape(plain.shape)
    row = lax.broadcasted_iota(jnp.int32, plain.shape, 2)
    both = jnp.where((row >= bounds[0]) & (row < bounds[1]), paired, plain)
    return both.reshape(blocks * count, rows, lanes // count)


def per_device(fingerprints, w_first, w_second):
    tok, width = fingerprints.shape
    hid, emb = w_second.shape
    blk_count = lax.axis_size("blk")
    dp_count = lax.axis_size("dp")
    group_rows = tok * blk_count
    all_rows = group_rows * dp_count
    factor = 2.0 / math.sqrt(group_rows * all_rows)
    bits = dp_count.bit_length() - 1
    k = CHUNKS
    part = tok // k

    rem = []
    rows, own = lax.optimization_barrier((fingerprints[:part], fingerprints))
    rem.append(blk_swap(rows, 2))
    for start, count in ((1, k - 1),):
        names = [("rows", j) for j in range(start, start + count)]
        out = run(
            functools.partial(fetch, [("arg", j * part, part, ("rows", j)) for _, j in names]),
            {"arg": fingerprints},
            {name: ((part, width), BF16) for name in names},
            {"sems": pltpu.SemaphoreType.DMA((count,))},
            limit=2 << 20,
        )
        rem += [blk_swap(out[name], 2) for name in names]
    sib = blk_swap(own, 1)
    rs = []

    base = {"w_first": w_first, "w_second": w_second}
    out = run(
        first_stage,
        {**base, "own": fingerprints, "sib": sib},
        {
            "feats": ((2 * tok, width), BF16),
            "hidden": ((tok, hid), BF16),
            "gate": ((2, 256, tok), F32),
            "embed": ((2 * tok, emb), BF16),
            "sq": ((2 * tok, 128), F32),
            ("summed", 0): ((tok, emb), F32),
            "token": ((8, 128), F32),
        },
        {"pre": ((tok // 3, hid), F32), "hidden": ((tok // 3, hid), BF16)},
    )
    token = out["token"]
    hidden, gate, feats = [out["hidden"]], [out["gate"]], [out["feats"]]
    embed, sq, summed = [out["embed"]], [out["sq"]], [out["summed", 0]]
    feats, embed, sq, summed = {0: feats[0]}, {0: embed[0]}, {0: sq[0]}, summed
    half = part // 2
    for step in range(1, k + 1):
        out = run(
            split,
            {"rem": rem[step - 1], "token": token},
            {("rows", h): ((half, width), BF16) for h in range(2)},
            {},
            limit=2 << 20,
        )
        rs = [blk_swap(out["rows", h], 1) for h in range(2)]
        ins = {**base, "new": rem[step - 1]}
        for name in feats:
            if name == 0 or name[0] == "rs":
                ins["feats", name] = feats[name]
                ins["embed", name] = embed[name]
                ins["sq", name] = sq[name]
        embed_shape, sq_shape = ((part, emb), BF16), ((part, 128), F32)
        out = run(
            functools.partial(rem_stage, step),
            ins,
            {
                "hidden": ((part, hid), BF16),
                "gate": ((2, 256, part), F32),
                "embed": embed_shape,
                "total": ((part, emb), F32),
            },
            {"pre": ((part, hid), F32)},
        )
        hidden.append(out["hidden"])
        gate.append(out["gate"])
        name = ("rem", step)
        feats[name], embed[name] = rem[step - 1], out["embed"]

        ins = {**base, ("new", 0): rs[0], ("new", 1): rs[1], "total": out["total"]}
        for j in range(step + 1):
            name = ("rem", j) if j else 0
            ins["feats", name] = feats[name]
            ins["embed", name] = embed[name]
            if j < step:
                ins["sq", name] = sq[name]
                ins["summed", j] = summed[j]
        outs = {"feats": ((part, width), BF16)}
        scratch = {"both": ((2 * part, width), BF16), "embeds": ((2 * part, emb), BF16)}
        if step < k:
            outs = {**outs, "embed": embed_shape, "sq_rem": sq_shape, "sq_rs": sq_shape}
            outs["token"] = ((8, 128), F32)
            for j in range(step + 1):
                outs["summed", j] = ((tok if j == 0 else part, emb), F32)
            out = run(functools.partial(rs_stage, step), ins, outs, scratch)
            token = out["token"]
            summed = [out["summed", j] for j in range(step + 1)]
            name = ("rs", step)
            feats[name], embed[name], sq[name] = out["feats"], out["embed"], out["sq_rs"]
            sq["rem", step] = out["sq_rem"]
    rows = {}
    for j in range(k + 1):
        rows["hidden", j] = hidden[j]
        rows["gate", j] = gate[j]
    out = run(
        functools.partial(last_stage, factor),
        {**ins, **rows},
        {
            "feats": ((part, width), BF16),
            "dembed": ((2 * tok, emb), BF16),
            "quarters": ((4, 2 * tok, emb // 4), BF16),
            "give": ((256, 2 * tok), BF16),
            "second_give": ((emb // 4, hid), F32),
        },
        scratch,
    )
    feats["rs", k] = out["feats"]
    got = blk_swap(out["give"], 1)
    second_got = blk_swap(out["second_give"], 1)
    mine = {("feats", n): v for n, v in feats.items() if n == 0 or n[0] == "rem"}
    theirs = {("feats", n): v for n, v in feats.items() if n == 0 or n[0] == "rs"}
    own = run(
        own_share,
        {
            "w_second": w_second,
            "dembed": out["dembed"],
            "quarters": out["quarters"],
            **rows,
            **mine,
        },
        {
            "keep": ((256, 2 * tok), BF16),
            "second": ((emb // 4, hid), F32),
            "first": ((8, 256, 256), F32),
        },
        {},
    )
    rows_one, rows_two = CUT + 64 + 16, 256 - CUT + 16
    lanes = 256 * 8 // dp_count
    extra = dp_count // 8
    out = run(
        first_gradients,
        {
            "keep": own["keep"],
            "got": got,
            "second_keep": own["second"],
            "second_got": second_got,
            "first": own["first"],
            **theirs,
        },
        {
            "second": ((emb // 4, hid), F32),
            "exps": ((2, 8, 256), F32),
            "one": ((4, rows_one, 256), F32),
            "kind_one": ((rows_one, 256), F32),
            "kind_two": ((rows_two, 256), F32),
            "kind_all": ((336, 256), F32),
        },
        {},
    )
    kinds, one_give = (out["kind_one"], out["kind_two"], out["kind_all"]), out["one"]
    more = extra.bit_length() - 1
    shape = (2,) * more
    kind_one, kind_two = kinds[0][:, :lanes], kinds[1][:, :lanes]
    shifts = [more + 1, more] + [more - 1 - n for n in range(more)]
    rest = list(range(2, more + 2))
    cut = functools.partial(split_lanes, bounds=(CUT, CUT + 64), count=extra)
    one_give = cut(one_give).reshape((4,) + shape + (rows_one, lanes))
    early = encode16(one_give, kind_one, rows_one - 16)
    got, early = lax.optimization_barrier((got, early))
    out = run(
        other_gradients,
        {"got": got, "first": own["first"], "second": out["second"], "exps": out["exps"], **theirs},
        {"one": ((4, rows_one, 256), F32), "two": ((8, rows_two, 256), F32)},
        {},
    )
    one_keep = cut(out["one"]).reshape(one_give.shape)
    two = split_lanes(out["two"], (0, 0), extra).reshape((4, 2) + shape + (rows_two, lanes))
    one = Sum(jnp.stack([one_keep, one_give], 1), kind_one, [1, 0] + rest, 2, (one_keep, one_give))
    two = Sum(two, kind_two, [0] + rest + [1], 2)
    one.pack(0, shifts)
    gots_one = one.swap(0, shifts, [early])
    gots_two = two.swap(0, shifts, two.pack(0, shifts))
    for step in range(1, more + 2):
        one.receive(gots_one)
        packs = one.pack(step, shifts)
        gots_two, packs = lax.optimization_barrier((gots_two, packs))
        gots_one = one.swap(step, shifts, packs)
        gots_two, gots_one[0] = lax.optimization_barrier((gots_two, gots_one[0]))
        two.receive(gots_two)
        gots_two = two.swap(step, shifts, two.pack(step, shifts))
    one.receive(gots_one)
    two.receive(gots_two)
    if extra == 1:
        out = run(
            turn_quarter,
            {"one": one.total, "two": two.total},
            {"all": ((336, 256), F32)},
            {},
        )
        every = gather(encode16(out["all"], kinds[2], 320))
        out = run(
            place_quarters,
            {"all": decode16(every, kinds[2], 320)},
            {"first": ((lanes, hid), F32), "second": ((lanes // 2, emb), F32)},
            {},
        )
        return out["first"], out["second"]
    packed = [encode16(one.total, kind_one, one.tail), encode16(two.total, kind_two, two.tail)]
    every = gather(jnp.concatenate(packed, 0))
    one = decode16(every[:, :rows_one], kind_one, one.tail)
    two = decode16(every[:, rows_one:], kind_two, two.tail)
    order = jnp.arange(4) ^ lax.axis_index("blk")
    first = jnp.concatenate([one[:, :CUT], two[:, : 256 - CUT]], 1)[order].reshape(hid, lanes)
    second = one[order, CUT : CUT + 64]
    second = jnp.concatenate([second[..., : lanes // 2], second[..., lanes // 2 :]], 1)
    return first.T, second.reshape(emb, lanes // 2).T


def gather(packed):
    across = blk_swap(packed, 2)
    pair = jnp.stack([packed, across])
    beside = blk_swap(pair, 1)
    return jnp.stack([packed, beside[0], across, beside[1]])


def solution(mesh):
    in_specs = (P(("blk", "dp"), None), P(), P())
    out_specs = (P("dp", None), P("dp", None))
    return jax.shard_map(
        per_device, mesh=mesh, in_specs=in_specs, out_specs=out_specs, check_vma=False
    )
```

time: 96.1 us -> 91 us (0.947)
  waiting for transfers between devices: 35.4 us -> 29.1 us
  Pallas kernels: 29.2 us -> 30.7 us
    ppermute x14, waiting for transfers between devices: 17.8 us -> 14.7 us  [blk_swap(): return lax.ppermute(value, 'blk', [(b, b ^ bit) for b in range(count)])]
    ppermute x8, waiting for transfers between devices: 17.5 us -> 14.4 us  [dp_swap(): return lax.ppermute(value, 'dp', [(d, d ^ bit) for d in range(count)])]
    pallas_call x10 -> x16, Pallas kernels: 29.2 us -> 30.7 us  [run(): pl.pallas_call(kernel, out_shape=shapes, in_specs=[pl.BlockSpec(memory_sp...]
    unnamed x26 -> x27, local copies, waits for them, and re-layouts: 4.85 us -> 4.86 us
  transfers between devices with their start and end apart: 22 -> 22, of which waited for: 13 -> 10; matrix products, arithmetic and copies ran while one was open for 1% -> 2% of each run, Pallas kernels for 19% -> 26%
where the time goes in v3:
time: 91 us; the launch traced here: 90.7 us
  Pallas kernels  30.7 us (34%)
  waiting for transfers between devices  29.1 us (32%)
  starting transfers between devices  20.8 us (23%)
  local copies, waits for them, and re-layouts  6.09 us (7%)
  other arithmetic  2.77 us (3%)
  between operations  1.23 us (1%)
    pallas_call x16, Pallas kernels, run(): pl.pallas_call(kernel, out_shape=shapes, in_specs=[pl.BlockSpec(memory_sp...  30.7 us
    ppermute x14, waiting for transfers between devices, blk_swap(): return lax.ppermute(value, 'blk', [(b, b ^ bit) for b in range(count)])  14.7 us
    ppermute x8, waiting for transfers between devices, dp_swap(): return lax.ppermute(value, 'dp', [(d, d ^ bit) for d in range(count)])  14.4 us
    ppermute x8, starting transfers between devices, dp_swap(): return lax.ppermute(value, 'dp', [(d, d ^ bit) for d in range(count)])  11.7 us
    ppermute x14, starting transfers between devices, blk_swap(): return lax.ppermute(value, 'blk', [(b, b ^ bit) for b in range(count)])  9.09 us
    unnamed x27, local copies, waits for them, and re-layouts  4.86 us
  transfers between devices with their start and end apart: 22, of which 10 were waited for; matrix products, arithmetic and copies ran while one was open for 2% of the time, Pallas kernels for 26%

profile of v3, /device:TPU:0, one launch (start us, length us, event | category | flops | bytes accessed | tf_op | source)
XLA Modules:
  0.0 90.7 jit_solution(1908554049131413554)
XLA Ops:
  0.6 1.2 %slice.173 = bf16[128,2048]{1,0:T(8,128)(2,1)S(1)} slice(bf16[384,2048]{1,0:T(8,128)(2,1)} %refs_2_.1), slice={[0:128], [0:2048]} | slice | bytes 1048576 | tf_op jit(solution)/shard_map/slice | solution.py:442
  1.8 0.5 collective-permute-start.3
  2.3 2.6 %collective-permute-start.2 = (bf16[128,2048]{1,0:T(8,128)(2,1)S(1)}, bf16[128,2048]{1,0:T(8,128)(2,1)S(1)}, u32[]{:S(2)}, u32[]{:S(2)}) collective-permute-start(bf16[128,2048]{1,0:T(8,128)(2,1)S(1)} %slice.173), channel_id=1, source_target_pairs={{0,16},{8,24},{16,0},{24,8},{1,17},{9,25},{17,1},{25,9},{2,18},{10... | collective-permute-start | bytes 1572872 | tf_op jit(solution)/shard_map/ppermute | solution.py:28
  4.9 1.4 %copy-done.3 = bf16[384,2048]{1,0:T(8,128)(2,1)S(1)} copy-done((bf16[384,2048]{1,0:T(8,128)(2,1)S(1)}, bf16[384,2048]{1,0:T(8,128)(2,1)}, u32[]{:S(2)}) %copy-start.3) | copy-done | bytes 1572888
  6.3 0.1 shard_map.50
  6.4 0.1 collective-permute-start.1
  6.5 1.2 %copy-done.4 = bf16[384,2048]{1,0:T(8,128)(2,1)S(1)} copy-done((bf16[384,2048]{1,0:T(8,128)(2,1)S(1)}, bf16[384,2048]{1,0:T(8,128)(2,1)}, u32[]{:S(2)}) %copy-start.4) | copy-done | bytes 1572888
  7.7 2.2 %copy-done = bf16[2048,1024]{1,0:T(8,128)(2,1)S(1)} copy-done((bf16[2048,1024]{1,0:T(8,128)(2,1)S(1)}, bf16[2048,1024]{1,0:T(8,128)(2,1)}, u32[]{:S(2)}) %copy-start) | copy-done | bytes 4194328
  9.9 7.1 %shard_map.51 = (bf16[768,2048]{1,0:T(8,128)(2,1)S(1)}, bf16[384,1024]{1,0:T(8,128)(2,1)S(1)}, f32[2,256,384]{2,1,0:T(8,128)S(1)}, bf16[768,512]{1,0:T(8,128)(2,...) custom-call(bf16[2048,1024]{1,0:T(8,128)(2,1)S(1)} %copy-done, ...), custom_call_target="tpu_custom_call" | custom-call | flops 1 | bytes 1 | tf_op jit(solution)/shard_map/pallas_call | solution.py:298
  17.1 0.6 collective-permute-done.2.refs_0_.refs_2_.refs_9_.refs_12_
  17.7 0.1 collective-permute-start.4
  17.8 0.5 collective-permute-start.5
  18.3 1.9 %collective-permute-start = (bf16[128,2048]{1,0:T(8,128)(2,1)S(1)}, bf16[128,2048]{1,0:T(8,128)(2,1)S(1)}, u32[]{:S(2)}, u32[]{:S(2)}) collective-permute-start(bf16[128,2048]{1,0:T(8,128)(2,1)S(1)} %get-tuple-element.74), channel_id=1, source_target_pairs={{0,16},{8,24},{16,0},{24,8},{1,17},{9,25},{17,1},{25,9},{2,18},{10... | collective-permute-start | bytes 1572872 | tf_op jit(solution)/shard_map/ppermute | solution.py:28
  20.3 1.9 %shard_map.53 = (bf16[128,1024]{1,0:T(8,128)(2,1)S(1)}, f32[2,256,128]{2,1,0:T(8,128)S(1)}, bf16[128,512]{1,0:T(8,128)(2,1)S(1)}, f32[128,512]{1,0:T(8,128)S(1)}) custom-call(bf16[2048,1024]{1,0:T(8,128)(2,1)S(1)} %copy-done.1, bf16[1024,512]{1,0:T(8,128)(2,1)S(1)} %copy-done.2, ...), custom_call_target="tpu_custom_call" | custom-call | flops 1 | bytes 1 | tf_op jit(solution)/shard_map/pallas_call | solution.py:298
  22.2 0.0 collective-permute-done.4.refs_2_
  22.2 0.0 collective-permute-done.5.refs_3_
  22.2 2.7 %shard_map.54 = (bf16[128,2048]{1,0:T(8,128)(2,1)S(1)}, bf16[128,512]{1,0:T(8,128)(2,1)S(1)}, f32[128,128]{1,0:T(8,128)S(1)}, f32[128,128]{1,0:T(8,128)S(1)}, f3...) custom-call(bf16[2048,1024]{1,0:T(8,128)(2,1)S(1)} %copy-done.1, ...), custom_call_target="tpu_custom_call" | custom-call | flops 1 | bytes 1 | tf_op jit(solution)/shard_map/pallas_call | solution.py:298
  24.9 4.0 %collective-permute-done.1.refs_0_.refs_2_.refs_13_ = bf16[128,2048]{1,0:T(8,128)(2,1)S(1)} collective-permute-done((bf16[128,2048]{1,0:T(8,128)(2,1)S(1)}, bf16[128,2048]{1,0:T(8,128)(2,1)S(1)}, u32[]{:S(2)}, u32[]{:S(2)}) %collective-permute-start.1) | collective-permute-done | bytes 524320 | tf_op jit(solution)/shard_map/ppermute | solution.py:28
  29.0 0.1 collective-permute-start.6
  29.1 0.5 collective-permute-start.7
  29.6 2.2 %shard_map.56 = (bf16[128,1024]{1,0:T(8,128)(2,1)S(1)}, f32[2,256,128]{2,1,0:T(8,128)S(1)}, bf16[128,512]{1,0:T(8,128)(2,1)S(1)}, f32[128,512]{1,0:T(8,128)S(1)}) custom-call(bf16[2048,1024]{1,0:T(8,128)(2,1)S(1)} %copy-done.1, bf16[1024,512]{1,0:T(8,128)(2,1)S(1)} %copy-done.2, bf16[128,2048]{1,0:T(8,128)(2,1)S(1)} %collective-permute-done.1.refs_0_.refs_2_.refs_13_, ...), custom_call_target="tpu_custom_call" | custom-call | flops 1 | bytes 1 | tf_op jit(solution)/shard_map/pallas_call | solution.py:298
  31.8 3.6 %shard_map.57 = (bf16[128,2048]{1,0:T(8,128)(2,1)S(1)}, bf16[128,512]{1,0:T(8,128)(2,1)S(1)}, f32[128,128]{1,0:T(8,128)S(1)}, f32[128,128]{1,0:T(8,128)S(1)}, f3...) custom-call(bf16[2048,1024]{1,0:T(8,128)(2,1)S(1)} %copy-done.1, ...), custom_call_target="tpu_custom_call" | custom-call | flops 1 | bytes 1 | tf_op jit(solution)/shard_map/pallas_call | solution.py:298
  35.4 4.5 %collective-permute-done.refs_0_.refs_2_.refs_17_.refs_14_ = bf16[128,2048]{1,0:T(8,128)(2,1)S(1)} collective-permute-done((bf16[128,2048]{1,0:T(8,128)(2,1)S(1)}, bf16[128,2048]{1,0:T(8,128)(2,1)S(1)}, u32[]{:S(2)}, u32[]{:S(2)}) %collective-permute-start) | collective-permute-done | bytes 524320 | tf_op jit(solution)/shard_map/ppermute | solution.py:28
  39.9 0.1 collective-permute-start.8
  40.0 0.5 collective-permute-start.9
  40.5 2.5 %shard_map.59 = (bf16[128,1024]{1,0:T(8,128)(2,1)S(1)}, f32[2,256,128]{2,1,0:T(8,128)S(1)}, bf16[128,512]{1,0:T(8,128)(2,1)S(1)}, f32[128,512]{1,0:T(8,128)S(1)}) custom-call(bf16[2048,1024]{1,0:T(8,128)(2,1)S(1)} %copy-done.1, bf16[1024,512]{1,0:T(8,128)(2,1)S(1)} %copy-done.2, bf16[128,2048]{1,0:T(8,128)(2,1)S(1)} %collective-permute-done.refs_0_.refs_2_.refs_17_.refs_14_, ...), custom_call_target="tpu_custom_call" | custom-call | flops 1 | bytes 1 | tf_op jit(solution)/shard_map/pallas_call | solution.py:298
  43.1 5.0 %shard_map.60 = (bf16[128,2048]{1,0:T(8,128)(2,1)S(1)}, bf16[768,512]{1,0:T(8,128)(2,1)S(1)}, bf16[4,768,128]{2,1,0:T(8,128)(2,1)S(1)}, bf16[256,768]{1,0:T(8,128)(2,1)S(1)}, f32[128,1024]{1,0:T(8,128)S(1)}) custom-call(bf16[2048,1024]{1,0:T(8,128)(2,1)S(1)} %copy-done.1, bf16[1024,512]{1,0:T(8,128)(2,1)S(1)} %copy-done.2, ...), custom_call_target="tpu_custom_call" | custom-call | flops 1 | bytes 1 | tf_op jit(solution)/shard_map/pallas_call | solution.py:298
  48.1 0.1 collective-permute-start.11
  48.3 0.4 collective-permute-start.10
  48.7 2.2 %shard_map.61 = (bf16[256,768]{1,0:T(8,128)(2,1)S(1)}, f32[128,1024]{1,0:T(8,128)S(1)}, f32[8,256,256]{2,1,0:T(8,128)S(1)}) custom-call(bf16[1024,512]{1,0:T(8,128)(2,1)S(1)} %copy-done.2, bf16[768,512]{1,0:T(8,128)(2,1)S(1)} %get-tuple-element.118.refs_1_, bf16[4,768,128]{2,1,0:T(8,128)(2,1)S(1)} %get-tuple-element.119.refs_2_, ...), custom_call_target="tpu_custom_call" | custom-call | flops 1 | bytes 1 | tf_op jit(solution)/shard_map/pallas_call | solution.py:298
  50.9 0.7 shard_map.62
  51.6 0.1 broadcast_compare_fusion.2
  51.8 0.2 multiply_convert_fusion
  52.0 1.8 %collective-permute-start.12 = (f16[4,256,256]{2,1,0:T(8,128)(2,1)S(1)}, f16[4,256,256]{2,1,0:T(8,128)(2,1)S(1)}, u32[]{:S(2)}, u32[]{:S(2)}) collective-permute-start(f16[4,256,256]{2,1,0:T(8,128)(2,1)S(1)} %multiply_convert_fusion), channel_id=1, source_target_pairs={{0,1},{1,0},{2,3},{3,2},{4,5},{5,4},{6,7},{7,6},{8,9},{9,8},{10,11... | collective-permute-start | bytes 1572872 | tf_op jit(solution)/shard_map/ppermute | solution.py:33
  53.8 1.1 %shard_map.63 = (f32[4,256,256]{2,1,0:T(8,128)S(1)}, f32[8,96,256]{2,1,0:T(8,128)S(1)}) custom-call(bf16[256,768]{1,0:T(8,128)(2,1)S(1)} %collective-permute-done.10.refs_1_.refs_0_, f32[8,256,256]{2,1,0:T(8,128)S(1)} %get-tuple-element.124.refs_4_.refs_1_, f32[128,1024]{1,0:T(8,128)S(1)} %get-tuple-element.129.refs_2_, ...), custom_call_target="tpu_custom_call" | custom-call | flops 1 | bytes 1 | tf_op jit(solution)/shard_map/pallas_call | solution.py:298
  55.1 0.3 multiply_convert_fusion.2
  55.4 3.7 %collective-permute-start.15 = (f16[2,96,256]{2,1,0:T(8,128)(2,1)S(1)}, f16[2,96,256]{2,1,0:T(8,128)(2,1)S(1)}, u32[]{:S(2)}, u32[]{:S(2)}) collective-permute-start(f16[2,96,256]{2,1,0:T(8,128)(2,1)S(1)} %get-tuple-element.164), channel_id=1, source_target_pairs={{0,6},{1,7},{2,4},{3,5},{4,2},{5,3},{6,0},{7,1},{8,14},{9,15},{10,... | collective-permute-start | bytes 294920 | tf_op jit(solution)/shard_map/ppermute | solution.py:33
  59.1 0.8 collective-permute-start.13
  59.9 6.1 %collective-permute-done.12 = f16[4,256,256]{2,1,0:T(8,128)(2,1)S(1)} collective-permute-done((f16[4,256,256]{2,1,0:T(8,128)(2,1)S(1)}, f16[4,256,256]{2,1,0:T(8,128)(2,1)S(1)}, u32[]{:S(2)}, u32[]{:S(2)}) %collective-permute-start.12) | collective-permute-done | bytes 524320 | tf_op jit(solution)/shard_map/ppermute | solution.py:33
  66.0 0.1 convert_element_type.55
  66.1 0.3 add_select_fusion
  66.5 0.2 fusion.1
  66.6 0.7 collective-permute-done.14
  67.3 1.2 %collective-permute-start.16 = (f16[256,256]{1,0:T(8,128)(2,1)S(1)}, f16[256,256]{1,0:T(8,128)(2,1)S(1)}, u32[]{:S(2)}, u32[]{:S(2)}) collective-permute-start(f16[256,256]{1,0:T(8,128)(2,1)S(1)} %get-tuple-element.138), channel_id=1, source_target_pairs={{0,2},{1,3},{2,0},{3,1},{4,6},{5,7},{6,4},{7,5},{8,10},{9,11},{10,... | collective-permute-start | bytes 393224 | tf_op jit(solution)/shard_map/ppermute | solution.py:33
  68.6 2.6 %collective-permute-start.17 = (f16[256,256]{1,0:T(8,128)(2,1)S(1)}, f16[256,256]{1,0:T(8,128)(2,1)S(1)}, u32[]{:S(2)}, u32[]{:S(2)}) collective-permute-start(f16[256,256]{1,0:T(8,128)(2,1)S(1)} %get-tuple-element.140), channel_id=1, source_target_pairs={{0,4},{1,5},{2,6},{3,7},{4,0},{5,1},{6,2},{7,3},{8,12},{9,13},{10,... | collective-permute-start | bytes 393224 | tf_op jit(solution)/shard_map/ppermute | solution.py:33
  71.1 0.6 collective-permute-start.18
  71.7 2.2 %collective-permute-done.16 = f16[256,256]{1,0:T(8,128)(2,1)S(1)} collective-permute-done((f16[256,256]{1,0:T(8,128)(2,1)S(1)}, f16[256,256]{1,0:T(8,128)(2,1)S(1)}, u32[]{:S(2)}, u32[]{:S(2)}) %collective-permute-start.16) | collective-permute-done | bytes 131104 | tf_op jit(solution)/shard_map/ppermute | solution.py:33
  74.1 0.2 add_select_fusion.2
  74.3 1.1 %collective-permute-start.19 = (f16[96,256]{1,0:T(8,128)(2,1)S(1)}, f16[96,256]{1,0:T(8,128)(2,1)S(1)}, u32[]{:S(2)}, u32[]{:S(2)}) collective-permute-start(f16[96,256]{1,0:T(8,128)(2,1)S(1)} %fusion.7), channel_id=1, source_target_pairs={{0,1},{1,0},{2,3},{3,2},{4,5},{5,4},{6,7},{7,6},{8,9},{9,8},{10,11... | collective-permute-start | bytes 147464 | tf_op jit(solution)/shard_map/ppermute | solution.py:33
  75.4 3.9 %collective-permute-done.18 = f16[256,256]{1,0:T(8,128)(2,1)S(1)} collective-permute-done((f16[256,256]{1,0:T(8,128)(2,1)S(1)}, f16[256,256]{1,0:T(8,128)(2,1)S(1)}, u32[]{:S(2)}, u32[]{:S(2)}) %collective-permute-start.18) | collective-permute-done | bytes 131104 | tf_op jit(solution)/shard_map/ppermute | solution.py:33
  79.3 1.6 %collective-permute-done.17 = f16[256,256]{1,0:T(8,128)(2,1)S(1)} collective-permute-done((f16[256,256]{1,0:T(8,128)(2,1)S(1)}, f16[256,256]{1,0:T(8,128)(2,1)S(1)}, u32[]{:S(2)}, u32[]{:S(2)}) %collective-permute-start.17) | collective-permute-done | bytes 131104 | tf_op jit(solution)/shard_map/ppermute | solution.py:33
  81.0 0.2 add_select_fusion.1.refs_0_
  81.3 0.1 add_select_fusion.3.refs_1_
  81.3 0.2 shard_map.64
  81.5 0.1 multiply_convert_fusion.1
  81.6 1.6 %collective-permute-start.20 = (f16[336,256]{1,0:T(8,128)(2,1)S(1)}, f16[336,256]{1,0:T(8,128)(2,1)S(1)}, u32[]{:S(2)}, u32[]{:S(2)}) collective-permute-start(f16[336,256]{1,0:T(8,128)(2,1)S(1)} %get-tuple-element.146), channel_id=1, source_target_pairs={{0,16},{8,24},{16,0},{24,8},{1,17},{9,25},{17,1},{25,9},{2,18},{10... | collective-permute-start | bytes 516104 | tf_op jit(solution)/shard_map/ppermute | solution.py:28
  83.2 3.9 %collective-permute-done.20 = f16[336,256]{1,0:T(8,128)(2,1)S(1)} collective-permute-done((f16[336,256]{1,0:T(8,128)(2,1)S(1)}, f16[336,256]{1,0:T(8,128)(2,1)S(1)}, u32[]{:S(2)}, u32[]{:S(2)}) %collective-permute-start.20) | collective-permute-done | bytes 172064 | tf_op jit(solution)/shard_map/ppermute | solution.py:28
  87.1 0.1 pad_maximum_fusion
  87.2 0.1 collective-permute-start.21
  87.3 1.6 %collective-permute-done.21 = f16[2,336,256]{2,1,0:T(8,128)(2,1)S(1)} collective-permute-done((f16[2,336,256]{2,1,0:T(8,128)(2,1)S(1)}, f16[2,336,256]{2,1,0:T(8,128)(2,1)S(1)}, u32[]{:S(2)}, u32[]{:S(2)}) %collective-permute-start.21) | collective-permute-done | bytes 344096 | tf_op jit(solution)/shard_map/ppermute | solution.py:28
  88.9 0.1 fusion.64
  89.0 0.1 maximum_convert_fusion
  89.2 0.3 select_multiply_fusion.refs_0_
  89.5 1.2 %shard_map.65 = (f32[256,1024]{1,0:T(8,128)}, f32[128,512]{1,0:T(8,128)}) custom-call(f32[4,336,256]{2,1,0:T(8,128)S(1)} %select_multiply_fusion.refs_0_), custom_call_target="tpu_custom_call" | custom-call | flops 1 | bytes 1 | tf_op jit(solution)/shard_map/pallas_call | solution.py:298
  (61 shorter events, 0.6 us)
Async XLA Ops:
  0.6 5.9 %copy-start.2 = (bf16[1024,512]{1,0:T(8,128)(2,1)S(1)}, bf16[1024,512]{1,0:T(8,128)(2,1)}, u32[]{:S(2)}) copy-start(bf16[1024,512]{1,0:T(8,128)(2,1)} %refs_0_.17) | copy-start | bytes 3145732
  1.8 4.7 %collective-permute-start.3 = (bf16[384,2048]{1,0:T(8,128)(2,1)}, bf16[384,2048]{1,0:T(8,128)(2,1)S(1)}, u32[]{:S(2)}, u32[]{:S(2)}) collective-permute-start(bf16[384,2048]{1,0:T(8,128)(2,1)} %refs_2_.1), channel_id=1, source_target_pairs={{0,8},{8,0},{16,24},{24,16},{1,9},{9,1},{17,25},{25,17},{2,10},{10... | collective-permute-start | bytes 4718600 | tf_op jit(solution)/shard_map/ppermute | solution.py:28
  2.3 15.4 %collective-permute-start.2 = (bf16[128,2048]{1,0:T(8,128)(2,1)S(1)}, bf16[128,2048]{1,0:T(8,128)(2,1)S(1)}, u32[]{:S(2)}, u32[]{:S(2)}) collective-permute-start(bf16[128,2048]{1,0:T(8,128)(2,1)S(1)} %slice.173), channel_id=1, source_target_pairs={{0,16},{8,24},{16,0},{24,8},{1,17},{9,25},{17,1},{25,9},{2,18},{10... | collective-permute-start | bytes 1572872 | tf_op jit(solution)/shard_map/ppermute | solution.py:28
  4.9 1.4 %copy-start.3 = (bf16[384,2048]{1,0:T(8,128)(2,1)S(1)}, bf16[384,2048]{1,0:T(8,128)(2,1)}, u32[]{:S(2)}) copy-start(bf16[384,2048]{1,0:T(8,128)(2,1)} %refs_2_.1) | copy-start | bytes 4718596
  6.3 1.4 %copy-start.4 = (bf16[384,2048]{1,0:T(8,128)(2,1)S(1)}, bf16[384,2048]{1,0:T(8,128)(2,1)}, u32[]{:S(2)}) copy-start(bf16[384,2048]{1,0:T(8,128)(2,1)} %refs_2_.1) | copy-start | bytes 4718596
  6.4 22.5 %collective-permute-start.1 = (bf16[128,2048]{1,0:T(8,128)(2,1)S(1)}, bf16[128,2048]{1,0:T(8,128)(2,1)S(1)}, u32[]{:S(2)}, u32[]{:S(2)}) collective-permute-start(bf16[128,2048]{1,0:T(8,128)(2,1)S(1)} %get-tuple-element.75), channel_id=1, source_target_pairs={{0,16},{8,24},{16,0},{24,8},{1,17},{9,25},{17,1},{25,9},{2,18},{10... | collective-permute-start | bytes 1572872 | tf_op jit(solution)/shard_map/ppermute | solution.py:28
  7.7 2.2 %copy-start = (bf16[2048,1024]{1,0:T(8,128)(2,1)S(1)}, bf16[2048,1024]{1,0:T(8,128)(2,1)}, u32[]{:S(2)}) copy-start(bf16[2048,1024]{1,0:T(8,128)(2,1)} %refs_0_.16) | copy-start | bytes 12582916
  9.9 10.3 %copy-start.1 = (bf16[2048,1024]{1,0:T(8,128)(2,1)S(1)}, bf16[2048,1024]{1,0:T(8,128)(2,1)}, u32[]{:S(2)}) copy-start(bf16[2048,1024]{1,0:T(8,128)(2,1)} %refs_0_.16) | copy-start | bytes 12582916
  17.7 4.4 %collective-permute-start.4 = (bf16[64,2048]{1,0:T(8,128)(2,1)S(1)}, bf16[64,2048]{1,0:T(8,128)(2,1)S(1)}, u32[]{:S(2)}, u32[]{:S(2)}) collective-permute-start(bf16[64,2048]{1,0:T(8,128)(2,1)S(1)} %get-tuple-element.79), channel_id=1, source_target_pairs={{0,8},{8,0},{16,24},{24,16},{1,9},{9,1},{17,25},{25,17},{2,10},{10... | collective-permute-start | bytes 786440 | tf_op jit(solution)/shard_map/ppermute | solution.py:28
  17.8 4.3 %collective-permute-start.5 = (bf16[64,2048]{1,0:T(8,128)(2,1)S(1)}, bf16[64,2048]{1,0:T(8,128)(2,1)S(1)}, u32[]{:S(2)}, u32[]{:S(2)}) collective-permute-start(bf16[64,2048]{1,0:T(8,128)(2,1)S(1)} %get-tuple-element.80), channel_id=1, source_target_pairs={{0,8},{8,0},{16,24},{24,16},{1,9},{9,1},{17,25},{25,17},{2,10},{10... | collective-permute-start | bytes 786440 | tf_op jit(solution)/shard_map/ppermute | solution.py:28
  18.3 21.6 %collective-permute-start = (bf16[128,2048]{1,0:T(8,128)(2,1)S(1)}, bf16[128,2048]{1,0:T(8,128)(2,1)S(1)}, u32[]{:S(2)}, u32[]{:S(2)}) collective-permute-start(bf16[128,2048]{1,0:T(8,128)(2,1)S(1)} %get-tuple-element.74), channel_id=1, source_target_pairs={{0,16},{8,24},{16,0},{24,8},{1,17},{9,25},{17,1},{25,9},{2,18},{10... | collective-permute-start | bytes 1572872 | tf_op jit(solution)/shard_map/ppermute | solution.py:28
  29.0 2.8 %collective-permute-start.6 = (bf16[64,2048]{1,0:T(8,128)(2,1)S(1)}, bf16[64,2048]{1,0:T(8,128)(2,1)S(1)}, u32[]{:S(2)}, u32[]{:S(2)}) collective-permute-start(bf16[64,2048]{1,0:T(8,128)(2,1)S(1)} %get-tuple-element.88), channel_id=1, source_target_pairs={{0,8},{8,0},{16,24},{24,16},{1,9},{9,1},{17,25},{25,17},{2,10},{10... | collective-permute-start | bytes 786440 | tf_op jit(solution)/shard_map/ppermute | solution.py:28
  29.1 2.7 %collective-permute-start.7 = (bf16[64,2048]{1,0:T(8,128)(2,1)S(1)}, bf16[64,2048]{1,0:T(8,128)(2,1)S(1)}, u32[]{:S(2)}, u32[]{:S(2)}) collective-permute-start(bf16[64,2048]{1,0:T(8,128)(2,1)S(1)} %get-tuple-element.89), channel_id=1, source_target_pairs={{0,8},{8,0},{16,24},{24,16},{1,9},{9,1},{17,25},{25,17},{2,10},{10... | collective-permute-start | bytes 786440 | tf_op jit(solution)/shard_map/ppermute | solution.py:28
  39.9 3.1 %collective-permute-start.8 = (bf16[64,2048]{1,0:T(8,128)(2,1)S(1)}, bf16[64,2048]{1,0:T(8,128)(2,1)S(1)}, u32[]{:S(2)}, u32[]{:S(2)}) collective-permute-start(bf16[64,2048]{1,0:T(8,128)(2,1)S(1)} %get-tuple-element.99), channel_id=1, source_target_pairs={{0,8},{8,0},{16,24},{24,16},{1,9},{9,1},{17,25},{25,17},{2,10},{10... | collective-permute-start | bytes 786440 | tf_op jit(solution)/shard_map/ppermute | solution.py:28
  40.0 3.0 %collective-permute-start.9 = (bf16[64,2048]{1,0:T(8,128)(2,1)S(1)}, bf16[64,2048]{1,0:T(8,128)(2,1)S(1)}, u32[]{:S(2)}, u32[]{:S(2)}) collective-permute-start(bf16[64,2048]{1,0:T(8,128)(2,1)S(1)} %get-tuple-element.100), channel_id=1, source_target_pairs={{0,8},{8,0},{16,24},{24,16},{1,9},{9,1},{17,25},{25,17},{2,10},{10... | collective-permute-start | bytes 786440 | tf_op jit(solution)/shard_map/ppermute | solution.py:28
  48.1 2.8 %collective-permute-start.11 = (f32[128,1024]{1,0:T(8,128)S(1)}, f32[128,1024]{1,0:T(8,128)S(1)}, u32[]{:S(2)}, u32[]{:S(2)}) collective-permute-start(f32[128,1024]{1,0:T(8,128)S(1)} %get-tuple-element.123), channel_id=1, source_target_pairs={{0,8},{8,0},{16,24},{24,16},{1,9},{9,1},{17,25},{25,17},{2,10},{10... | collective-permute-start | bytes 1572872 | tf_op jit(solution)/shard_map/ppermute | solution.py:28
  48.3 2.6 %collective-permute-start.10 = (bf16[256,768]{1,0:T(8,128)(2,1)S(1)}, bf16[256,768]{1,0:T(8,128)(2,1)S(1)}, u32[]{:S(2)}, u32[]{:S(2)}) collective-permute-start(bf16[256,768]{1,0:T(8,128)(2,1)S(1)} %get-tuple-element.121), channel_id=1, source_target_pairs={{0,8},{8,0},{16,24},{24,16},{1,9},{9,1},{17,25},{25,17},{2,10},{10... | collective-permute-start | bytes 1179656 | tf_op jit(solution)/shard_map/ppermute | solution.py:28
  52.0 14.0 %collective-permute-start.12 = (f16[4,256,256]{2,1,0:T(8,128)(2,1)S(1)}, f16[4,256,256]{2,1,0:T(8,128)(2,1)S(1)}, u32[]{:S(2)}, u32[]{:S(2)}) collective-permute-start(f16[4,256,256]{2,1,0:T(8,128)(2,1)S(1)} %multiply_convert_fusion), channel_id=1, source_target_pairs={{0,1},{1,0},{2,3},{3,2},{4,5},{5,4},{6,7},{7,6},{8,9},{9,8},{10,11... | collective-permute-start | bytes 1572872 | tf_op jit(solution)/shard_map/ppermute | solution.py:33
  55.4 11.2 %collective-permute-start.15 = (f16[2,96,256]{2,1,0:T(8,128)(2,1)S(1)}, f16[2,96,256]{2,1,0:T(8,128)(2,1)S(1)}, u32[]{:S(2)}, u32[]{:S(2)}) collective-permute-start(f16[2,96,256]{2,1,0:T(8,128)(2,1)S(1)} %get-tuple-element.164), channel_id=1, source_target_pairs={{0,6},{1,7},{2,4},{3,5},{4,2},{5,3},{6,0},{7,1},{8,14},{9,15},{10,... | collective-permute-start | bytes 294920 | tf_op jit(solution)/shard_map/ppermute | solution.py:33
  59.1 8.2 %collective-permute-start.14 = (f16[2,96,256]{2,1,0:T(8,128)(2,1)S(1)}, f16[2,96,256]{2,1,0:T(8,128)(2,1)S(1)}, u32[]{:S(2)}, u32[]{:S(2)}) collective-permute-start(f16[2,96,256]{2,1,0:T(8,128)(2,1)S(1)} %get-tuple-element.165), channel_id=1, source_target_pairs={{0,4},{1,5},{2,6},{3,7},{4,0},{5,1},{6,2},{7,3},{8,12},{9,13},{10,... | collective-permute-start | bytes 294920 | tf_op jit(solution)/shard_map/ppermute | solution.py:33
  59.1 8.2 %collective-permute-start.13 = (f16[2,96,256]{2,1,0:T(8,128)(2,1)S(1)}, f16[2,96,256]{2,1,0:T(8,128)(2,1)S(1)}, u32[]{:S(2)}, u32[]{:S(2)}) collective-permute-start(f16[2,96,256]{2,1,0:T(8,128)(2,1)S(1)} %get-tuple-element.166), channel_id=1, source_target_pairs={{0,2},{1,3},{2,0},{3,1},{4,6},{5,7},{6,4},{7,5},{8,10},{9,11},{10,... | collective-permute-start | bytes 294920 | tf_op jit(solution)/shard_map/ppermute | solution.py:33
  67.3 6.5 %collective-permute-start.16 = (f16[256,256]{1,0:T(8,128)(2,1)S(1)}, f16[256,256]{1,0:T(8,128)(2,1)S(1)}, u32[]{:S(2)}, u32[]{:S(2)}) collective-permute-start(f16[256,256]{1,0:T(8,128)(2,1)S(1)} %get-tuple-element.138), channel_id=1, source_target_pairs={{0,2},{1,3},{2,0},{3,1},{4,6},{5,7},{6,4},{7,5},{8,10},{9,11},{10,... | collective-permute-start | bytes 393224 | tf_op jit(solution)/shard_map/ppermute | solution.py:33
  68.6 12.3 %collective-permute-start.17 = (f16[256,256]{1,0:T(8,128)(2,1)S(1)}, f16[256,256]{1,0:T(8,128)(2,1)S(1)}, u32[]{:S(2)}, u32[]{:S(2)}) collective-permute-start(f16[256,256]{1,0:T(8,128)(2,1)S(1)} %get-tuple-element.140), channel_id=1, source_target_pairs={{0,4},{1,5},{2,6},{3,7},{4,0},{5,1},{6,2},{7,3},{8,12},{9,13},{10,... | collective-permute-start | bytes 393224 | tf_op jit(solution)/shard_map/ppermute | solution.py:33
  71.1 8.1 %collective-permute-start.18 = (f16[256,256]{1,0:T(8,128)(2,1)S(1)}, f16[256,256]{1,0:T(8,128)(2,1)S(1)}, u32[]{:S(2)}, u32[]{:S(2)}) collective-permute-start(f16[256,256]{1,0:T(8,128)(2,1)S(1)} %get-tuple-element.141), channel_id=1, source_target_pairs={{0,6},{1,7},{2,4},{3,5},{4,2},{5,3},{6,0},{7,1},{8,14},{9,15},{10,... | collective-permute-start | bytes 393224 | tf_op jit(solution)/shard_map/ppermute | solution.py:33
  74.3 6.9 %collective-permute-start.19 = (f16[96,256]{1,0:T(8,128)(2,1)S(1)}, f16[96,256]{1,0:T(8,128)(2,1)S(1)}, u32[]{:S(2)}, u32[]{:S(2)}) collective-permute-start(f16[96,256]{1,0:T(8,128)(2,1)S(1)} %fusion.7), channel_id=1, source_target_pairs={{0,1},{1,0},{2,3},{3,2},{4,5},{5,4},{6,7},{7,6},{8,9},{9,8},{10,11... | collective-permute-start | bytes 147464 | tf_op jit(solution)/shard_map/ppermute | solution.py:33
  81.6 5.5 %collective-permute-start.20 = (f16[336,256]{1,0:T(8,128)(2,1)S(1)}, f16[336,256]{1,0:T(8,128)(2,1)S(1)}, u32[]{:S(2)}, u32[]{:S(2)}) collective-permute-start(f16[336,256]{1,0:T(8,128)(2,1)S(1)} %get-tuple-element.146), channel_id=1, source_target_pairs={{0,16},{8,24},{16,0},{24,8},{1,17},{9,25},{17,1},{25,9},{2,18},{10... | collective-permute-start | bytes 516104 | tf_op jit(solution)/shard_map/ppermute | solution.py:28
  87.2 1.7 %collective-permute-start.21 = (f16[2,336,256]{2,1,0:T(8,128)(2,1)S(1)}, f16[2,336,256]{2,1,0:T(8,128)(2,1)S(1)}, u32[]{:S(2)}, u32[]{:S(2)}) collective-permute-start(f16[2,336,256]{2,1,0:T(8,128)(2,1)S(1)} %pad_maximum_fusion), channel_id=1, source_target_pairs={{0,8},{8,0},{16,24},{24,16},{1,9},{9,1},{17,25},{25,17},{2,10},{10... | collective-permute-start | bytes 1032200 | tf_op jit(solution)/shard_map/ppermute | solution.py:28

commit v4 on v3

--- a/solution.py
+++ b/solution.py
@@ -15,7 +15,7 @@
 NT = (((1,), (1,)), ((), ()))
 TN = (((0,), (0,)), ((), ()))
 CHUNKS = 3
-CUT = 176
+CUT = 240
 VMEM_LIMIT = 20 * 1024 * 1024
 
 
@@ -85,6 +85,7 @@
     pred = dot(embed[:tok], embed, NT)
     resid = residual(inter, pred, sq[:tok, :1], sq_cols, emb)
     o["summed", 0][...] = dot(resid, embed)
+    put_kinds(o)
     o["token"][...] = jnp.zeros((8, 128), F32)
 
 
@@ -116,13 +117,14 @@
 
 def rs_stage(k, i, o, s):
     emb = i["w_second"].shape[1]
-    half = i["new", 0].shape[0]
-    part = 2 * half
-    for h in range(2):
-        o["feats"][h * half : (h + 1) * half] = i["new", h][...]
-    embed_rs = encode(o["feats"][...], i["w_first"], i["w_second"])
+    part = i["feats", ("rem", k)].shape[0]
+    count = i["new", 0].shape[0]
     s["both"][:part] = i["feats", ("rem", k)][...]
-    s["both"][part:] = o["feats"][...]
+    for h in range(part // count):
+        s["both"][part + h * count : part + (h + 1) * count] = i["new", h][...]
+    if "feats" in o:
+        o["feats"][...] = s["both"][part:]
+    embed_rs = encode(s["both"][part:], i["w_first"], i["w_second"])
     s["embeds"][:part] = i["embed", ("rem", k)][...]
     s["embeds"][part:] = embed_rs
     top, embed_new = s["both"][...], s["embeds"][...]
@@ -154,18 +156,12 @@
 
 
 def last_stage(factor, i, o, s):
-    place = lax.axis_index("blk")
-    wide = i["w_second"].shape[1] // 4
     start = 0
     for value in rs_stage(CHUNKS, i, o, s):
         rows = pl.ds(start, value.shape[0])
-        piece = (value * factor).astype(BF16)
-        o["dembed"][rows, :] = piece
-        for q in range(4):
-            o["quarters"][q, rows, :] = piece[:, q * wide : (q + 1) * wide]
+        o["dembed"][rows, :] = (value * factor).astype(BF16)
         start += value.shape[0]
-    dpre_share(place, 1, i, o["dembed"], o["give"])
-    second_share(place ^ 1, o["quarters"], hiddens_of(i), o["second_give"])
+    dpre_share(lax.axis_index("blk"), 1, i, o["dembed"], o["give"])
 
 
 def hiddens_of(i):
@@ -185,10 +181,19 @@
 def own_share(i, o, s):
     place = lax.axis_index("blk")
     dpre_share(place, 0, i, i["dembed"], o["keep"])
-    second_share(place, i["quarters"], hiddens_of(i), o["second"])
-    me = dp_high()
-    for d in range(8):
-        o["first"][d] = first_block(o["keep"], core_rows(i, 0), me ^ d)
+    for z in range(4):
+        block = dp_high() ^ (2 * z + 1)
+        o["first"][z] = first_block(o["keep"], core_rows(i, 0), block, 0, CUT)
+    o["second_give"][...] = second_share(place ^ 1, i["dembed"], hiddens_of(i))
+
+
+def put_kinds(o):
+    for name, first, second in (("one", CUT, 0), ("two", 256 - CUT, 64), ("all", 256, 64)):
+        kind = o["kind_" + name]
+        kind[:first] = jnp.zeros((first, 256), F32)
+        if second:
+            kind[first : first + second] = jnp.ones((second, 256), F32)
+        kind[first + second :] = jnp.full((16, 256), 2.0, F32)
 
 
 def dp_high():
@@ -214,14 +219,15 @@
     return total
 
 
-def second_share(quarter, dembed, hiddens, out):
+def second_share(quarter, dembed, hiddens):
     total, start = None, 0
+    columns = pl.ds(pl.multiple_of(quarter * 128, 128), 128)
     for hidden in hiddens:
         count = hidden.shape[0]
-        part = dot(dembed[quarter, start : start + count, :], hidden[...], TN)
+        part = dot(dembed[pl.ds(start, count), columns], hidden[...], TN)
         total = part if total is None else total + part
         start += count
-    out[...] = total
+    return total
 
 
 def exponent(bound):
@@ -233,57 +239,42 @@
     ref[d, start + 8 : start + 16] = exp_second
 
 
-def put_second(ref, d, second, block):
-    value = second[:, pl.ds(pl.multiple_of(block * 128, 128), 128)]
-    ref[d, CUT : CUT + 64, :128] = value[:64]
-    ref[d, CUT : CUT + 64, 128:] = value[64:]
-
-
 def first_gradients(i, o, s):
-    o["second"][...] = i["second_keep"][...] + i["second_got"][...]
     sums = jnp.sum(jnp.abs(i["keep"][...].astype(F32)), axis=1, keepdims=True)
     sums += jnp.sum(jnp.abs(i["got"][...].astype(F32)), axis=1, keepdims=True)
-    exp_first = exponent(3.0 * jnp.max(sums, axis=0, keepdims=True))
-    most = jnp.max(jnp.abs(o["second"][...]), axis=1, keepdims=True)
-    exp_second = exponent(jnp.max(most, axis=0, keepdims=True))
-    o["exps"][0] = jnp.broadcast_to(exp_first, (8, 256))
-    o["exps"][1] = jnp.broadcast_to(exp_second, (8, 256))
+    top = exponent(3.0 * jnp.max(sums, axis=0, keepdims=True))
+    o["exp_first"][...] = jnp.broadcast_to(top, (8, 256))
+    for z in range(4):
+        value = first_block(i["got"], core_rows(i, 1), dp_high() ^ (2 * z + 1), 0, CUT)
+        o["one"][z, :CUT] = value + i["first"][z]
+        put_tail(o["one"], z, CUT, o["exp_first"][...], o["exp_first"][...])
+
+
+def second_gradients(i, o, s):
+    me = dp_high()
     bottom = 256 - CUT
-    o["kind_one"][:CUT] = jnp.zeros((CUT, 256), F32)
-    o["kind_one"][CUT : CUT + 64] = jnp.ones((64, 256), F32)
-    o["kind_one"][CUT + 64 :] = jnp.full((16, 256), 2.0, F32)
-    o["kind_two"][:bottom] = jnp.zeros((bottom, 256), F32)
-    o["kind_two"][bottom:] = jnp.full((16, 256), 2.0, F32)
-    o["kind_all"][:256] = jnp.zeros((256, 256), F32)
-    o["kind_all"][256:320] = jnp.ones((64, 256), F32)
-    o["kind_all"][320:] = jnp.full((16, 256), 2.0, F32)
-    me = dp_high()
+    mine = second_share(lax.axis_index("blk"), i["dembed"], hiddens_of(i))
+    s["second"][...] = mine + i["second_got"][...]
+    most = jnp.max(jnp.abs(s["second"][...]), axis=1, keepdims=True)
+    exp_second = jnp.broadcast_to(exponent(jnp.max(most, axis=0, keepdims=True)), (8, 256))
+    for d in range(8):
+        value = first_block(i["keep"], core_rows(i, 0), me ^ d, CUT, 256)
+        o["two"][d, :bottom] = value + first_block(i["got"], core_rows(i, 1), me ^ d, CUT, 256)
+        second = s["second"][:, pl.ds(pl.multiple_of((me ^ d) * 128, 128), 128)]
+        o["two"][d, bottom : bottom + 64, :128] = second[:64]
+        o["two"][d, bottom : bottom + 64, 128:] = second[64:]
+        put_tail(o["two"], d, bottom + 64, i["exp_first"][...], exp_second)
+
+
+def kept_gradients(i, o, s):
     for z in range(4):
-        d = 2 * z + 1
-        value = first_block(i["got"], core_rows(i, 1), me ^ d, 0, CUT)
-        o["one"][z, :CUT] = value + i["first"][d, :CUT]
-        put_second(o["one"], z, o["second"], me ^ d)
-        put_tail(o["one"], z, CUT + 64, o["exps"][0], o["exps"][1])
-
-
-def other_gradients(i, o, s):
-    me = dp_high()
-    rows = core_rows(i, 1)
-    bottom = 256 - CUT
-    for z in range(4):
-        for x in range(2):
-            d = 2 * z + x
-            top = CUT if x else 0
-            value = first_block(i["got"], rows, me ^ d, top, 256) + i["first"][d, top:]
-            o["two"][d, :bottom] = value[CUT - top :]
-            put_tail(o["two"], d, bottom, i["exps"][0], i["exps"][0])
-            if x == 0:
-                o["one"][z, :CUT] = value[:CUT]
-                put_second(o["one"], z, i["second"], me ^ d)
-                put_tail(o["one"], z, CUT + 64, i["exps"][0], i["exps"][1])
-
-
-def run(body, ins, outs, scratch, limit=VMEM_LIMIT):
+        block = dp_high() ^ (2 * z)
+        value = first_block(i["keep"], core_rows(i, 0), block, 0, CUT)
+        o["one"][z, :CUT] = value + first_block(i["got"], core_rows(i, 1), block, 0, CUT)
+        put_tail(o["one"], z, CUT, i["exp_first"][...], i["exp_first"][...])
+
+
+def run(body, ins, outs, scratch, limit=VMEM_LIMIT, to_hbm=False):
     names_in, names_out, names_s = list(ins), list(outs), list(scratch)
 
     def kernel(*refs):
@@ -299,7 +290,7 @@
         kernel,
         out_shape=shapes,
         in_specs=[pl.BlockSpec(memory_space=spaces.get(n, vmem)) for n in names_in],
-        out_specs=[pl.BlockSpec(memory_space=vmem)] * len(shapes),
+        out_specs=[pl.BlockSpec(memory_space=pl.ANY if to_hbm else vmem)] * len(shapes),
         scratch_shapes=[vmem(*v) if isinstance(v, tuple) else v for v in scratch.values()],
         compiler_params=pltpu.CompilerParams(vmem_limit_bytes=limit),
         cost_estimate=pl.CostEstimate(flops=1, bytes_accessed=1, transcendentals=0),
@@ -308,9 +299,9 @@
 
 
 def split(i, o, s):
-    half = i["rem"].shape[0] // 2
-    for h in range(2):
-        o["rows", h][...] = i["rem"][h * half : (h + 1) * half]
+    count = i["rem"].shape[0] // len(o)
+    for h in range(len(o)):
+        o["rows", h][...] = i["rem"][h * count : (h + 1) * count]
 
 
 def fetch(pairs, i, o, s):
@@ -327,25 +318,32 @@
     one, two, out = i["one"], i["two"], o["all"]
     bottom = 256 - CUT
     out[:256] = jnp.concatenate([one[:CUT], two[:bottom]], 0).T
-    block = one[CUT : CUT + 64]
+    block = two[bottom : bottom + 64]
     second = jnp.concatenate([block[:, :128], block[:, 128:]], 0).T
     out[256:320, :128] = second[:64]
     out[256:320, 128:] = second[64:]
-    out[320:328, :128] = one[CUT + 64 : CUT + 72, :128]
-    lane = lax.broadcasted_iota(jnp.int32, (8, 128), 1)
-    tail = two[bottom : bottom + 8, 128:]
-    out[320:328, 128:] = jnp.where(lane < CUT - 128, one[CUT + 64 : CUT + 72, 128:], tail)
-    out[328:] = one[CUT + 72 :]
+    lane = lax.broadcasted_iota(jnp.int32, (8, 256), 1)
+    tail = two[bottom + 64 : bottom + 72]
+    out[320:328] = jnp.where(lane < CUT, one[CUT : CUT + 8], tail)
+    out[328:] = two[bottom + 72 :]
 
 
 def place_quarters(i, o, s):
     me = lax.axis_index("blk")
+    copies = []
     for j in range(4):
         q = me ^ j
-        o["first"][:, pl.ds(pl.multiple_of(q * 256, 256), 256)] = i["all"][j, :256]
+        first = o["first"].at[:, pl.ds(pl.multiple_of(q * 256, 256), 256)]
         columns = pl.ds(pl.multiple_of(q * 128, 128), 128)
-        o["second"][:64, columns] = i["all"][j, 256:320, :128]
-        o["second"][64:, columns] = i["all"][j, 256:320, 128:]
+        pairs = [(i["all", j].at[pl.ds(0, 256), :], first)]
+        for h in range(2):
+            block = i["all", j].at[pl.ds(256, 64), pl.ds(128 * h, 128)]
+            pairs.append((block, o["second"].at[pl.ds(64 * h, 64), columns]))
+        for n, (source, target) in enumerate(pairs):
+            copies.append(pltpu.make_async_copy(source, target, s["sems"].at[3 * j + n]))
+            copies[-1].start()
+    for copy in copies:
+        copy.wait()
 
 
 def encode16(total, kind, tail):
@@ -437,23 +435,21 @@
     bits = dp_count.bit_length() - 1
     k = CHUNKS
     part = tok // k
-
-    rem = []
+    rows_one, rows_two = CUT + 16, 256 - CUT + 64 + 16
+    lanes = 256 * 8 // dp_count
+    extra = dp_count // 8
+
     rows, own = lax.optimization_barrier((fingerprints[:part], fingerprints))
-    rem.append(blk_swap(rows, 2))
-    for start, count in ((1, k - 1),):
-        names = [("rows", j) for j in range(start, start + count)]
-        out = run(
-            functools.partial(fetch, [("arg", j * part, part, ("rows", j)) for _, j in names]),
-            {"arg": fingerprints},
-            {name: ((part, width), BF16) for name in names},
-            {"sems": pltpu.SemaphoreType.DMA((count,))},
-            limit=2 << 20,
-        )
-        rem += [blk_swap(out[name], 2) for name in names]
+    rem = [blk_swap(rows, 2)]
+    out = run(
+        functools.partial(fetch, [("arg", j * part, part, ("rows", j)) for j in range(1, k)]),
+        {"arg": fingerprints},
+        {("rows", j): ((part, width), BF16) for j in range(1, k)},
+        {"sems": pltpu.SemaphoreType.DMA((k - 1,))},
+        limit=2 << 20,
+    )
+    rem += [blk_swap(out["rows", j], 2) for j in range(1, k)]
     sib = blk_swap(own, 1)
-    rs = []
-
     base = {"w_first": w_first, "w_second": w_second}
     out = run(
         first_stage,
@@ -466,23 +462,27 @@
             "sq": ((2 * tok, 128), F32),
             ("summed", 0): ((tok, emb), F32),
             "token": ((8, 128), F32),
+            "kind_one": ((rows_one, 256), F32),
+            "kind_two": ((rows_two, 256), F32),
+            "kind_all": ((336, 256), F32),
         },
         {"pre": ((tok // 3, hid), F32), "hidden": ((tok // 3, hid), BF16)},
     )
     token = out["token"]
+    kinds = [out["kind_one"], out["kind_two"], out["kind_all"]]
     hidden, gate, feats = [out["hidden"]], [out["gate"]], [out["feats"]]
     embed, sq, summed = [out["embed"]], [out["sq"]], [out["summed", 0]]
     feats, embed, sq, summed = {0: feats[0]}, {0: embed[0]}, {0: sq[0]}, summed
-    half = part // 2
     for step in range(1, k + 1):
+        pieces = 2 if step < k else 1
         out = run(
             split,
             {"rem": rem[step - 1], "token": token},
-            {("rows", h): ((half, width), BF16) for h in range(2)},
+            {("rows", h): ((part // pieces, width), BF16) for h in range(pieces)},
             {},
             limit=2 << 20,
         )
-        rs = [blk_swap(out["rows", h], 1) for h in range(2)]
+        rs = [blk_swap(out["rows", h], 1) for h in range(pieces)]
         ins = {**base, "new": rem[step - 1]}
         for name in feats:
             if name == 0 or name[0] == "rs":
@@ -506,7 +506,7 @@
         name = ("rem", step)
         feats[name], embed[name] = rem[step - 1], out["embed"]
 
-        ins = {**base, ("new", 0): rs[0], ("new", 1): rs[1], "total": out["total"]}
+        ins = {**base, **{("new", h): r for h, r in enumerate(rs)}, "total": out["total"]}
         for j in range(step + 1):
             name = ("rem", j) if j else 0
             ins["feats", name] = feats[name]
@@ -535,81 +535,65 @@
         functools.partial(last_stage, factor),
         {**ins, **rows},
         {
-            "feats": ((part, width), BF16),
             "dembed": ((2 * tok, emb), BF16),
-            "quarters": ((4, 2 * tok, emb // 4), BF16),
             "give": ((256, 2 * tok), BF16),
-            "second_give": ((emb // 4, hid), F32),
         },
         scratch,
     )
-    feats["rs", k] = out["feats"]
+    feats["rs", k] = rs[0]
     got = blk_swap(out["give"], 1)
-    second_got = blk_swap(out["second_give"], 1)
     mine = {("feats", n): v for n, v in feats.items() if n == 0 or n[0] == "rem"}
     theirs = {("feats", n): v for n, v in feats.items() if n == 0 or n[0] == "rs"}
+    dembed = out["dembed"]
     own = run(
         own_share,
-        {
-            "w_second": w_second,
-            "dembed": out["dembed"],
-            "quarters": out["quarters"],
-            **rows,
-            **mine,
-        },
+        {"w_second": w_second, "dembed": dembed, **rows, **mine},
         {
             "keep": ((256, 2 * tok), BF16),
-            "second": ((emb // 4, hid), F32),
-            "first": ((8, 256, 256), F32),
+            "second_give": ((emb // 4, hid), F32),
+            "first": ((4, CUT, 256), F32),
         },
         {},
     )
-    rows_one, rows_two = CUT + 64 + 16, 256 - CUT + 16
-    lanes = 256 * 8 // dp_count
-    extra = dp_count // 8
+    second_got = blk_swap(own["second_give"], 1)
     out = run(
         first_gradients,
-        {
-            "keep": own["keep"],
-            "got": got,
-            "second_keep": own["second"],
-            "second_got": second_got,
-            "first": own["first"],
-            **theirs,
-        },
-        {
-            "second": ((emb // 4, hid), F32),
-            "exps": ((2, 8, 256), F32),
-            "one": ((4, rows_one, 256), F32),
-            "kind_one": ((rows_one, 256), F32),
-            "kind_two": ((rows_two, 256), F32),
-            "kind_all": ((336, 256), F32),
-        },
+        {"keep": own["keep"], "got": got, "first": own["first"], **theirs},
+        {"one": ((4, rows_one, 256), F32), "exp_first": ((8, 256), F32)},
         {},
     )
-    kinds, one_give = (out["kind_one"], out["kind_two"], out["kind_all"]), out["one"]
+    one_give = out["one"]
     more = extra.bit_length() - 1
     shape = (2,) * more
     kind_one, kind_two = kinds[0][:, :lanes], kinds[1][:, :lanes]
     shifts = [more + 1, more] + [more - 1 - n for n in range(more)]
     rest = list(range(2, more + 2))
-    cut = functools.partial(split_lanes, bounds=(CUT, CUT + 64), count=extra)
+    cut = functools.partial(split_lanes, bounds=(0, 0), count=extra)
     one_give = cut(one_give).reshape((4,) + shape + (rows_one, lanes))
     early = encode16(one_give, kind_one, rows_one - 16)
     got, early = lax.optimization_barrier((got, early))
+    ins = {"keep": own["keep"], "got": got, "exp_first": out["exp_first"], **mine, **theirs}
     out = run(
-        other_gradients,
-        {"got": got, "first": own["first"], "second": out["second"], "exps": out["exps"], **theirs},
-        {"one": ((4, rows_one, 256), F32), "two": ((8, rows_two, 256), F32)},
-        {},
+        second_gradients,
+        {
+            **ins,
+            "dembed": dembed,
+            "second_got": second_got,
+            **{n: v for n, v in rows.items() if n[0] == "hidden"},
+        },
+        {"two": ((8, rows_two, 256), F32)},
+        {"second": ((emb // 4, hid), F32)},
     )
-    one_keep = cut(out["one"]).reshape(one_give.shape)
-    two = split_lanes(out["two"], (0, 0), extra).reshape((4, 2) + shape + (rows_two, lanes))
+    two = split_lanes(out["two"], (256 - CUT, 320 - CUT), extra)
+    two = Sum(two.reshape((4, 2) + shape + (rows_two, lanes)), kind_two, [0] + rest + [1], 2)
+    packs_two = two.pack(0, shifts)
+    ins["got"], packs_two = lax.optimization_barrier((got, packs_two))
+    kept = run(kept_gradients, ins, {"one": ((4, rows_one, 256), F32)}, {})
+    one_keep = cut(kept["one"]).reshape(one_give.shape)
     one = Sum(jnp.stack([one_keep, one_give], 1), kind_one, [1, 0] + rest, 2, (one_keep, one_give))
-    two = Sum(two, kind_two, [0] + rest + [1], 2)
     one.pack(0, shifts)
     gots_one = one.swap(0, shifts, [early])
-    gots_two = two.swap(0, shifts, two.pack(0, shifts))
+    gots_two = two.swap(0, shifts, packs_two)
     for step in range(1, more + 2):
         one.receive(gots_one)
         packs = one.pack(step, shifts)
@@ -627,21 +611,23 @@
             {"all": ((336, 256), F32)},
             {},
         )
-        every = gather(encode16(out["all"], kinds[2], 320))
+        four = [out["all"]]
+        four += [decode16(g, kinds[2], 320) for g in gather(encode16(out["all"], kinds[2], 320))[1:]]
         out = run(
             place_quarters,
-            {"all": decode16(every, kinds[2], 320)},
+            {("all", j): v for j, v in enumerate(four)},
             {"first": ((lanes, hid), F32), "second": ((lanes // 2, emb), F32)},
-            {},
+            {"sems": pltpu.SemaphoreType.DMA((12,))},
+            to_hbm=True,
         )
         return out["first"], out["second"]
     packed = [encode16(one.total, kind_one, one.tail), encode16(two.total, kind_two, two.tail)]
-    every = gather(jnp.concatenate(packed, 0))
+    every = jnp.stack(gather(jnp.concatenate(packed, 0)))
     one = decode16(every[:, :rows_one], kind_one, one.tail)
     two = decode16(every[:, rows_one:], kind_two, two.tail)
     order = jnp.arange(4) ^ lax.axis_index("blk")
     first = jnp.concatenate([one[:, :CUT], two[:, : 256 - CUT]], 1)[order].reshape(hid, lanes)
-    second = one[order, CUT : CUT + 64]
+    second = two[order, 256 - CUT : 320 - CUT]
     second = jnp.concatenate([second[..., : lanes // 2], second[..., lanes // 2 :]], 1)
     return first.T, second.reshape(emb, lanes // 2).T
 
@@ -650,7 +636,7 @@
     across = blk_swap(packed, 2)
     pair = jnp.stack([packed, across])
     beside = blk_swap(pair, 1)
-    return jnp.stack([packed, beside[0], across, beside[1]])
+    return [packed, beside[0], across, beside[1]]
 
 
 def solution(mesh):

time: 91 us -> 90.7 us (level)
  waiting for transfers between devices: 29.1 us -> 27.5 us
  Pallas kernels: 30.7 us -> 32.2 us
    pallas_call x16 -> x17, Pallas kernels: 30.7 us -> 32.2 us  [run(): pl.pallas_call(kernel, out_shape=shapes, in_specs=[pl.BlockSpec(memory_sp...]
    ppermute x8, waiting for transfers between devices: 14.4 us -> 13.1 us  [dp_swap(): return lax.ppermute(value, 'dp', [(d, d ^ bit) for d in range(count)])]
    ppermute x14 -> x13, starting transfers between devices: 9.09 us -> 8.64 us  [blk_swap(): return lax.ppermute(value, 'blk', [(b, b ^ bit) for b in range(count)])]
    ppermute x14 -> x13, waiting for transfers between devices: 14.7 us -> 14.4 us  [blk_swap(): return lax.ppermute(value, 'blk', [(b, b ^ bit) for b in range(count)])]
    unnamed x27 -> x23, local copies, waits for them, and re-layouts: 4.86 us -> 5.04 us
  transfers between devices with their start and end apart: 22 -> 21, of which waited for: 10 -> 10; matrix products, arithmetic and copies ran while one was open for 2% -> 2% of each run, Pallas kernels for 26% -> 29%
where the time goes in v4:
time: 90.7 us; the launch traced here: 90.5 us
  Pallas kernels  32.2 us (36%)
  waiting for transfers between devices  27.5 us (30%)
  starting transfers between devices  20.8 us (23%)
  local copies, waits for them, and re-layouts  6.21 us (7%)
  other arithmetic  2.37 us (3%)
  between operations  1.4 us (2%)
    pallas_call x17, Pallas kernels, run(): pl.pallas_call(kernel, out_shape=shapes, in_specs=[pl.BlockSpec(memory_sp...  32.2 us
    ppermute x13, waiting for transfers between devices, blk_swap(): return lax.ppermute(value, 'blk', [(b, b ^ bit) for b in range(count)])  14.4 us
    ppermute x8, waiting for transfers between devices, dp_swap(): return lax.ppermute(value, 'dp', [(d, d ^ bit) for d in range(count)])  13.1 us
    ppermute x8, starting transfers between devices, dp_swap(): return lax.ppermute(value, 'dp', [(d, d ^ bit) for d in range(count)])  12.2 us
    ppermute x13, starting transfers between devices, blk_swap(): return lax.ppermute(value, 'blk', [(b, b ^ bit) for b in range(count)])  8.64 us
    unnamed x23, local copies, waits for them, and re-layouts  5.04 us
  transfers between devices with their start and end apart: 21, of which 10 were waited for; matrix products, arithmetic and copies ran while one was open for 2% of the time, Pallas kernels for 29%

profile of v4, /device:TPU:0, one launch (start us, length us, event | category | flops | bytes accessed | tf_op | source)
XLA Modules:
  0.0 90.5 jit_solution(1114093909578581631)
XLA Ops:
  0.6 1.2 %slice.189 = bf16[128,2048]{1,0:T(8,128)(2,1)S(1)} slice(bf16[384,2048]{1,0:T(8,128)(2,1)} %refs_0_.10), slice={[0:128], [0:2048]} | slice | bytes 1048576 | tf_op jit(solution)/shard_map/slice | solution.py:442
  1.8 0.5 collective-permute-start
  2.3 2.6 %collective-permute-start.3 = (bf16[128,2048]{1,0:T(8,128)(2,1)S(1)}, bf16[128,2048]{1,0:T(8,128)(2,1)S(1)}, u32[]{:S(2)}, u32[]{:S(2)}) collective-permute-start(bf16[128,2048]{1,0:T(8,128)(2,1)S(1)} %slice.189), channel_id=1, source_target_pairs={{0,16},{8,24},{16,0},{24,8},{1,17},{9,25},{17,1},{25,9},{2,18},{10... | collective-permute-start | bytes 1572872 | tf_op jit(solution)/shard_map/ppermute | solution.py:28
  4.9 1.4 %copy-done.2 = bf16[384,2048]{1,0:T(8,128)(2,1)S(1)} copy-done((bf16[384,2048]{1,0:T(8,128)(2,1)S(1)}, bf16[384,2048]{1,0:T(8,128)(2,1)}, u32[]{:S(2)}) %copy-start.2) | copy-done | bytes 1572888
  6.3 0.1 shard_map.51
  6.4 0.1 collective-permute-start.2
  6.5 0.0 collective-permute-done.refs_3_
  6.5 0.0 copy-start
  6.5 2.2 %copy-done = bf16[2048,1024]{1,0:T(8,128)(2,1)S(1)} copy-done((bf16[2048,1024]{1,0:T(8,128)(2,1)S(1)}, bf16[2048,1024]{1,0:T(8,128)(2,1)}, u32[]{:S(2)}) %copy-start) | copy-done | bytes 4194328
  8.7 1.4 %copy-done.3 = bf16[384,2048]{1,0:T(8,128)(2,1)S(1)} copy-done((bf16[384,2048]{1,0:T(8,128)(2,1)S(1)}, bf16[384,2048]{1,0:T(8,128)(2,1)}, u32[]{:S(2)}) %copy-start.3) | copy-done | bytes 1572888
  10.1 7.1 %shard_map.50 = (bf16[768,2048]{1,0:T(8,128)(2,1)S(1)}, bf16[384,1024]{1,0:T(8,128)(2,1)S(1)}, f32[2,256,384]{2,1,0:T(8,128)S(1)}, bf16[768,512]{1,0:T(8,128)(2,...) custom-call(bf16[2048,1024]{1,0:T(8,128)(2,1)S(1)} %copy-done, ...), custom_call_target="tpu_custom_call" | custom-call | flops 1 | bytes 1 | tf_op jit(solution)/shard_map/pallas_call | solution.py:289
  17.3 0.4 collective-permute-done.3.refs_0_.refs_2_.refs_9_.refs_8_.refs_11_.refs_4_
  17.7 0.1 collective-permute-start.4
  17.8 0.5 collective-permute-start.5
  18.3 1.9 %collective-permute-start.1 = (bf16[128,2048]{1,0:T(8,128)(2,1)S(1)}, bf16[128,2048]{1,0:T(8,128)(2,1)S(1)}, u32[]{:S(2)}, u32[]{:S(2)}) collective-permute-start(bf16[128,2048]{1,0:T(8,128)(2,1)S(1)} %get-tuple-element.72), channel_id=1, source_target_pairs={{0,16},{8,24},{16,0},{24,8},{1,17},{9,25},{17,1},{25,9},{2,18},{10... | collective-permute-start | bytes 1572872 | tf_op jit(solution)/shard_map/ppermute | solution.py:28
  20.3 1.9 %shard_map.53 = (bf16[128,1024]{1,0:T(8,128)(2,1)S(1)}, f32[2,256,128]{2,1,0:T(8,128)S(1)}, bf16[128,512]{1,0:T(8,128)(2,1)S(1)}, f32[128,512]{1,0:T(8,128)S(1)}) custom-call(bf16[2048,1024]{1,0:T(8,128)(2,1)S(1)} %copy-done, bf16[1024,512]{1,0:T(8,128)(2,1)S(1)} %copy-done.1, ...), custom_call_target="tpu_custom_call" | custom-call | flops 1 | bytes 1 | tf_op jit(solution)/shard_map/pallas_call | solution.py:289
  22.2 0.0 collective-permute-done.4.refs_2_
  22.2 2.7 %shard_map.54 = (bf16[128,2048]{1,0:T(8,128)(2,1)S(1)}, bf16[128,512]{1,0:T(8,128)(2,1)S(1)}, f32[128,128]{1,0:T(8,128)S(1)}, f32[128,128]{1,0:T(8,128)S(1)}, f3...) custom-call(bf16[2048,1024]{1,0:T(8,128)(2,1)S(1)} %copy-done, ...), custom_call_target="tpu_custom_call" | custom-call | flops 1 | bytes 1 | tf_op jit(solution)/shard_map/pallas_call | solution.py:289
  24.9 4.0 %collective-permute-done.2.refs_0_.refs_2_.refs_13_.refs_12_.refs_5_ = bf16[128,2048]{1,0:T(8,128)(2,1)S(1)} collective-permute-done((bf16[128,2048]{1,0:T(8,128)(2,1)S(1)}, bf16[128,2048]{1,0:T(8,128)(2,1)S(1)}, u32[]{:S(2)}, u32[]{:S(2)}) %collective-permute-start.2) | collective-permute-done | bytes 524320 | tf_op jit(solution)/shard_map/ppermute | solution.py:28
  29.0 0.1 collective-permute-start.6
  29.1 0.5 collective-permute-start.7
  29.6 2.2 %shard_map.56 = (bf16[128,1024]{1,0:T(8,128)(2,1)S(1)}, f32[2,256,128]{2,1,0:T(8,128)S(1)}, bf16[128,512]{1,0:T(8,128)(2,1)S(1)}, f32[128,512]{1,0:T(8,128)S(1)}) custom-call(bf16[2048,1024]{1,0:T(8,128)(2,1)S(1)} %copy-done, bf16[1024,512]{1,0:T(8,128)(2,1)S(1)} %copy-done.1, ...), custom_call_target="tpu_custom_call" | custom-call | flops 1 | bytes 1 | tf_op jit(solution)/shard_map/pallas_call | solution.py:289
  31.8 3.6 %shard_map.57 = (bf16[128,2048]{1,0:T(8,128)(2,1)S(1)}, bf16[128,512]{1,0:T(8,128)(2,1)S(1)}, f32[128,128]{1,0:T(8,128)S(1)}, f32[128,128]{1,0:T(8,128)S(1)}, f3...) custom-call(bf16[2048,1024]{1,0:T(8,128)(2,1)S(1)} %copy-done, ...), custom_call_target="tpu_custom_call" | custom-call | flops 1 | bytes 1 | tf_op jit(solution)/shard_map/pallas_call | solution.py:289
  35.4 4.5 %collective-permute-done.1.refs_0_.refs_2_.refs_16_.refs_13_.refs_6_ = bf16[128,2048]{1,0:T(8,128)(2,1)S(1)} collective-permute-done((bf16[128,2048]{1,0:T(8,128)(2,1)S(1)}, bf16[128,2048]{1,0:T(8,128)(2,1)S(1)}, u32[]{:S(2)}, u32[]{:S(2)}) %collective-permute-start.1) | collective-permute-done | bytes 524320 | tf_op jit(solution)/shard_map/ppermute | solution.py:28
  40.0 0.1 collective-permute-start.8
  40.0 2.5 %shard_map.59 = (bf16[128,1024]{1,0:T(8,128)(2,1)S(1)}, f32[2,256,128]{2,1,0:T(8,128)S(1)}, bf16[128,512]{1,0:T(8,128)(2,1)S(1)}, f32[128,512]{1,0:T(8,128)S(1)}) custom-call(bf16[2048,1024]{1,0:T(8,128)(2,1)S(1)} %copy-done, bf16[1024,512]{1,0:T(8,128)(2,1)S(1)} %copy-done.1, ...), custom_call_target="tpu_custom_call" | custom-call | flops 1 | bytes 1 | tf_op jit(solution)/shard_map/pallas_call | solution.py:289
  42.6 4.8 %shard_map.60 = (bf16[768,512]{1,0:T(8,128)(2,1)S(1)}, bf16[256,768]{1,0:T(8,128)(2,1)S(1)}) custom-call(bf16[2048,1024]{1,0:T(8,128)(2,1)S(1)} %copy-done, bf16[1024,512]{1,0:T(8,128)(2,1)S(1)} %copy-done.1, bf16[128,2048]{1,0:T(8,128)(2,1)S(1)} %collective-permute-done.8.refs_2_.refs_6_.refs_9_, f32[128,512]{1,0:T(8,128)S(1)} %get-tuple-element.99.refs_3_, ...), custom_call_target="tpu_custom_call" | custom-call | flops 1 | bytes 1 | tf_op jit(solution)/shard_map/pallas_call | solution.py:289
  47.4 0.6 collective-permute-start.9
  47.9 0.1 broadcast_compare_fusion.2
  48.0 1.8 %shard_map.61 = (bf16[256,768]{1,0:T(8,128)(2,1)S(1)}, f32[128,1024]{1,0:T(8,128)S(1)}, f32[4,240,256]{2,1,0:T(8,128)S(1)}) custom-call(bf16[1024,512]{1,0:T(8,128)(2,1)S(1)} %copy-done.1, bf16[768,512]{1,0:T(8,128)(2,1)S(1)} %get-tuple-element.113.refs_1_.refs_10_, bf16[384,1024]{1,0:T(8,128)(2,1)S(1)} %get-tuple-element.105.refs_18_.refs_2_.refs_12_, ...), custom_call_target="tpu_custom_call" | custom-call | flops 1 | bytes 1 | tf_op jit(solution)/shard_map/pallas_call | solution.py:289
  49.9 0.1 collective-permute-start.10
  49.9 0.8 shard_map.62
  50.8 0.2 multiply_convert_fusion
  51.0 1.8 %collective-permute-start.11 = (f16[4,256,256]{2,1,0:T(8,128)(2,1)S(1)}, f16[4,256,256]{2,1,0:T(8,128)(2,1)S(1)}, u32[]{:S(2)}, u32[]{:S(2)}) collective-permute-start(f16[4,256,256]{2,1,0:T(8,128)(2,1)S(1)} %multiply_convert_fusion), channel_id=1, source_target_pairs={{0,1},{1,0},{2,3},{3,2},{4,5},{5,4},{6,7},{7,6},{8,9},{9,8},{10,11... | collective-permute-start | bytes 1572872 | tf_op jit(solution)/shard_map/ppermute | solution.py:33
  52.8 1.4 %shard_map.63 = f32[8,96,256]{2,1,0:T(8,128)S(1)} custom-call(bf16[256,768]{1,0:T(8,128)(2,1)S(1)} %get-tuple-element.114.refs_0_, bf16[256,768]{1,0:T(8,128)(2,1)S(1)} %collective-permute-done.9.refs_1_, f32[8,256]{1,0:T(8,128)S(1)} %get-tuple-element.119.refs_2_, bf16[768,2048]{1,0:T(8,128)(2,1)S(1)} %get-tuple-element.78.refs_3_.refs_5_.refs_4_.refs_10_, ...), custom_call_target="tpu_custom_call" | custom-call | flops 1 | bytes 1 | tf_op jit(solution)/shard_map/pallas_call | solution.py:289
  54.4 0.1 fusion.6
  54.5 1.7 %collective-permute-start.12 = (f16[2,96,256]{2,1,0:T(8,128)(2,1)S(1)}, f16[2,96,256]{2,1,0:T(8,128)(2,1)S(1)}, u32[]{:S(2)}, u32[]{:S(2)}) collective-permute-start(f16[2,96,256]{2,1,0:T(8,128)(2,1)S(1)} %get-tuple-element.124), channel_id=1, source_target_pairs={{0,2},{1,3},{2,0},{3,1},{4,6},{5,7},{6,4},{7,5},{8,10},{9,11},{10,... | collective-permute-start | bytes 294920 | tf_op jit(solution)/shard_map/ppermute | solution.py:33
  56.2 2.6 %collective-permute-start.13 = (f16[2,96,256]{2,1,0:T(8,128)(2,1)S(1)}, f16[2,96,256]{2,1,0:T(8,128)(2,1)S(1)}, u32[]{:S(2)}, u32[]{:S(2)}) collective-permute-start(f16[2,96,256]{2,1,0:T(8,128)(2,1)S(1)} %get-tuple-element.125), channel_id=1, source_target_pairs={{0,4},{1,5},{2,6},{3,7},{4,0},{5,1},{6,2},{7,3},{8,12},{9,13},{10,... | collective-permute-start | bytes 294920 | tf_op jit(solution)/shard_map/ppermute | solution.py:33
  58.7 0.2 collective-permute-start.14
  59.0 1.7 %shard_map.64 = f32[4,256,256]{2,1,0:T(8,128)S(1)} custom-call(bf16[256,768]{1,0:T(8,128)(2,1)S(1)} %get-tuple-element.114.refs_0_, bf16[256,768]{1,0:T(8,128)(2,1)S(1)} %collective-permute-done.9.refs_1_, f32[8,256]{1,0:T(8,128)S(1)} %get-tuple-element.119.refs_2_, bf16[768,2048]{1,0:T(8,128)(2,1)S(1)} %get-tuple-element.78.refs_3_.refs_5_.refs_4_.refs_10_, ...), custom_call_target="tpu_custom_call" | custom-call | flops 1 | bytes 1 | tf_op jit(solution)/shard_map/pallas_call | solution.py:289
  60.6 4.8 %collective-permute-done.11 = f16[4,256,256]{2,1,0:T(8,128)(2,1)S(1)} collective-permute-done((f16[4,256,256]{2,1,0:T(8,128)(2,1)S(1)}, f16[4,256,256]{2,1,0:T(8,128)(2,1)S(1)}, u32[]{:S(2)}, u32[]{:S(2)}) %collective-permute-start.11) | collective-permute-done | bytes 524320 | tf_op jit(solution)/shard_map/ppermute | solution.py:33
  65.4 0.1 convert_element_type.70
  65.5 0.3 add_select_fusion
  65.9 0.2 fusion.1
  66.1 0.7 collective-permute-done.13
  66.8 1.8 %collective-permute-start.15 = (f16[256,256]{1,0:T(8,128)(2,1)S(1)}, f16[256,256]{1,0:T(8,128)(2,1)S(1)}, u32[]{:S(2)}, u32[]{:S(2)}) collective-permute-start(f16[256,256]{1,0:T(8,128)(2,1)S(1)} %get-tuple-element.130), channel_id=1, source_target_pairs={{0,2},{1,3},{2,0},{3,1},{4,6},{5,7},{6,4},{7,5},{8,10},{9,11},{10,... | collective-permute-start | bytes 393224 | tf_op jit(solution)/shard_map/ppermute | solution.py:33
  68.6 2.0 %collective-permute-start.16 = (f16[256,256]{1,0:T(8,128)(2,1)S(1)}, f16[256,256]{1,0:T(8,128)(2,1)S(1)}, u32[]{:S(2)}, u32[]{:S(2)}) collective-permute-start(f16[256,256]{1,0:T(8,128)(2,1)S(1)} %get-tuple-element.132), channel_id=1, source_target_pairs={{0,4},{1,5},{2,6},{3,7},{4,0},{5,1},{6,2},{7,3},{8,12},{9,13},{10,... | collective-permute-start | bytes 393224 | tf_op jit(solution)/shard_map/ppermute | solution.py:33
  70.6 0.6 collective-permute-start.17
  71.2 1.8 %collective-permute-done.15 = f16[256,256]{1,0:T(8,128)(2,1)S(1)} collective-permute-done((f16[256,256]{1,0:T(8,128)(2,1)S(1)}, f16[256,256]{1,0:T(8,128)(2,1)S(1)}, u32[]{:S(2)}, u32[]{:S(2)}) %collective-permute-start.15) | collective-permute-done | bytes 131104 | tf_op jit(solution)/shard_map/ppermute | solution.py:33
  73.2 0.2 add_select_fusion.2
  73.4 1.6 %collective-permute-start.18 = (f16[96,256]{1,0:T(8,128)(2,1)S(1)}, f16[96,256]{1,0:T(8,128)(2,1)S(1)}, u32[]{:S(2)}, u32[]{:S(2)}) collective-permute-start(f16[96,256]{1,0:T(8,128)(2,1)S(1)} %fusion.10), channel_id=1, source_target_pairs={{0,1},{1,0},{2,3},{3,2},{4,5},{5,4},{6,7},{7,6},{8,9},{9,8},{10,11... | collective-permute-start | bytes 147464 | tf_op jit(solution)/shard_map/ppermute | solution.py:33
  75.0 4.2 %collective-permute-done.17 = f16[256,256]{1,0:T(8,128)(2,1)S(1)} collective-permute-done((f16[256,256]{1,0:T(8,128)(2,1)S(1)}, f16[256,256]{1,0:T(8,128)(2,1)S(1)}, u32[]{:S(2)}, u32[]{:S(2)}) %collective-permute-start.17) | collective-permute-done | bytes 131104 | tf_op jit(solution)/shard_map/ppermute | solution.py:33
  79.2 1.6 %collective-permute-done.16 = f16[256,256]{1,0:T(8,128)(2,1)S(1)} collective-permute-done((f16[256,256]{1,0:T(8,128)(2,1)S(1)}, f16[256,256]{1,0:T(8,128)(2,1)S(1)}, u32[]{:S(2)}, u32[]{:S(2)}) %collective-permute-start.16) | collective-permute-done | bytes 131104 | tf_op jit(solution)/shard_map/ppermute | solution.py:33
  80.9 0.2 add_select_fusion.1.refs_0_
  81.2 0.1 add_select_fusion.3.refs_1_
  81.3 0.2 shard_map.65.refs_0_
  81.4 0.2 multiply_convert_fusion.1
  81.6 1.6 %collective-permute-start.19 = (f16[336,256]{1,0:T(8,128)(2,1)S(1)}, f16[336,256]{1,0:T(8,128)(2,1)S(1)}, u32[]{:S(2)}, u32[]{:S(2)}) collective-permute-start(f16[336,256]{1,0:T(8,128)(2,1)S(1)} %get-tuple-element.138), channel_id=1, source_target_pairs={{0,16},{8,24},{16,0},{24,8},{1,17},{9,25},{17,1},{25,9},{2,18},{10... | collective-permute-start | bytes 516104 | tf_op jit(solution)/shard_map/ppermute | solution.py:28
  83.2 3.9 %collective-permute-done.19 = f16[336,256]{1,0:T(8,128)(2,1)S(1)} collective-permute-done((f16[336,256]{1,0:T(8,128)(2,1)S(1)}, f16[336,256]{1,0:T(8,128)(2,1)S(1)}, u32[]{:S(2)}, u32[]{:S(2)}) %collective-permute-start.19) | collective-permute-done | bytes 172064 | tf_op jit(solution)/shard_map/ppermute | solution.py:28
  87.1 0.1 pad_maximum_fusion
  87.2 0.1 collective-permute-start.20
  87.3 1.6 %collective-permute-done.20 = f16[2,336,256]{2,1,0:T(8,128)(2,1)S(1)} collective-permute-done((f16[2,336,256]{2,1,0:T(8,128)(2,1)S(1)}, f16[2,336,256]{2,1,0:T(8,128)(2,1)S(1)}, u32[]{:S(2)}, u32[]{:S(2)}) %collective-permute-start.20) | collective-permute-done | bytes 344096 | tf_op jit(solution)/shard_map/ppermute | solution.py:28
  89.0 0.2 bitcast_multiply_fusion
  89.2 1.1 %shard_map.66 = (f32[256,1024]{1,0:T(8,128)}, f32[128,512]{1,0:T(8,128)}) custom-call(f32[336,256]{1,0:T(8,128)S(1)} %shard_map.65.refs_0_, f32[336,256]{1,0:T(8,128)S(1)} %get-tuple-element.164.refs_1_, f32[336,256]{1,0:T(8,128)S(1)} %get-tuple-element.192.refs_2_, f32[336,256]{1,0:T(8,128)S(1)} %get-tuple-element.163.refs_3_), custom_call_target="tpu_custom_call" | custom-call | flops 1 | bytes 1 | tf_op jit(solution)/shard_map/pallas_call | solution.py:289
  (58 shorter events, 0.7 us)
Async XLA Ops:
  0.6 5.9 %copy-start.1 = (bf16[1024,512]{1,0:T(8,128)(2,1)S(1)}, bf16[1024,512]{1,0:T(8,128)(2,1)}, u32[]{:S(2)}) copy-start(bf16[1024,512]{1,0:T(8,128)(2,1)} %refs_0_.17) | copy-start | bytes 3145732
  1.8 4.7 %collective-permute-start = (bf16[384,2048]{1,0:T(8,128)(2,1)}, bf16[384,2048]{1,0:T(8,128)(2,1)S(1)}, u32[]{:S(2)}, u32[]{:S(2)}) collective-permute-start(bf16[384,2048]{1,0:T(8,128)(2,1)} %refs_0_.10), channel_id=1, source_target_pairs={{0,8},{8,0},{16,24},{24,16},{1,9},{9,1},{17,25},{25,17},{2,10},{10... | collective-permute-start | bytes 4718600 | tf_op jit(solution)/shard_map/ppermute | solution.py:28
  2.3 15.4 %collective-permute-start.3 = (bf16[128,2048]{1,0:T(8,128)(2,1)S(1)}, bf16[128,2048]{1,0:T(8,128)(2,1)S(1)}, u32[]{:S(2)}, u32[]{:S(2)}) collective-permute-start(bf16[128,2048]{1,0:T(8,128)(2,1)S(1)} %slice.189), channel_id=1, source_target_pairs={{0,16},{8,24},{16,0},{24,8},{1,17},{9,25},{17,1},{25,9},{2,18},{10... | collective-permute-start | bytes 1572872 | tf_op jit(solution)/shard_map/ppermute | solution.py:28
  4.9 1.4 %copy-start.2 = (bf16[384,2048]{1,0:T(8,128)(2,1)S(1)}, bf16[384,2048]{1,0:T(8,128)(2,1)}, u32[]{:S(2)}) copy-start(bf16[384,2048]{1,0:T(8,128)(2,1)} %refs_0_.10) | copy-start | bytes 4718596
  6.4 22.5 %collective-permute-start.2 = (bf16[128,2048]{1,0:T(8,128)(2,1)S(1)}, bf16[128,2048]{1,0:T(8,128)(2,1)S(1)}, u32[]{:S(2)}, u32[]{:S(2)}) collective-permute-start(bf16[128,2048]{1,0:T(8,128)(2,1)S(1)} %get-tuple-element.73), channel_id=1, source_target_pairs={{0,16},{8,24},{16,0},{24,8},{1,17},{9,25},{17,1},{25,9},{2,18},{10... | collective-permute-start | bytes 1572872 | tf_op jit(solution)/shard_map/ppermute | solution.py:28
  6.5 2.2 %copy-start = (bf16[2048,1024]{1,0:T(8,128)(2,1)S(1)}, bf16[2048,1024]{1,0:T(8,128)(2,1)}, u32[]{:S(2)}) copy-start(bf16[2048,1024]{1,0:T(8,128)(2,1)} %refs_0_.16) | copy-start | bytes 12582916
  8.7 1.4 %copy-start.3 = (bf16[384,2048]{1,0:T(8,128)(2,1)S(1)}, bf16[384,2048]{1,0:T(8,128)(2,1)}, u32[]{:S(2)}) copy-start(bf16[384,2048]{1,0:T(8,128)(2,1)} %refs_0_.10) | copy-start | bytes 4718596
  17.7 4.4 %collective-permute-start.4 = (bf16[64,2048]{1,0:T(8,128)(2,1)S(1)}, bf16[64,2048]{1,0:T(8,128)(2,1)S(1)}, u32[]{:S(2)}, u32[]{:S(2)}) collective-permute-start(bf16[64,2048]{1,0:T(8,128)(2,1)S(1)} %get-tuple-element.76), channel_id=1, source_target_pairs={{0,8},{8,0},{16,24},{24,16},{1,9},{9,1},{17,25},{25,17},{2,10},{10... | collective-permute-start | bytes 786440 | tf_op jit(solution)/shard_map/ppermute | solution.py:28
  17.8 4.3 %collective-permute-start.5 = (bf16[64,2048]{1,0:T(8,128)(2,1)S(1)}, bf16[64,2048]{1,0:T(8,128)(2,1)S(1)}, u32[]{:S(2)}, u32[]{:S(2)}) collective-permute-start(bf16[64,2048]{1,0:T(8,128)(2,1)S(1)} %get-tuple-element.77), channel_id=1, source_target_pairs={{0,8},{8,0},{16,24},{24,16},{1,9},{9,1},{17,25},{25,17},{2,10},{10... | collective-permute-start | bytes 786440 | tf_op jit(solution)/shard_map/ppermute | solution.py:28
  18.3 21.6 %collective-permute-start.1 = (bf16[128,2048]{1,0:T(8,128)(2,1)S(1)}, bf16[128,2048]{1,0:T(8,128)(2,1)S(1)}, u32[]{:S(2)}, u32[]{:S(2)}) collective-permute-start(bf16[128,2048]{1,0:T(8,128)(2,1)S(1)} %get-tuple-element.72), channel_id=1, source_target_pairs={{0,16},{8,24},{16,0},{24,8},{1,17},{9,25},{17,1},{25,9},{2,18},{10... | collective-permute-start | bytes 1572872 | tf_op jit(solution)/shard_map/ppermute | solution.py:28
  29.0 2.8 %collective-permute-start.6 = (bf16[64,2048]{1,0:T(8,128)(2,1)S(1)}, bf16[64,2048]{1,0:T(8,128)(2,1)S(1)}, u32[]{:S(2)}, u32[]{:S(2)}) collective-permute-start(bf16[64,2048]{1,0:T(8,128)(2,1)S(1)} %get-tuple-element.85), channel_id=1, source_target_pairs={{0,8},{8,0},{16,24},{24,16},{1,9},{9,1},{17,25},{25,17},{2,10},{10... | collective-permute-start | bytes 786440 | tf_op jit(solution)/shard_map/ppermute | solution.py:28
  29.1 2.7 %collective-permute-start.7 = (bf16[64,2048]{1,0:T(8,128)(2,1)S(1)}, bf16[64,2048]{1,0:T(8,128)(2,1)S(1)}, u32[]{:S(2)}, u32[]{:S(2)}) collective-permute-start(bf16[64,2048]{1,0:T(8,128)(2,1)S(1)} %get-tuple-element.86), channel_id=1, source_target_pairs={{0,8},{8,0},{16,24},{24,16},{1,9},{9,1},{17,25},{25,17},{2,10},{10... | collective-permute-start | bytes 786440 | tf_op jit(solution)/shard_map/ppermute | solution.py:28
  40.0 2.6 %collective-permute-start.8 = (bf16[128,2048]{1,0:T(8,128)(2,1)S(1)}, bf16[128,2048]{1,0:T(8,128)(2,1)S(1)}, u32[]{:S(2)}, u32[]{:S(2)}) collective-permute-start(bf16[128,2048]{1,0:T(8,128)(2,1)S(1)} %shard_map.58), channel_id=1, source_target_pairs={{0,8},{8,0},{16,24},{24,16},{1,9},{9,1},{17,25},{25,17},{2,10},{10... | collective-permute-start | bytes 1572872 | tf_op jit(solution)/shard_map/ppermute | solution.py:28
  47.4 2.6 %collective-permute-start.9 = (bf16[256,768]{1,0:T(8,128)(2,1)S(1)}, bf16[256,768]{1,0:T(8,128)(2,1)S(1)}, u32[]{:S(2)}, u32[]{:S(2)}) collective-permute-start(bf16[256,768]{1,0:T(8,128)(2,1)S(1)} %get-tuple-element.115), channel_id=1, source_target_pairs={{0,8},{8,0},{16,24},{24,16},{1,9},{9,1},{17,25},{25,17},{2,10},{10... | collective-permute-start | bytes 1179656 | tf_op jit(solution)/shard_map/ppermute | solution.py:28
  49.9 3.0 %collective-permute-start.10 = (f32[128,1024]{1,0:T(8,128)S(1)}, f32[128,1024]{1,0:T(8,128)S(1)}, u32[]{:S(2)}, u32[]{:S(2)}) collective-permute-start(f32[128,1024]{1,0:T(8,128)S(1)} %get-tuple-element.120), channel_id=1, source_target_pairs={{0,8},{8,0},{16,24},{24,16},{1,9},{9,1},{17,25},{25,17},{2,10},{10... | collective-permute-start | bytes 1572872 | tf_op jit(solution)/shard_map/ppermute | solution.py:28
  51.0 14.4 %collective-permute-start.11 = (f16[4,256,256]{2,1,0:T(8,128)(2,1)S(1)}, f16[4,256,256]{2,1,0:T(8,128)(2,1)S(1)}, u32[]{:S(2)}, u32[]{:S(2)}) collective-permute-start(f16[4,256,256]{2,1,0:T(8,128)(2,1)S(1)} %multiply_convert_fusion), channel_id=1, source_target_pairs={{0,1},{1,0},{2,3},{3,2},{4,5},{5,4},{6,7},{7,6},{8,9},{9,8},{10,11... | collective-permute-start | bytes 1572872 | tf_op jit(solution)/shard_map/ppermute | solution.py:33
  54.5 11.6 %collective-permute-start.12 = (f16[2,96,256]{2,1,0:T(8,128)(2,1)S(1)}, f16[2,96,256]{2,1,0:T(8,128)(2,1)S(1)}, u32[]{:S(2)}, u32[]{:S(2)}) collective-permute-start(f16[2,96,256]{2,1,0:T(8,128)(2,1)S(1)} %get-tuple-element.124), channel_id=1, source_target_pairs={{0,2},{1,3},{2,0},{3,1},{4,6},{5,7},{6,4},{7,5},{8,10},{9,11},{10,... | collective-permute-start | bytes 294920 | tf_op jit(solution)/shard_map/ppermute | solution.py:33
  56.2 10.6 %collective-permute-start.13 = (f16[2,96,256]{2,1,0:T(8,128)(2,1)S(1)}, f16[2,96,256]{2,1,0:T(8,128)(2,1)S(1)}, u32[]{:S(2)}, u32[]{:S(2)}) collective-permute-start(f16[2,96,256]{2,1,0:T(8,128)(2,1)S(1)} %get-tuple-element.125), channel_id=1, source_target_pairs={{0,4},{1,5},{2,6},{3,7},{4,0},{5,1},{6,2},{7,3},{8,12},{9,13},{10,... | collective-permute-start | bytes 294920 | tf_op jit(solution)/shard_map/ppermute | solution.py:33
  58.7 8.0 %collective-permute-start.14 = (f16[2,96,256]{2,1,0:T(8,128)(2,1)S(1)}, f16[2,96,256]{2,1,0:T(8,128)(2,1)S(1)}, u32[]{:S(2)}, u32[]{:S(2)}) collective-permute-start(f16[2,96,256]{2,1,0:T(8,128)(2,1)S(1)} %get-tuple-element.126), channel_id=1, source_target_pairs={{0,6},{1,7},{2,4},{3,5},{4,2},{5,3},{6,0},{7,1},{8,14},{9,15},{10,... | collective-permute-start | bytes 294920 | tf_op jit(solution)/shard_map/ppermute | solution.py:33
  66.8 6.2 %collective-permute-start.15 = (f16[256,256]{1,0:T(8,128)(2,1)S(1)}, f16[256,256]{1,0:T(8,128)(2,1)S(1)}, u32[]{:S(2)}, u32[]{:S(2)}) collective-permute-start(f16[256,256]{1,0:T(8,128)(2,1)S(1)} %get-tuple-element.130), channel_id=1, source_target_pairs={{0,2},{1,3},{2,0},{3,1},{4,6},{5,7},{6,4},{7,5},{8,10},{9,11},{10,... | collective-permute-start | bytes 393224 | tf_op jit(solution)/shard_map/ppermute | solution.py:33
  68.6 12.3 %collective-permute-start.16 = (f16[256,256]{1,0:T(8,128)(2,1)S(1)}, f16[256,256]{1,0:T(8,128)(2,1)S(1)}, u32[]{:S(2)}, u32[]{:S(2)}) collective-permute-start(f16[256,256]{1,0:T(8,128)(2,1)S(1)} %get-tuple-element.132), channel_id=1, source_target_pairs={{0,4},{1,5},{2,6},{3,7},{4,0},{5,1},{6,2},{7,3},{8,12},{9,13},{10,... | collective-permute-start | bytes 393224 | tf_op jit(solution)/shard_map/ppermute | solution.py:33
  70.6 8.6 %collective-permute-start.17 = (f16[256,256]{1,0:T(8,128)(2,1)S(1)}, f16[256,256]{1,0:T(8,128)(2,1)S(1)}, u32[]{:S(2)}, u32[]{:S(2)}) collective-permute-start(f16[256,256]{1,0:T(8,128)(2,1)S(1)} %get-tuple-element.133), channel_id=1, source_target_pairs={{0,6},{1,7},{2,4},{3,5},{4,2},{5,3},{6,0},{7,1},{8,14},{9,15},{10,... | collective-permute-start | bytes 393224 | tf_op jit(solution)/shard_map/ppermute | solution.py:33
  73.4 7.7 %collective-permute-start.18 = (f16[96,256]{1,0:T(8,128)(2,1)S(1)}, f16[96,256]{1,0:T(8,128)(2,1)S(1)}, u32[]{:S(2)}, u32[]{:S(2)}) collective-permute-start(f16[96,256]{1,0:T(8,128)(2,1)S(1)} %fusion.10), channel_id=1, source_target_pairs={{0,1},{1,0},{2,3},{3,2},{4,5},{5,4},{6,7},{7,6},{8,9},{9,8},{10,11... | collective-permute-start | bytes 147464 | tf_op jit(solution)/shard_map/ppermute | solution.py:33
  81.6 5.5 %collective-permute-start.19 = (f16[336,256]{1,0:T(8,128)(2,1)S(1)}, f16[336,256]{1,0:T(8,128)(2,1)S(1)}, u32[]{:S(2)}, u32[]{:S(2)}) collective-permute-start(f16[336,256]{1,0:T(8,128)(2,1)S(1)} %get-tuple-element.138), channel_id=1, source_target_pairs={{0,16},{8,24},{16,0},{24,8},{1,17},{9,25},{17,1},{25,9},{2,18},{10... | collective-permute-start | bytes 516104 | tf_op jit(solution)/shard_map/ppermute | solution.py:28
  87.2 1.7 %collective-permute-start.20 = (f16[2,336,256]{2,1,0:T(8,128)(2,1)S(1)}, f16[2,336,256]{2,1,0:T(8,128)(2,1)S(1)}, u32[]{:S(2)}, u32[]{:S(2)}) collective-permute-start(f16[2,336,256]{2,1,0:T(8,128)(2,1)S(1)} %pad_maximum_fusion), channel_id=1, source_target_pairs={{0,8},{8,0},{16,24},{24,16},{1,9},{9,1},{17,25},{25,17},{2,10},{10... | collective-permute-start | bytes 1032200 | tf_op jit(solution)/shard_map/ppermute | solution.py:28

commit v5 on v4

--- a/solution.py
+++ b/solution.py
@@ -105,8 +105,8 @@
     _, sq_cols = diagonals(dot(top, top, NT))
     tok = i["feats", 0].shape[0] // 2
     total = None
-    for name in [0] + [("rs", j) for j in range(1, k)]:
-        rows = pl.ds(tok, tok) if name == 0 else pl.ds(0, top.shape[0])
+    for name in names_of(k, "rs"):
+        rows = pl.ds(tok, tok) if name == 0 else pl.ds(0, i["sq", name].shape[0])
         old = i["embed", name][rows, :]
         inter = dot(i["feats", name][rows, :], top, NT)
         resid = residual(inter, dot(old, embed_new, NT), i["sq", name][rows, :1], sq_cols, emb)
@@ -139,20 +139,38 @@
     resid = residual(inter[:part], pred, sq_rows[:part], sq_cols, emb)
     total = i["total"][...] + dot(resid, embed_new)
     out = []
-    for j in range(k):
-        name = ("rem", j) if j else 0
-        rows = pl.ds(0, i["summed", j].shape[0])
+    for name in names_of(k, "rem"):
+        rows = pl.ds(0, i["summed", name].shape[0])
         old = i["embed", name][rows, :]
         inter = dot(i["feats", name][rows, :], top, NT)
         pred = dot(old, embed_new, NT)
         resid = residual(inter, pred, i["sq", name][rows, :1], sq_cols, emb)
         total += dot(resid[:, :part], old, TN)
-        out.append(i["summed", j][...] + dot(resid, embed_new))
+        out.append(i["summed", name][...] + dot(resid, embed_new))
     out.append(total)
-    for j in range(k + 1):
-        if ("summed", j) in o:
-            o["summed", j][...] = out[j]
+    for name, value in zip(names_of(k, "rem") + [("rem", k)], out):
+        if ("summed", name) in o:
+            o["summed", name][...] = value
     return out
+
+
+def names_of(k, kind):
+    if k == CHUNKS:
+        return [0, (kind, 0)]
+    return [0] + [(kind, j) for j in range(1, k)]
+
+
+def join(i, o, s):
+    for target, out in o.items():
+        if target == "token":
+            out[...] = jnp.zeros((8, 128), F32)
+            continue
+        what, (kind, _) = target
+        start = 0
+        for j in range(1, CHUNKS):
+            count = i[what, (kind, j)].shape[0]
+            out[start : start + count] = i[what, (kind, j)][...]
+            start += count
 
 
 def last_stage(factor, i, o, s):
@@ -201,11 +219,10 @@
 
 
 def core_rows(i, core):
-    both = i["feats", 0]
-    tok = both.shape[0] // 2
-    name = ("rem", "rs")[core]
-    return [(both, core * tok, tok)] + [
-        (i["feats", (name, j)], 0, i["feats", (name, j)].shape[0]) for j in range(1, CHUNKS + 1)
+    tok = i["feats", 0].shape[0] // 2
+    kind = ("rem", "rs")[core]
+    return [(i["feats", 0], core * tok, tok)] + [
+        (i["feats", (kind, j)], 0, i["feats", (kind, j)].shape[0]) for j in (0, CHUNKS)
     ]
 
 
@@ -472,8 +489,26 @@
     kinds = [out["kind_one"], out["kind_two"], out["kind_all"]]
     hidden, gate, feats = [out["hidden"]], [out["gate"]], [out["feats"]]
     embed, sq, summed = [out["embed"]], [out["sq"]], [out["summed", 0]]
-    feats, embed, sq, summed = {0: feats[0]}, {0: embed[0]}, {0: sq[0]}, summed
+    feats, embed, sq, summed = {0: feats[0]}, {0: embed[0]}, {0: sq[0]}, {0: summed[0]}
     for step in range(1, k + 1):
+        if step == k:
+            ins, outs = {}, {"token": ((8, 128), F32)}
+            for kind in ("rem", "rs"):
+                for what, values in (("feats", feats), ("embed", embed), ("sq", sq), ("summed", summed)):
+                    if what == "summed" and kind == "rs":
+                        continue
+                    for j in range(1, k):
+                        ins[what, (kind, j)] = values[kind, j]
+                    count, lanes_of = values[kind, 1].shape
+                    outs[what, (kind, 0)] = ((count * (k - 1), lanes_of), values[kind, 1].dtype)
+            ins["token"] = token
+            joined = run(join, ins, outs, {})
+            token = joined["token"]
+            for target, value in joined.items():
+                if target != "token":
+                    {"feats": feats, "embed": embed, "sq": sq, "summed": summed}[target[0]][
+                        target[1]
+                    ] = value
         pieces = 2 if step < k else 1
         out = run(
             split,
@@ -484,11 +519,10 @@
         )
         rs = [blk_swap(out["rows", h], 1) for h in range(pieces)]
         ins = {**base, "new": rem[step - 1]}
-        for name in feats:
-            if name == 0 or name[0] == "rs":
-                ins["feats", name] = feats[name]
-                ins["embed", name] = embed[name]
-                ins["sq", name] = sq[name]
+        for name in names_of(step, "rs"):
+            ins["feats", name] = feats[name]
+            ins["embed", name] = embed[name]
+            ins["sq", name] = sq[name]
         embed_shape, sq_shape = ((part, emb), BF16), ((part, 128), F32)
         out = run(
             functools.partial(rem_stage, step),
@@ -507,23 +541,23 @@
         feats[name], embed[name] = rem[step - 1], out["embed"]
 
         ins = {**base, **{("new", h): r for h, r in enumerate(rs)}, "total": out["total"]}
-        for j in range(step + 1):
-            name = ("rem", j) if j else 0
+        for name in names_of(step, "rem") + [("rem", step)]:
             ins["feats", name] = feats[name]
             ins["embed", name] = embed[name]
-            if j < step:
+            if name != ("rem", step):
                 ins["sq", name] = sq[name]
-                ins["summed", j] = summed[j]
+                ins["summed", name] = summed[name]
         outs = {"feats": ((part, width), BF16)}
         scratch = {"both": ((2 * part, width), BF16), "embeds": ((2 * part, emb), BF16)}
         if step < k:
             outs = {**outs, "embed": embed_shape, "sq_rem": sq_shape, "sq_rs": sq_shape}
             outs["token"] = ((8, 128), F32)
-            for j in range(step + 1):
-                outs["summed", j] = ((tok if j == 0 else part, emb), F32)
+            for name in names_of(step, "rem") + [("rem", step)]:
+                outs["summed", name] = ((tok if name == 0 else part, emb), F32)
             out = run(functools.partial(rs_stage, step), ins, outs, scratch)
             token = out["token"]
-            summed = [out["summed", j] for j in range(step + 1)]
+            for name in names_of(step, "rem") + [("rem", step)]:
+                summed[name] = out["summed", name]
             name = ("rs", step)
             feats[name], embed[name], sq[name] = out["feats"], out["embed"], out["sq_rs"]
             sq["rem", step] = out["sq_rem"]
@@ -542,8 +576,8 @@
     )
     feats["rs", k] = rs[0]
     got = blk_swap(out["give"], 1)
-    mine = {("feats", n): v for n, v in feats.items() if n == 0 or n[0] == "rem"}
-    theirs = {("feats", n): v for n, v in feats.items() if n == 0 or n[0] == "rs"}
+    mine = {("feats", n): feats[n] for n in (0, ("rem", 0), ("rem", k))}
+    theirs = {("feats", n): feats[n] for n in (0, ("rs", 0), ("rs", k))}
     dembed = out["dembed"]
     own = run(
         own_share,

time: 90.7 us -> 89.5 us (0.987)
  Pallas kernels: 32.2 us -> 30.9 us
    pallas_call x17 -> x18, Pallas kernels: 32.2 us -> 30.9 us  [run(): pl.pallas_call(kernel, out_shape=shapes, in_specs=[pl.BlockSpec(memory_sp...]
    unnamed x23 -> x25, local copies, waits for them, and re-layouts: 5.04 us -> 5.05 us
where the time goes in v5:
time: 89.5 us; the launch traced here: 89.2 us
  Pallas kernels  30.9 us (35%)
  waiting for transfers between devices  27.5 us (31%)
  starting transfers between devices  20.9 us (23%)
  local copies, waits for them, and re-layouts  6.21 us (7%)
  other arithmetic  2.35 us (3%)
  between operations  1.42 us (2%)
    pallas_call x18, Pallas kernels, run(): pl.pallas_call(kernel, out_shape=shapes, in_specs=[pl.BlockSpec(memory_sp...  30.9 us
    ppermute x13, waiting for transfers between devices, blk_swap(): return lax.ppermute(value, 'blk', [(b, b ^ bit) for b in range(count)])  14.2 us
    ppermute x8, waiting for transfers between devices, dp_swap(): return lax.ppermute(value, 'dp', [(d, d ^ bit) for d in range(count)])  13.2 us
    ppermute x8, starting transfers between devices, dp_swap(): return lax.ppermute(value, 'dp', [(d, d ^ bit) for d in range(count)])  12.2 us
    ppermute x13, starting transfers between devices, blk_swap(): return lax.ppermute(value, 'blk', [(b, b ^ bit) for b in range(count)])  8.62 us
    unnamed x25, local copies, waits for them, and re-layouts  5.05 us
  transfers between devices with their start and end apart: 21, of which 10 were waited for; matrix products, arithmetic and copies ran while one was open for 2% of the time, Pallas kernels for 29%

profile of v5, /device:TPU:0, one launch (start us, length us, event | category | flops | bytes accessed | tf_op | source)
XLA Modules:
  0.0 89.2 jit_solution(10591706206445047478)
XLA Ops:
  0.6 1.2 %slice.189 = bf16[128,2048]{1,0:T(8,128)(2,1)S(1)} slice(bf16[384,2048]{1,0:T(8,128)(2,1)} %refs_0_.10), slice={[0:128], [0:2048]} | slice | bytes 1048576 | tf_op jit(solution)/shard_map/slice | solution.py:459
  1.8 0.5 collective-permute-start
  2.3 2.6 %collective-permute-start.2 = (bf16[128,2048]{1,0:T(8,128)(2,1)S(1)}, bf16[128,2048]{1,0:T(8,128)(2,1)S(1)}, u32[]{:S(2)}, u32[]{:S(2)}) collective-permute-start(bf16[128,2048]{1,0:T(8,128)(2,1)S(1)} %slice.189), channel_id=1, source_target_pairs={{0,16},{8,24},{16,0},{24,8},{1,17},{9,25},{17,1},{25,9},{2,18},{10... | collective-permute-start | bytes 1572872 | tf_op jit(solution)/shard_map/ppermute | solution.py:28
  4.9 1.4 %copy-done.3 = bf16[384,2048]{1,0:T(8,128)(2,1)S(1)} copy-done((bf16[384,2048]{1,0:T(8,128)(2,1)S(1)}, bf16[384,2048]{1,0:T(8,128)(2,1)}, u32[]{:S(2)}) %copy-start.3) | copy-done | bytes 1572888
  6.3 0.1 shard_map.51
  6.4 0.1 collective-permute-start.3
  6.5 0.0 copy-start
  6.5 2.2 %copy-done = bf16[2048,1024]{1,0:T(8,128)(2,1)S(1)} copy-done((bf16[2048,1024]{1,0:T(8,128)(2,1)S(1)}, bf16[2048,1024]{1,0:T(8,128)(2,1)}, u32[]{:S(2)}) %copy-start) | copy-done | bytes 4194328
  8.7 1.4 %copy-done.4 = bf16[384,2048]{1,0:T(8,128)(2,1)S(1)} copy-done((bf16[384,2048]{1,0:T(8,128)(2,1)S(1)}, bf16[384,2048]{1,0:T(8,128)(2,1)}, u32[]{:S(2)}) %copy-start.4) | copy-done | bytes 1572888
  10.1 7.1 %shard_map.50 = (bf16[768,2048]{1,0:T(8,128)(2,1)S(1)}, bf16[384,1024]{1,0:T(8,128)(2,1)S(1)}, f32[2,256,384]{2,1,0:T(8,128)S(1)}, bf16[768,512]{1,0:T(8,128)(2,...) custom-call(bf16[2048,1024]{1,0:T(8,128)(2,1)S(1)} %copy-done, ...), custom_call_target="tpu_custom_call" | custom-call | flops 1 | bytes 1 | tf_op jit(solution)/shard_map/pallas_call | solution.py:306
  17.3 0.4 collective-permute-done.2.refs_2_.refs_0_.refs_9_
  17.7 0.1 collective-permute-start.4
  17.8 0.5 collective-permute-start.5
  18.3 1.9 %collective-permute-start.1 = (bf16[128,2048]{1,0:T(8,128)(2,1)S(1)}, bf16[128,2048]{1,0:T(8,128)(2,1)S(1)}, u32[]{:S(2)}, u32[]{:S(2)}) collective-permute-start(bf16[128,2048]{1,0:T(8,128)(2,1)S(1)} %get-tuple-element.80), channel_id=1, source_target_pairs={{0,16},{8,24},{16,0},{24,8},{1,17},{9,25},{17,1},{25,9},{2,18},{10... | collective-permute-start | bytes 1572872 | tf_op jit(solution)/shard_map/ppermute | solution.py:28
  20.3 1.9 %shard_map.52 = (bf16[128,1024]{1,0:T(8,128)(2,1)S(1)}, f32[2,256,128]{2,1,0:T(8,128)S(1)}, bf16[128,512]{1,0:T(8,128)(2,1)S(1)}, f32[128,512]{1,0:T(8,128)S(1)}) custom-call(bf16[2048,1024]{1,0:T(8,128)(2,1)S(1)} %copy-done, bf16[1024,512]{1,0:T(8,128)(2,1)S(1)} %copy-done.2, bf16[128,2048]{1,0:T(8,128)(2,1)S(1)} %collective-permute-done.2.refs_2_.refs_0_.refs_9_, ...), custom_call_target="tpu_custom_call" | custom-call | flops 1 | bytes 1 | tf_op jit(solution)/shard_map/pallas_call | solution.py:306
  22.2 2.7 %shard_map.54 = (bf16[128,2048]{1,0:T(8,128)(2,1)S(1)}, bf16[128,512]{1,0:T(8,128)(2,1)S(1)}, f32[128,128]{1,0:T(8,128)S(1)}, f32[128,128]{1,0:T(8,128)S(1)}, f3...) custom-call(bf16[2048,1024]{1,0:T(8,128)(2,1)S(1)} %copy-done, ...), custom_call_target="tpu_custom_call" | custom-call | flops 1 | bytes 1 | tf_op jit(solution)/shard_map/pallas_call | solution.py:306
  24.9 4.0 %collective-permute-done.3.refs_2_.refs_0_.refs_13_.refs_1_ = bf16[128,2048]{1,0:T(8,128)(2,1)S(1)} collective-permute-done((bf16[128,2048]{1,0:T(8,128)(2,1)S(1)}, bf16[128,2048]{1,0:T(8,128)(2,1)S(1)}, u32[]{:S(2)}, u32[]{:S(2)}) %collective-permute-start.3) | collective-permute-done | bytes 524320 | tf_op jit(solution)/shard_map/ppermute | solution.py:28
  29.0 0.1 collective-permute-start.6
  29.1 0.5 collective-permute-start.7
  29.5 2.2 %shard_map.55 = (bf16[128,1024]{1,0:T(8,128)(2,1)S(1)}, f32[2,256,128]{2,1,0:T(8,128)S(1)}, bf16[128,512]{1,0:T(8,128)(2,1)S(1)}, f32[128,512]{1,0:T(8,128)S(1)}) custom-call(bf16[2048,1024]{1,0:T(8,128)(2,1)S(1)} %copy-done, bf16[1024,512]{1,0:T(8,128)(2,1)S(1)} %copy-done.2, bf16[128,2048]{1,0:T(8,128)(2,1)S(1)} %collective-permute-done.3.refs_2_.refs_0_.refs_13_.refs_1_, ...), custom_call_target="tpu_custom_call" | custom-call | flops 1 | bytes 1 | tf_op jit(solution)/shard_map/pallas_call | solution.py:306
  31.8 3.6 %shard_map.57 = (bf16[128,2048]{1,0:T(8,128)(2,1)S(1)}, bf16[128,512]{1,0:T(8,128)(2,1)S(1)}, f32[128,128]{1,0:T(8,128)S(1)}, f32[128,128]{1,0:T(8,128)S(1)}, f3...) custom-call(bf16[2048,1024]{1,0:T(8,128)(2,1)S(1)} %copy-done, ...), custom_call_target="tpu_custom_call" | custom-call | flops 1 | bytes 1 | tf_op jit(solution)/shard_map/pallas_call | solution.py:306
  35.4 0.0 copy-start.1
  35.4 0.2 shard_map.58
  35.7 4.2 %collective-permute-done.1.refs_0_.refs_2_.refs_12_.refs_5_ = bf16[128,2048]{1,0:T(8,128)(2,1)S(1)} collective-permute-done((bf16[128,2048]{1,0:T(8,128)(2,1)S(1)}, bf16[128,2048]{1,0:T(8,128)(2,1)S(1)}, u32[]{:S(2)}, u32[]{:S(2)}) %collective-permute-start.1) | collective-permute-done | bytes 524320 | tf_op jit(solution)/shard_map/ppermute | solution.py:28
  39.9 0.1 collective-permute-start.8
  40.0 2.4 %shard_map.60 = (bf16[128,1024]{1,0:T(8,128)(2,1)S(1)}, f32[2,256,128]{2,1,0:T(8,128)S(1)}, bf16[128,512]{1,0:T(8,128)(2,1)S(1)}, f32[128,512]{1,0:T(8,128)S(1)}) custom-call(bf16[2048,1024]{1,0:T(8,128)(2,1)S(1)} %copy-done.1, bf16[1024,512]{1,0:T(8,128)(2,1)S(1)} %copy-done.2, ...), custom_call_target="tpu_custom_call" | custom-call | flops 1 | bytes 1 | tf_op jit(solution)/shard_map/pallas_call | solution.py:306
  42.5 3.9 %shard_map.61 = (bf16[768,512]{1,0:T(8,128)(2,1)S(1)}, bf16[256,768]{1,0:T(8,128)(2,1)S(1)}) custom-call(bf16[2048,1024]{1,0:T(8,128)(2,1)S(1)} %copy-done.1, bf16[1024,512]{1,0:T(8,128)(2,1)S(1)} %copy-done.2, bf16[128,2048]{1,0:T(8,128)(2,1)S(1)} %collective-permute-done.8.refs_2_.refs_5_.refs_7_, f32[128,512]{1,0:T(8,128)S(1)} %get-tuple-element.114.refs_3_, ...), custom_call_target="tpu_custom_call" | custom-call | flops 1 | bytes 1 | tf_op jit(solution)/shard_map/pallas_call | solution.py:306
  46.4 0.6 collective-permute-start.9
  46.9 0.1 broadcast_compare_fusion.2
  47.0 1.7 %shard_map.62 = (bf16[256,768]{1,0:T(8,128)(2,1)S(1)}, f32[128,1024]{1,0:T(8,128)S(1)}, f32[4,240,256]{2,1,0:T(8,128)S(1)}) custom-call(bf16[1024,512]{1,0:T(8,128)(2,1)S(1)} %copy-done.2, bf16[768,512]{1,0:T(8,128)(2,1)S(1)} %get-tuple-element.129.refs_1_.refs_8_, bf16[384,1024]{1,0:T(8,128)(2,1)S(1)} %get-tuple-element.121.refs_14_.refs_2_.refs_10_, ...), custom_call_target="tpu_custom_call" | custom-call | flops 1 | bytes 1 | tf_op jit(solution)/shard_map/pallas_call | solution.py:306
  48.7 0.1 collective-permute-start.10
  48.8 0.7 shard_map.63
  49.6 0.2 multiply_convert_fusion
  49.8 1.8 %collective-permute-start.11 = (f16[4,256,256]{2,1,0:T(8,128)(2,1)S(1)}, f16[4,256,256]{2,1,0:T(8,128)(2,1)S(1)}, u32[]{:S(2)}, u32[]{:S(2)}) collective-permute-start(f16[4,256,256]{2,1,0:T(8,128)(2,1)S(1)} %multiply_convert_fusion), channel_id=1, source_target_pairs={{0,1},{1,0},{2,3},{3,2},{4,5},{5,4},{6,7},{7,6},{8,9},{9,8},{10,11... | collective-permute-start | bytes 1572872 | tf_op jit(solution)/shard_map/ppermute | solution.py:33
  51.6 1.4 %shard_map.64 = f32[8,96,256]{2,1,0:T(8,128)S(1)} custom-call(bf16[256,768]{1,0:T(8,128)(2,1)S(1)} %get-tuple-element.130.refs_0_, bf16[256,768]{1,0:T(8,128)(2,1)S(1)} %collective-permute-done.9.refs_1_, f32[8,256]{1,0:T(8,128)S(1)} %get-tuple-element.135.refs_2_, bf16[768,2048]{1,0:T(8,128)(2,1)S(1)} %get-tuple-element.83.refs_3_.refs_5_.refs_4_.refs_10_, ...), custom_call_target="tpu_custom_call" | custom-call | flops 1 | bytes 1 | tf_op jit(solution)/shard_map/pallas_call | solution.py:306
  53.2 0.1 fusion.6
  53.3 1.6 %collective-permute-start.12 = (f16[2,96,256]{2,1,0:T(8,128)(2,1)S(1)}, f16[2,96,256]{2,1,0:T(8,128)(2,1)S(1)}, u32[]{:S(2)}, u32[]{:S(2)}) collective-permute-start(f16[2,96,256]{2,1,0:T(8,128)(2,1)S(1)} %get-tuple-element.140), channel_id=1, source_target_pairs={{0,2},{1,3},{2,0},{3,1},{4,6},{5,7},{6,4},{7,5},{8,10},{9,11},{10,... | collective-permute-start | bytes 294920 | tf_op jit(solution)/shard_map/ppermute | solution.py:33
  54.9 2.6 %collective-permute-start.13 = (f16[2,96,256]{2,1,0:T(8,128)(2,1)S(1)}, f16[2,96,256]{2,1,0:T(8,128)(2,1)S(1)}, u32[]{:S(2)}, u32[]{:S(2)}) collective-permute-start(f16[2,96,256]{2,1,0:T(8,128)(2,1)S(1)} %get-tuple-element.141), channel_id=1, source_target_pairs={{0,4},{1,5},{2,6},{3,7},{4,0},{5,1},{6,2},{7,3},{8,12},{9,13},{10,... | collective-permute-start | bytes 294920 | tf_op jit(solution)/shard_map/ppermute | solution.py:33
  57.5 0.2 collective-permute-start.14
  57.7 1.4 %shard_map.65 = f32[4,256,256]{2,1,0:T(8,128)S(1)} custom-call(bf16[256,768]{1,0:T(8,128)(2,1)S(1)} %get-tuple-element.130.refs_0_, bf16[256,768]{1,0:T(8,128)(2,1)S(1)} %collective-permute-done.9.refs_1_, f32[8,256]{1,0:T(8,128)S(1)} %get-tuple-element.135.refs_2_, bf16[768,2048]{1,0:T(8,128)(2,1)S(1)} %get-tuple-element.83.refs_3_.refs_5_.refs_4_.refs_10_, ...), custom_call_target="tpu_custom_call" | custom-call | flops 1 | bytes 1 | tf_op jit(solution)/shard_map/pallas_call | solution.py:306
  59.2 5.0 %collective-permute-done.11 = f16[4,256,256]{2,1,0:T(8,128)(2,1)S(1)} collective-permute-done((f16[4,256,256]{2,1,0:T(8,128)(2,1)S(1)}, f16[4,256,256]{2,1,0:T(8,128)(2,1)S(1)}, u32[]{:S(2)}, u32[]{:S(2)}) %collective-permute-start.11) | collective-permute-done | bytes 524320 | tf_op jit(solution)/shard_map/ppermute | solution.py:33
  64.2 0.1 convert_element_type.70
  64.3 0.3 add_select_fusion
  64.7 0.2 fusion.1
  64.9 0.7 collective-permute-done.13
  65.5 1.8 %collective-permute-start.15 = (f16[256,256]{1,0:T(8,128)(2,1)S(1)}, f16[256,256]{1,0:T(8,128)(2,1)S(1)}, u32[]{:S(2)}, u32[]{:S(2)}) collective-permute-start(f16[256,256]{1,0:T(8,128)(2,1)S(1)} %get-tuple-element.146), channel_id=1, source_target_pairs={{0,2},{1,3},{2,0},{3,1},{4,6},{5,7},{6,4},{7,5},{8,10},{9,11},{10,... | collective-permute-start | bytes 393224 | tf_op jit(solution)/shard_map/ppermute | solution.py:33
  67.3 2.0 %collective-permute-start.16 = (f16[256,256]{1,0:T(8,128)(2,1)S(1)}, f16[256,256]{1,0:T(8,128)(2,1)S(1)}, u32[]{:S(2)}, u32[]{:S(2)}) collective-permute-start(f16[256,256]{1,0:T(8,128)(2,1)S(1)} %get-tuple-element.148), channel_id=1, source_target_pairs={{0,4},{1,5},{2,6},{3,7},{4,0},{5,1},{6,2},{7,3},{8,12},{9,13},{10,... | collective-permute-start | bytes 393224 | tf_op jit(solution)/shard_map/ppermute | solution.py:33
  69.3 0.6 collective-permute-start.17
  69.9 1.8 %collective-permute-done.15 = f16[256,256]{1,0:T(8,128)(2,1)S(1)} collective-permute-done((f16[256,256]{1,0:T(8,128)(2,1)S(1)}, f16[256,256]{1,0:T(8,128)(2,1)S(1)}, u32[]{:S(2)}, u32[]{:S(2)}) %collective-permute-start.15) | collective-permute-done | bytes 131104 | tf_op jit(solution)/shard_map/ppermute | solution.py:33
  71.9 0.2 add_select_fusion.2
  72.1 1.6 %collective-permute-start.18 = (f16[96,256]{1,0:T(8,128)(2,1)S(1)}, f16[96,256]{1,0:T(8,128)(2,1)S(1)}, u32[]{:S(2)}, u32[]{:S(2)}) collective-permute-start(f16[96,256]{1,0:T(8,128)(2,1)S(1)} %fusion.10), channel_id=1, source_target_pairs={{0,1},{1,0},{2,3},{3,2},{4,5},{5,4},{6,7},{7,6},{8,9},{9,8},{10,11... | collective-permute-start | bytes 147464 | tf_op jit(solution)/shard_map/ppermute | solution.py:33
  73.8 4.2 %collective-permute-done.17 = f16[256,256]{1,0:T(8,128)(2,1)S(1)} collective-permute-done((f16[256,256]{1,0:T(8,128)(2,1)S(1)}, f16[256,256]{1,0:T(8,128)(2,1)S(1)}, u32[]{:S(2)}, u32[]{:S(2)}) %collective-permute-start.17) | collective-permute-done | bytes 131104 | tf_op jit(solution)/shard_map/ppermute | solution.py:33
  78.0 1.6 %collective-permute-done.16 = f16[256,256]{1,0:T(8,128)(2,1)S(1)} collective-permute-done((f16[256,256]{1,0:T(8,128)(2,1)S(1)}, f16[256,256]{1,0:T(8,128)(2,1)S(1)}, u32[]{:S(2)}, u32[]{:S(2)}) %collective-permute-start.16) | collective-permute-done | bytes 131104 | tf_op jit(solution)/shard_map/ppermute | solution.py:33
  79.7 0.2 add_select_fusion.1.refs_0_
  80.0 0.1 add_select_fusion.3.refs_1_
  80.0 0.2 shard_map.66.refs_0_
  80.2 0.1 multiply_convert_fusion.1
  80.4 1.6 %collective-permute-start.19 = (f16[336,256]{1,0:T(8,128)(2,1)S(1)}, f16[336,256]{1,0:T(8,128)(2,1)S(1)}, u32[]{:S(2)}, u32[]{:S(2)}) collective-permute-start(f16[336,256]{1,0:T(8,128)(2,1)S(1)} %get-tuple-element.154), channel_id=1, source_target_pairs={{0,16},{8,24},{16,0},{24,8},{1,17},{9,25},{17,1},{25,9},{2,18},{10... | collective-permute-start | bytes 516104 | tf_op jit(solution)/shard_map/ppermute | solution.py:28
  81.9 3.9 %collective-permute-done.19 = f16[336,256]{1,0:T(8,128)(2,1)S(1)} collective-permute-done((f16[336,256]{1,0:T(8,128)(2,1)S(1)}, f16[336,256]{1,0:T(8,128)(2,1)S(1)}, u32[]{:S(2)}, u32[]{:S(2)}) %collective-permute-start.19) | collective-permute-done | bytes 172064 | tf_op jit(solution)/shard_map/ppermute | solution.py:28
  85.8 0.1 pad_maximum_fusion
  85.9 0.1 collective-permute-start.20
  86.0 1.6 %collective-permute-done.20 = f16[2,336,256]{2,1,0:T(8,128)(2,1)S(1)} collective-permute-done((f16[2,336,256]{2,1,0:T(8,128)(2,1)S(1)}, f16[2,336,256]{2,1,0:T(8,128)(2,1)S(1)}, u32[]{:S(2)}, u32[]{:S(2)}) %collective-permute-start.20) | collective-permute-done | bytes 344096 | tf_op jit(solution)/shard_map/ppermute | solution.py:28
  87.7 0.2 bitcast_multiply_fusion
  87.9 1.1 %shard_map.67 = (f32[256,1024]{1,0:T(8,128)}, f32[128,512]{1,0:T(8,128)}) custom-call(f32[336,256]{1,0:T(8,128)S(1)} %shard_map.66.refs_0_, f32[336,256]{1,0:T(8,128)S(1)} %get-tuple-element.180.refs_1_, f32[336,256]{1,0:T(8,128)S(1)} %get-tuple-element.208.refs_2_, f32[336,256]{1,0:T(8,128)S(1)} %get-tuple-element.179.refs_3_), custom_call_target="tpu_custom_call" | custom-call | flops 1 | bytes 1 | tf_op jit(solution)/shard_map/pallas_call | solution.py:306
  (61 shorter events, 0.7 us)
Async XLA Ops:
  0.6 5.9 %copy-start.2 = (bf16[1024,512]{1,0:T(8,128)(2,1)S(1)}, bf16[1024,512]{1,0:T(8,128)(2,1)}, u32[]{:S(2)}) copy-start(bf16[1024,512]{1,0:T(8,128)(2,1)} %refs_0_.17) | copy-start | bytes 3145732
  1.8 4.7 %collective-permute-start = (bf16[384,2048]{1,0:T(8,128)(2,1)}, bf16[384,2048]{1,0:T(8,128)(2,1)S(1)}, u32[]{:S(2)}, u32[]{:S(2)}) collective-permute-start(bf16[384,2048]{1,0:T(8,128)(2,1)} %refs_0_.10), channel_id=1, source_target_pairs={{0,8},{8,0},{16,24},{24,16},{1,9},{9,1},{17,25},{25,17},{2,10},{10... | collective-permute-start | bytes 4718600 | tf_op jit(solution)/shard_map/ppermute | solution.py:28
  2.3 15.4 %collective-permute-start.2 = (bf16[128,2048]{1,0:T(8,128)(2,1)S(1)}, bf16[128,2048]{1,0:T(8,128)(2,1)S(1)}, u32[]{:S(2)}, u32[]{:S(2)}) collective-permute-start(bf16[128,2048]{1,0:T(8,128)(2,1)S(1)} %slice.189), channel_id=1, source_target_pairs={{0,16},{8,24},{16,0},{24,8},{1,17},{9,25},{17,1},{25,9},{2,18},{10... | collective-permute-start | bytes 1572872 | tf_op jit(solution)/shard_map/ppermute | solution.py:28
  4.9 1.4 %copy-start.3 = (bf16[384,2048]{1,0:T(8,128)(2,1)S(1)}, bf16[384,2048]{1,0:T(8,128)(2,1)}, u32[]{:S(2)}) copy-start(bf16[384,2048]{1,0:T(8,128)(2,1)} %refs_0_.10) | copy-start | bytes 4718596
  6.4 22.5 %collective-permute-start.3 = (bf16[128,2048]{1,0:T(8,128)(2,1)S(1)}, bf16[128,2048]{1,0:T(8,128)(2,1)S(1)}, u32[]{:S(2)}, u32[]{:S(2)}) collective-permute-start(bf16[128,2048]{1,0:T(8,128)(2,1)S(1)} %get-tuple-element.82), channel_id=1, source_target_pairs={{0,16},{8,24},{16,0},{24,8},{1,17},{9,25},{17,1},{25,9},{2,18},{10... | collective-permute-start | bytes 1572872 | tf_op jit(solution)/shard_map/ppermute | solution.py:28
  6.5 2.2 %copy-start = (bf16[2048,1024]{1,0:T(8,128)(2,1)S(1)}, bf16[2048,1024]{1,0:T(8,128)(2,1)}, u32[]{:S(2)}) copy-start(bf16[2048,1024]{1,0:T(8,128)(2,1)} %refs_0_.16) | copy-start | bytes 12582916
  8.7 1.4 %copy-start.4 = (bf16[384,2048]{1,0:T(8,128)(2,1)S(1)}, bf16[384,2048]{1,0:T(8,128)(2,1)}, u32[]{:S(2)}) copy-start(bf16[384,2048]{1,0:T(8,128)(2,1)} %refs_0_.10) | copy-start | bytes 4718596
  17.7 4.4 %collective-permute-start.4 = (bf16[64,2048]{1,0:T(8,128)(2,1)S(1)}, bf16[64,2048]{1,0:T(8,128)(2,1)S(1)}, u32[]{:S(2)}, u32[]{:S(2)}) collective-permute-start(bf16[64,2048]{1,0:T(8,128)(2,1)S(1)} %get-tuple-element.88), channel_id=1, source_target_pairs={{0,8},{8,0},{16,24},{24,16},{1,9},{9,1},{17,25},{25,17},{2,10},{10... | collective-permute-start | bytes 786440 | tf_op jit(solution)/shard_map/ppermute | solution.py:28
  17.8 4.3 %collective-permute-start.5 = (bf16[64,2048]{1,0:T(8,128)(2,1)S(1)}, bf16[64,2048]{1,0:T(8,128)(2,1)S(1)}, u32[]{:S(2)}, u32[]{:S(2)}) collective-permute-start(bf16[64,2048]{1,0:T(8,128)(2,1)S(1)} %get-tuple-element.89), channel_id=1, source_target_pairs={{0,8},{8,0},{16,24},{24,16},{1,9},{9,1},{17,25},{25,17},{2,10},{10... | collective-permute-start | bytes 786440 | tf_op jit(solution)/shard_map/ppermute | solution.py:28
  18.3 21.6 %collective-permute-start.1 = (bf16[128,2048]{1,0:T(8,128)(2,1)S(1)}, bf16[128,2048]{1,0:T(8,128)(2,1)S(1)}, u32[]{:S(2)}, u32[]{:S(2)}) collective-permute-start(bf16[128,2048]{1,0:T(8,128)(2,1)S(1)} %get-tuple-element.80), channel_id=1, source_target_pairs={{0,16},{8,24},{16,0},{24,8},{1,17},{9,25},{17,1},{25,9},{2,18},{10... | collective-permute-start | bytes 1572872 | tf_op jit(solution)/shard_map/ppermute | solution.py:28
  29.0 2.8 %collective-permute-start.6 = (bf16[64,2048]{1,0:T(8,128)(2,1)S(1)}, bf16[64,2048]{1,0:T(8,128)(2,1)S(1)}, u32[]{:S(2)}, u32[]{:S(2)}) collective-permute-start(bf16[64,2048]{1,0:T(8,128)(2,1)S(1)} %get-tuple-element.98), channel_id=1, source_target_pairs={{0,8},{8,0},{16,24},{24,16},{1,9},{9,1},{17,25},{25,17},{2,10},{10... | collective-permute-start | bytes 786440 | tf_op jit(solution)/shard_map/ppermute | solution.py:28
  29.1 2.7 %collective-permute-start.7 = (bf16[64,2048]{1,0:T(8,128)(2,1)S(1)}, bf16[64,2048]{1,0:T(8,128)(2,1)S(1)}, u32[]{:S(2)}, u32[]{:S(2)}) collective-permute-start(bf16[64,2048]{1,0:T(8,128)(2,1)S(1)} %get-tuple-element.99), channel_id=1, source_target_pairs={{0,8},{8,0},{16,24},{24,16},{1,9},{9,1},{17,25},{25,17},{2,10},{10... | collective-permute-start | bytes 786440 | tf_op jit(solution)/shard_map/ppermute | solution.py:28
  35.4 4.6 %copy-start.1 = (bf16[2048,1024]{1,0:T(8,128)(2,1)S(1)}, bf16[2048,1024]{1,0:T(8,128)(2,1)}, u32[]{:S(2)}) copy-start(bf16[2048,1024]{1,0:T(8,128)(2,1)} %refs_0_.16) | copy-start | bytes 12582916
  39.9 2.5 %collective-permute-start.8 = (bf16[128,2048]{1,0:T(8,128)(2,1)S(1)}, bf16[128,2048]{1,0:T(8,128)(2,1)S(1)}, u32[]{:S(2)}, u32[]{:S(2)}) collective-permute-start(bf16[128,2048]{1,0:T(8,128)(2,1)S(1)} %shard_map.59), channel_id=1, source_target_pairs={{0,8},{8,0},{16,24},{24,16},{1,9},{9,1},{17,25},{25,17},{2,10},{10... | collective-permute-start | bytes 1572872 | tf_op jit(solution)/shard_map/ppermute | solution.py:28
  46.4 2.5 %collective-permute-start.9 = (bf16[256,768]{1,0:T(8,128)(2,1)S(1)}, bf16[256,768]{1,0:T(8,128)(2,1)S(1)}, u32[]{:S(2)}, u32[]{:S(2)}) collective-permute-start(bf16[256,768]{1,0:T(8,128)(2,1)S(1)} %get-tuple-element.131), channel_id=1, source_target_pairs={{0,8},{8,0},{16,24},{24,16},{1,9},{9,1},{17,25},{25,17},{2,10},{10... | collective-permute-start | bytes 1179656 | tf_op jit(solution)/shard_map/ppermute | solution.py:28
  48.7 2.9 %collective-permute-start.10 = (f32[128,1024]{1,0:T(8,128)S(1)}, f32[128,1024]{1,0:T(8,128)S(1)}, u32[]{:S(2)}, u32[]{:S(2)}) collective-permute-start(f32[128,1024]{1,0:T(8,128)S(1)} %get-tuple-element.136), channel_id=1, source_target_pairs={{0,8},{8,0},{16,24},{24,16},{1,9},{9,1},{17,25},{25,17},{2,10},{10... | collective-permute-start | bytes 1572872 | tf_op jit(solution)/shard_map/ppermute | solution.py:28
  49.8 14.4 %collective-permute-start.11 = (f16[4,256,256]{2,1,0:T(8,128)(2,1)S(1)}, f16[4,256,256]{2,1,0:T(8,128)(2,1)S(1)}, u32[]{:S(2)}, u32[]{:S(2)}) collective-permute-start(f16[4,256,256]{2,1,0:T(8,128)(2,1)S(1)} %multiply_convert_fusion), channel_id=1, source_target_pairs={{0,1},{1,0},{2,3},{3,2},{4,5},{5,4},{6,7},{7,6},{8,9},{9,8},{10,11... | collective-permute-start | bytes 1572872 | tf_op jit(solution)/shard_map/ppermute | solution.py:33
  53.3 11.6 %collective-permute-start.12 = (f16[2,96,256]{2,1,0:T(8,128)(2,1)S(1)}, f16[2,96,256]{2,1,0:T(8,128)(2,1)S(1)}, u32[]{:S(2)}, u32[]{:S(2)}) collective-permute-start(f16[2,96,256]{2,1,0:T(8,128)(2,1)S(1)} %get-tuple-element.140), channel_id=1, source_target_pairs={{0,2},{1,3},{2,0},{3,1},{4,6},{5,7},{6,4},{7,5},{8,10},{9,11},{10,... | collective-permute-start | bytes 294920 | tf_op jit(solution)/shard_map/ppermute | solution.py:33
  54.9 10.6 %collective-permute-start.13 = (f16[2,96,256]{2,1,0:T(8,128)(2,1)S(1)}, f16[2,96,256]{2,1,0:T(8,128)(2,1)S(1)}, u32[]{:S(2)}, u32[]{:S(2)}) collective-permute-start(f16[2,96,256]{2,1,0:T(8,128)(2,1)S(1)} %get-tuple-element.141), channel_id=1, source_target_pairs={{0,4},{1,5},{2,6},{3,7},{4,0},{5,1},{6,2},{7,3},{8,12},{9,13},{10,... | collective-permute-start | bytes 294920 | tf_op jit(solution)/shard_map/ppermute | solution.py:33
  57.5 8.0 %collective-permute-start.14 = (f16[2,96,256]{2,1,0:T(8,128)(2,1)S(1)}, f16[2,96,256]{2,1,0:T(8,128)(2,1)S(1)}, u32[]{:S(2)}, u32[]{:S(2)}) collective-permute-start(f16[2,96,256]{2,1,0:T(8,128)(2,1)S(1)} %get-tuple-element.142), channel_id=1, source_target_pairs={{0,6},{1,7},{2,4},{3,5},{4,2},{5,3},{6,0},{7,1},{8,14},{9,15},{10,... | collective-permute-start | bytes 294920 | tf_op jit(solution)/shard_map/ppermute | solution.py:33
  65.5 6.2 %collective-permute-start.15 = (f16[256,256]{1,0:T(8,128)(2,1)S(1)}, f16[256,256]{1,0:T(8,128)(2,1)S(1)}, u32[]{:S(2)}, u32[]{:S(2)}) collective-permute-start(f16[256,256]{1,0:T(8,128)(2,1)S(1)} %get-tuple-element.146), channel_id=1, source_target_pairs={{0,2},{1,3},{2,0},{3,1},{4,6},{5,7},{6,4},{7,5},{8,10},{9,11},{10,... | collective-permute-start | bytes 393224 | tf_op jit(solution)/shard_map/ppermute | solution.py:33
  67.3 12.3 %collective-permute-start.16 = (f16[256,256]{1,0:T(8,128)(2,1)S(1)}, f16[256,256]{1,0:T(8,128)(2,1)S(1)}, u32[]{:S(2)}, u32[]{:S(2)}) collective-permute-start(f16[256,256]{1,0:T(8,128)(2,1)S(1)} %get-tuple-element.148), channel_id=1, source_target_pairs={{0,4},{1,5},{2,6},{3,7},{4,0},{5,1},{6,2},{7,3},{8,12},{9,13},{10,... | collective-permute-start | bytes 393224 | tf_op jit(solution)/shard_map/ppermute | solution.py:33
  69.3 8.6 %collective-permute-start.17 = (f16[256,256]{1,0:T(8,128)(2,1)S(1)}, f16[256,256]{1,0:T(8,128)(2,1)S(1)}, u32[]{:S(2)}, u32[]{:S(2)}) collective-permute-start(f16[256,256]{1,0:T(8,128)(2,1)S(1)} %get-tuple-element.149), channel_id=1, source_target_pairs={{0,6},{1,7},{2,4},{3,5},{4,2},{5,3},{6,0},{7,1},{8,14},{9,15},{10,... | collective-permute-start | bytes 393224 | tf_op jit(solution)/shard_map/ppermute | solution.py:33
  72.1 7.8 %collective-permute-start.18 = (f16[96,256]{1,0:T(8,128)(2,1)S(1)}, f16[96,256]{1,0:T(8,128)(2,1)S(1)}, u32[]{:S(2)}, u32[]{:S(2)}) collective-permute-start(f16[96,256]{1,0:T(8,128)(2,1)S(1)} %fusion.10), channel_id=1, source_target_pairs={{0,1},{1,0},{2,3},{3,2},{4,5},{5,4},{6,7},{7,6},{8,9},{9,8},{10,11... | collective-permute-start | bytes 147464 | tf_op jit(solution)/shard_map/ppermute | solution.py:33
  80.4 5.5 %collective-permute-start.19 = (f16[336,256]{1,0:T(8,128)(2,1)S(1)}, f16[336,256]{1,0:T(8,128)(2,1)S(1)}, u32[]{:S(2)}, u32[]{:S(2)}) collective-permute-start(f16[336,256]{1,0:T(8,128)(2,1)S(1)} %get-tuple-element.154), channel_id=1, source_target_pairs={{0,16},{8,24},{16,0},{24,8},{1,17},{9,25},{17,1},{25,9},{2,18},{10... | collective-permute-start | bytes 516104 | tf_op jit(solution)/shard_map/ppermute | solution.py:28
  85.9 1.7 %collective-permute-start.20 = (f16[2,336,256]{2,1,0:T(8,128)(2,1)S(1)}, f16[2,336,256]{2,1,0:T(8,128)(2,1)S(1)}, u32[]{:S(2)}, u32[]{:S(2)}) collective-permute-start(f16[2,336,256]{2,1,0:T(8,128)(2,1)S(1)} %pad_maximum_fusion), channel_id=1, source_target_pairs={{0,8},{8,0},{16,24},{24,16},{1,9},{9,1},{17,25},{25,17},{2,10},{10... | collective-permute-start | bytes 1032200 | tf_op jit(solution)/shard_map/ppermute | solution.py:28
